TPU v7x, 32 devices: a whole 2x2x4 slice. The times are simulated.
32 devices in a mesh: dom: 8 (over z, x), bin: 4 (over y, core).
Axes of the slice: x: 2, y: 2, z: 4, core: 2. Of those that a mesh axis runs over, the one named last changes fastest.
Arguments:
- displacement: float32 [3, 64, 64, 512], P(None, 'dom', 'bin'), may hold values from -0.3 to 0.3
- velocity: float32 [3, 64, 64, 512], P(None, 'dom', 'bin'), may hold values from -0.3 to 0.3
- moduli: float32 [2, 64, 64, 512], P(None, 'dom', 'bin'), may hold values from 0.2 to 2
- nodal_mass: float32 [64, 64, 512], P('dom', 'bin'), may hold values from 0.5 to 2
- segment_node: int32 [32768], P(('dom', 'bin')), may hold values from 0 to 65535
- segment_base: float32 [3, 32768], P(None, ('dom', 'bin')), may hold values from 0 to 1
- contact_bin: int32 [4, 256, 1], P(None, ('dom', 'bin')), may hold values from 0 to 3; in each aligned block of 8 rows (0 to 7, 8 to 15, ..., all dimensions but the last counted through in order) at most 4 rows name the same one
- element_tile: int32 [64, 64, 512], P('dom', 'bin'), may hold values from 0 to 8191, as said below
Outputs:
- new_displacement: float32 [3, 64, 64, 512], P(None, 'dom', 'bin')
- new_velocity: float32 [3, 64, 64, 512], P(None, 'dom', 'bin')
- tile_heat: float32 [8192], P(('dom', 'bin'))
Inputs may be any that keep to these rules, and one draw needn't show every extreme that they name: `contact_bin`: in each substep no device sends more than 4 of its blocks to one bin, and at least one device sends exactly 4. `segment_node`: A node of the holding device's own block, numbered row-major over (8, 16, 512). `element_tile`: tiles are numbered device-major (256 to a device, devices in the order dom, then bin). An element's tile belongs to the device that holds it, except that elements of a device's first or last layer along the first dimension may take a tile of the device one step lower or higher along dom (same bin index).
All inputs are finite; a program needn't handle non-finite values.
Results may differ from a plain program's by a relative error of at most 0.0003.
Values sent between devices are 32-bit elements; how exact they have to be, the bound alone decides.
No kernel may reach another device: no remote copies, remote signals or barrier semaphores. Data moves between devices by JAX's collectives and lax.ppermute only.
A program may use at most 128 MiB of HBM per device.

v0:
```python
import functools
import jax
import jax.numpy as jnp
from jax import lax
from jax.experimental import pallas as pl
from jax.experimental.pallas import tpu as pltpu
from jax.sharding import PartitionSpec as P

SEG = 128
TILE_DEV = 256
RADIUS = 0.09
PENALTY = 4.0
SHORT_GAIN = 100.0
TIME_STEP = 0.2
VMEM_BYTES = 40 * 1024 * 1024
F32 = jnp.float32
BF16 = jnp.bfloat16
WHOLE = pl.BlockSpec(memory_space=pltpu.VMEM)
SCALARS = pl.BlockSpec(memory_space=pltpu.SMEM)
NT = (((1,), (1,)), ((), ()))


def shifted(value, axis, steps):
    count = lax.axis_size(axis)
    first, last = (max(0, -steps), min(count, count - steps))
    return lax.ppermute(value, axis, [(source, source + steps) for source in range(first, last)])


def cycled(value, axis, steps):
    count = lax.axis_size(axis)
    return lax.ppermute(value, axis, [(source, (source + steps) % count) for source in range(count)])


def call(body, outs, scratch=(), specs=None):
    return functools.partial(
        pl.pallas_call,
        body,
        out_shape=outs,
        out_specs=[WHOLE] * len(outs),
        scratch_shapes=list(scratch),
        compiler_params=pltpu.CompilerParams(vmem_limit_bytes=VMEM_BYTES),
        cost_estimate=pl.CostEstimate(flops=1_000, bytes_accessed=1_000, transcendentals=0),
    )(in_specs=specs)


def split_two(value):
    high = value.astype(BF16)
    return high, (value - high.astype(F32)).astype(BF16)


def node_split(node_ref, extent_z):
    node = jnp.concatenate([node_ref[j : j + 1, :] for j in range(node_ref.shape[0])], axis=1)
    return lax.div(node, jnp.int32(extent_z)), lax.rem(node, jnp.int32(extent_z))


def one_hot_z(column, extent_z):
    depth = lax.broadcasted_iota(jnp.int32, (extent_z, column.shape[1]), 0)
    return jnp.where(depth == column, 1.0, 0.0).astype(BF16)


def gather_nodes(pieces, row, hot):
    rows = pieces[0].shape[0]
    picked = sum(jnp.dot(piece, hot, preferred_element_type=F32) for piece in pieces)
    at_row = lax.broadcasted_iota(jnp.int32, (rows, row.shape[1]), 0) == row
    return jnp.sum(jnp.where(at_row, picked, 0.0), axis=0, keepdims=True)


def store_positions(disp_ref, base_ref, node_ref, hot, targets):
    extent_x, extent_y, extent_z = disp_ref.shape[1:]
    rows = extent_x * extent_y
    blocks = node_ref.shape[0]
    row, _ = node_split(node_ref, extent_z)
    for p in range(3):
        plane = disp_ref[p].reshape(rows, extent_z)
        points = base_ref[p : p + 1, :] + gather_nodes(split_two(plane), row, hot)
        tile = jnp.concatenate([points[:, j * SEG : (j + 1) * SEG] for j in range(blocks)], axis=0)
        for ref, lane in targets:
            ref[p * blocks : (p + 1) * blocks, lane : lane + SEG] = tile


def store_column(source_ref, at, target_ref, first):
    count, extent_x, _, extent_z = source_ref.shape
    for p in range(count):
        tile = jnp.concatenate([source_ref[p, x, at : at + 1, :] for x in range(extent_x)], axis=0)
        target_ref[first + p * extent_x : first + (p + 1) * extent_x, 0:extent_z] = tile


def store_messages(disp_ref, base_ref, node_ref, hot, up_ref, down_ref, far_ref):
    extent_y, extent_z = disp_ref.shape[2:]
    store_column(disp_ref, extent_y - 1, up_ref, 0)
    store_column(disp_ref, 0, down_ref, 0)
    store_positions(disp_ref, base_ref, node_ref, hot, [(up_ref, extent_z), (down_ref, extent_z), (far_ref, 0)])


def first_body(disp_ref, base_ref, node_ref, moduli_ref, bins_ref, up_ref, down_ref, far_ref, hot_ref):
    _, extent_x, extent_y, extent_z = disp_ref.shape
    _, column = node_split(node_ref, extent_z)
    hot_ref[...] = one_hot_z(column, extent_z)
    store_messages(disp_ref, base_ref, node_ref, hot_ref[...], up_ref, down_ref, far_ref)
    rows = 3 * extent_x
    store_column(moduli_ref, moduli_ref.shape[2] - 1, up_ref, rows)
    bins = bins_ref[...]
    zeros = jnp.zeros((8, SEG), F32)
    up_ref[rows : rows + 8, extent_z:] = bins
    up_ref[rows + 8 : rows + 16, extent_z:] = zeros
    down_ref[rows : rows + 8, 0:extent_z] = jnp.zeros((8, extent_z), F32)
    down_ref[rows : rows + 8, extent_z:] = bins
    far_ref[rows : rows + 8, :] = bins


def layer_body(with_moduli, *refs):
    flag_ref, first_ref, last_ref, lower_ref, upper_ref = refs[:5]
    if with_moduli:
        moduli_ref, up_ref, down_ref = refs[7:]
    else:
        up_ref, down_ref = refs[7:]
    extent_y, extent_z = first_ref.shape[2:]
    main = 3 * extent_y
    extent_x = lower_ref.shape[0] // (5 if with_moduli else 3)
    has_lower, has_upper = flag_ref[0], flag_ref[1]
    for x, source_ref, target_ref in ((0, first_ref, down_ref), (extent_x - 1, last_ref, up_ref)):
        for p in range(3):
            target_ref[p * extent_y : (p + 1) * extent_y, :] = source_ref[p, 0]
        at = [p * extent_x + x for p in range(3)]
        above = [upper_ref[i : i + 1, 0:extent_z] * has_upper for i in at]
        below = [lower_ref[i : i + 1, 0:extent_z] * has_lower for i in at]
        if with_moduli and x > 0:
            at = [(3 + m) * extent_x + x for m in range(2)]
            rest = [lower_ref[i : i + 1, 0:extent_z] * has_lower for i in at]
        else:
            rest = [jnp.zeros((2, extent_z), F32)]
        target_ref[main : main + 8, :] = jnp.concatenate(above + below + rest, axis=0)
    if with_moduli:
        for m in range(2):
            up_ref[main + 8 + m * extent_y : main + 8 + (m + 1) * extent_y, :] = moduli_ref[m, 0]


def pair_sums(bins_ref, own_ref, sources, begin, bin_count, sums_of, store, spread, listed):
    rows = own_ref.shape[0] // 24 * 24
    blocks = rows // 3
    total_blocks = blocks * len(sources)
    stride = total_blocks + 2
    counts = [jnp.int32(0)] * bin_count
    for i in range(total_blocks):
        named = bins_ref[begin + i]
        taken = counts[0]
        for b in range(1, bin_count):
            taken = jnp.where(named == b, counts[b], taken)
        listed[named * stride + taken] = i
        counts = [count + (named == b).astype(jnp.int32) for b, count in enumerate(counts)]
    for b in range(bin_count):
        listed[b * stride + counts[b]] = total_blocks
    spread[total_blocks] = jnp.full((3, SEG, SEG), 1000.0, F32)
    for d, source in enumerate(sources):
        turned = source.T
        for p in range(3):
            for j in range(blocks):
                at = p * blocks + j
                spread[d * blocks + j, p] = jnp.broadcast_to(turned[:, at : at + 1], (SEG, SEG))
    for j in range(blocks):
        named = bins_ref[j]
        count = counts[0]
        for b in range(1, bin_count):
            count = jnp.where(named == b, counts[b], count)
        point = [jnp.broadcast_to(own_ref[p * blocks + j : p * blocks + j + 1, :], (8, SEG)) for p in range(3)]

        def against(i, sums):
            sums = list(sums)
            others = [listed[named * stride + 2 * i + half] for half in range(2)]
            for other, g in [(other, g) for other in others for g in range(SEG // 8)]:
                delta = [point[p] - spread[other, p, g * 8 : (g + 1) * 8, :] for p in range(3)]
                square = delta[0] * delta[0] + delta[1] * delta[1] + delta[2] * delta[2]
                inverse = lax.rsqrt(jnp.maximum(square, 1e-30))
                pressure = jnp.maximum(RADIUS - square * inverse, 0.0)
                factor = pressure * jnp.minimum(inverse, 1.0 / (0.25 * RADIUS))
                for p in range(3):
                    sums[p] = sums[p] + factor * delta[p]
                sums[3] = sums[3] + pressure * pressure
            return tuple(sums)

        store(j, lax.fori_loop(0, (count + 1) // 2, against, sums_of(j)))


def near_body(bin_count, bins_ref, own_ref, lower_ref, _, sums_ref, spread, listed):
    rows = own_ref.shape[0] // 24 * 24
    extent_z = lower_ref.shape[1] - SEG

    def store(j, sums):
        for q in range(4):
            sums_ref[j, q] = sums[q]

    sources = [own_ref[0:rows, :], lower_ref[0:rows, extent_z:]]
    zero = (jnp.zeros((8, SEG), F32),) * 4
    pair_sums(bins_ref, own_ref, sources, 0, bin_count, lambda j: zero, store, spread, listed)


def rest_body(bin_count, last, *refs):
    bins_ref, own_ref, upper_ref, far_ref, sums_ref, node_ref, hot_ref, heat_ref = refs[:8]
    if last:
        tile_ref, contact_ref, partial_ref, spread, listed, push = refs[8:]
    else:
        contact_ref, total_ref, spread, listed, push = refs[8:]
    extent_z = contact_ref.shape[1]
    rows = contact_ref.shape[0] // 3
    point_rows = own_ref.shape[0] // 24 * 24
    blocks = node_ref.shape[0]
    heats = []

    def store(j, sums):
        for p in range(3):
            push[p : p + 1, j * SEG : (j + 1) * SEG] = PENALTY * jnp.sum(sums[p], axis=0, keepdims=True)
        heats.append(SHORT_GAIN * jnp.sum(sums[3], axis=0, keepdims=True))

    sources = [upper_ref[0:point_rows, extent_z:]] + [far_ref[i, 0:point_rows, :] for i in range(far_ref.shape[0])]
    sums_of = lambda j: tuple(sums_ref[j, q] for q in range(4))
    pair_sums(bins_ref, own_ref, sources, 2 * blocks, bin_count, sums_of, store, spread, listed)
    row, _ = node_split(node_ref, extent_z)
    at_row = lax.broadcasted_iota(jnp.int32, (rows, row.shape[1]), 0) == row
    for p in range(3):
        placed = jnp.where(at_row, push[p : p + 1, :], 0.0)
        contact_ref[p * rows : (p + 1) * rows, :] = sum(
            jnp.dot(piece, hot_ref[...], preferred_element_type=F32) for piece in split_two(placed)
        )
    total = heat_ref[...] + jnp.concatenate(heats, axis=0)
    if not last:
        total_ref[...] = total
        return
    flat = jnp.concatenate([total[j : j + 1, :] for j in range(blocks)], axis=1)
    side, slot = tile_ref[0:1, :], tile_ref[1:2, :]
    hot_slot = one_hot_z(slot, TILE_DEV)
    at_side = lax.broadcasted_iota(jnp.int32, (8, flat.shape[1]), 0) == side
    placed = jnp.where(at_side, flat, 0.0)
    high, low = split_two(placed)
    lowest = (placed - high.astype(F32) - low.astype(F32)).astype(BF16)
    partial_ref[...] = sum(
        lax.dot_general(piece, hot_slot, NT, preferred_element_type=F32) for piece in (high, low, lowest)
    )


def turn_body(extent_z, node_ref, out_ref):
    node = node_ref[...]
    column = lax.rem(node, jnp.int32(extent_z)).astype(F32).T
    lane = lax.broadcasted_iota(jnp.int32, (SEG, extent_z), 1).astype(F32)
    for j in range(node.shape[0]):
        out_ref[j * SEG : (j + 1) * SEG, :] = jnp.where(lane == column[:, j : j + 1], 1.0, 0.0).astype(BF16)


def tile_body(own_ref, tiles_ref, node_ref, hot_ref, out_ref):
    extent_x, extent_y, extent_z = tiles_ref.shape
    row, _ = node_split(node_ref, extent_z)
    hot = hot_ref[...]
    tiles = tiles_ref[...].reshape(extent_x * extent_y, extent_z)
    device = lax.div(tiles, jnp.int32(TILE_DEV))
    slot = tiles - device * TILE_DEV
    offset = (device - own_ref[0]).astype(F32).astype(BF16)
    found = gather_nodes([offset], row, hot)
    side = jnp.where(found < -0.5, 0, jnp.where(found > 0.5, 2, 1))
    found_slot = gather_nodes([slot.astype(F32).astype(BF16)], row, hot).astype(jnp.int32)
    rest = jnp.zeros((6, row.shape[1]), jnp.int32)
    out_ref[...] = jnp.concatenate([side, found_slot, rest], axis=0)


WHICH = ((0, 3, 4), (3, 1, 5), (4, 5, 2))
SCALE = -1.0 / 16.0


def ahead_z(value):
    return pltpu.roll(value, value.shape[1] - 1, 1)


def behind_z(value):
    return pltpu.roll(value, 1, 1)


def ahead_row(value):
    return pltpu.roll(value, value.shape[0] - 1, 0)


def behind_row(value):
    return pltpu.roll(value, 1, 0)


def features(near, far):
    total, change = near + far, far - near
    total_z = ahead_z(total)
    return total + total_z, change + ahead_z(change), total_z - total


def stress_of(along_x, along_y, along_z, volume_modulus, shear):
    volume = volume_modulus * (along_x[0] + along_y[1] + along_z[2])
    twice = shear + shear
    return (
        twice * along_x[0] + volume,
        twice * along_y[1] + volume,
        twice * along_z[2] + volume,
        shear * (along_y[0] + along_x[1]),
        shear * (along_z[0] + along_x[2]),
        shear * (along_z[1] + along_y[2]),
    )


def spread_z(plain, slope):
    return (plain - slope) + behind_z(plain + slope)


def inner_body(disp_ref, moduli_ref, out_ref, feature, stress):
    _, extent_x, extent_y, extent_z = disp_ref.shape

    def fill(x, carry):
        for p in range(3):
            value = disp_ref[p, x]
            for q, part in enumerate(features(value, ahead_row(value))):
                feature[x, 3 * q + p] = part
        return carry

    lax.fori_loop(0, extent_x, fill, 0)
    for c in range(6):
        stress[0, c] = jnp.zeros((extent_y, extent_z), F32)
        stress[extent_x, c] = jnp.zeros((extent_y, extent_z), F32)
    place = lax.broadcasted_iota(jnp.int32, (8, extent_z), 0)

    def load(x, carry):
        for t in range(extent_y // 8):
            rows = slice(t * 8, t * 8 + 8)
            scale = jnp.where(place == 7, 0.0, SCALE) if t == extent_y // 8 - 1 else SCALE
            along_x = [feature[x + 1, p, rows] - feature[x, p, rows] for p in range(3)]
            along_y = [feature[x + 1, 3 + p, rows] + feature[x, 3 + p, rows] for p in range(3)]
            along_z = [feature[x + 1, 6 + p, rows] + feature[x, 6 + p, rows] for p in range(3)]
            found = stress_of(along_x, along_y, along_z, moduli_ref[0, x, rows] * scale, moduli_ref[1, x, rows] * scale)
            for c in range(6):
                stress[x + 1, c, rows] = found[c]
        return carry

    lax.fori_loop(0, extent_x - 1, load, 0)

    def force(x, carry):
        for p in range(3):
            of_x, of_y, of_z = WHICH[p]
            part_x = stress[x, of_x] - stress[x + 1, of_x]
            part_y = stress[x, of_y] + stress[x + 1, of_y]
            part_z = stress[x, of_z] + stress[x + 1, of_z]
            plain = (part_x - part_y) + behind_row(part_x + part_y)
            out_ref[p, x] = spread_z(plain, part_z + behind_row(part_z))
        return carry

    lax.fori_loop(0, extent_x, force, 0)


def update_body(first, last, *refs):
    refs = list(refs)
    take = lambda count: [refs.pop(0) for _ in range(count)]
    flag_ref, disp_ref, vel_ref, mass_ref, inner_ref, contact_ref = take(6)
    own_up_ref, own_down_ref, lower_ref, upper_ref, back_ref, front_ref, rim_ref = take(7)
    if not last:
        base_ref, node_ref, hot_ref = take(3)
    new_disp_ref, new_vel_ref = take(2)
    if not last:
        up_ref, down_ref, far_ref = take(3)
    if first:
        moduli_ref, rim_ref = rim_ref, take(1)[0]
    (side_low, side_high, face_low, face_high) = take(4)
    _, extent_x, extent_y, extent_z = disp_ref.shape
    has_lower, has_upper = flag_ref[0], flag_ref[1]
    place = lax.broadcasted_iota(jnp.int32, (8, extent_z), 0)
    all_but_last = lax.broadcasted_iota(jnp.int32, (extent_y, extent_z), 0) < extent_y - 1
    main = 3 * extent_y

    def ring(tile, above, below):
        return jnp.concatenate([tile, jnp.where(place == 0, above, jnp.where(place == 7, below, 0.0))], axis=0)

    if first:
        for m in range(2):
            at = slice((3 + m) * extent_x, (4 + m) * extent_x)
            begin = main + 8 + m * extent_y
            of_back = back_ref[begin : begin + extent_y, :]
            high = ring(own_up_ref[at, 0:extent_z], 0.0, of_back[extent_y - 1 :])
            low = ring(lower_ref[at, 0:extent_z] * has_lower, 0.0, back_ref[main + 6 + m : main + 7 + m, :])
            rim_ref[m] = high * SCALE
            rim_ref[2 + m] = low * SCALE
            rim_ref[4 + m] = jnp.where(all_but_last, of_back * SCALE, 0.0)
            rim_ref[6 + m] = jnp.where(all_but_last, moduli_ref[m, extent_x - 1] * SCALE, 0.0)

    def rows_of(tile_ref, weight, row, extra):
        made = []
        for p in range(3):
            at = main + extra + p if row is None else p * extent_y + row
            tile = tile_ref[p * extent_x : (p + 1) * extent_x, 0:extent_z]
            tile = tile if weight is None else tile * weight
            made.append(ring(tile, front_ref[at : at + 1, :], back_ref[at : at + 1, :]))
        return made

    def side(near, far, at, sign, target):
        parts = [features(near[p], far[p]) for p in range(3)]
        along_x = [ahead_row(parts[p][0]) - parts[p][0] for p in range(3)]
        along_y = [ahead_row(parts[p][1]) + parts[p][1] for p in range(3)]
        along_z = [ahead_row(parts[p][2]) + parts[p][2] for p in range(3)]
        found = stress_of(along_x, along_y, along_z, rim_ref[at], rim_ref[at + 1])
        for p in range(3):
            of_x, of_y, of_z = [found[c] for c in WHICH[p]]
            part_x = (behind_row(of_x) - of_x)[:extent_x]
            part_y = (behind_row(of_y) + of_y)[:extent_x]
            part_z = (behind_row(of_z) + of_z)[:extent_x]
            target[p] = spread_z(part_x + sign * part_y, part_z)

    side(rows_of(own_up_ref, None, extent_y - 1, 0), rows_of(upper_ref, has_upper, None, 0), 0, -1.0, side_high)
    side(rows_of(lower_ref, has_lower, None, 3), rows_of(own_down_ref, None, 0, 0), 2, 1.0, side_low)

    def face(near, far, at, sign, target):
        parts_near = [features(value, ahead_row(value)) for value in near]
        parts_far = [features(value, ahead_row(value)) for value in far]
        along_x = [parts_far[p][0] - parts_near[p][0] for p in range(3)]
        along_y = [parts_far[p][1] + parts_near[p][1] for p in range(3)]
        along_z = [parts_far[p][2] + parts_near[p][2] for p in range(3)]
        found = stress_of(along_x, along_y, along_z, rim_ref[at], rim_ref[at + 1])
        for p in range(3):
            of_x, of_y, of_z = [found[c] for c in WHICH[p]]
            of_x = of_x * sign
            plain = (of_x - of_y) + behind_row(of_x + of_y)
            target[p] = spread_z(plain, of_z + behind_row(of_z))

    layer_of = lambda ref: [ref[p * extent_y : (p + 1) * extent_y, :] for p in range(3)]
    own_layer = lambda x: [disp_ref[p, x] for p in range(3)]
    face(layer_of(back_ref), own_layer(0), 4, 1.0, face_low)
    face(own_layer(extent_x - 1), layer_of(front_ref), 6, -1.0, face_high)

    for x in range(extent_x):
        step_mass = TIME_STEP / mass_ref[x]
        for p in range(3):
            at = (p * extent_x + x) * extent_y
            load = inner_ref[p, x] + contact_ref[at : at + extent_y, :]
            if x == 0:
                load = load + face_low[p]
            if x == extent_x - 1:
                load = load + face_high[p]
            begin = load[:8] + jnp.where(place == 0, side_low[p, x : x + 1, :], 0.0)
            end = load[extent_y - 8 :] + jnp.where(place == 7, side_high[p, x : x + 1, :], 0.0)
            load = jnp.concatenate([begin, load[8 : extent_y - 8], end] if extent_y > 16 else [begin, end], axis=0)
            speed = vel_ref[p, x] + step_mass * load
            new_vel_ref[p, x] = speed
            new_disp_ref[p, x] = disp_ref[p, x] + TIME_STEP * speed
    if not last:
        store_messages(new_disp_ref, base_ref, node_ref, hot_ref[...], up_ref, down_ref, far_ref)


def per_device(displacement, velocity, moduli, nodal_mass, segment_node, segment_base, contact_bin, element_tile):
    shape = displacement.shape
    _, extent_x, extent_y, extent_z = shape
    steps = contact_bin.shape[0]
    segments = segment_node.shape[0]
    blocks = segments // SEG
    bin_count = lax.axis_size("bin")
    bin_at = lax.axis_index("bin")
    own_device = lax.axis_index("dom") * bin_count + bin_at
    flags = jnp.stack([bin_at > 0, bin_at < bin_count - 1]).astype(F32)
    node = segment_node.reshape(blocks, SEG)
    bins = contact_bin[:, :, 0].astype(F32)
    bins = jnp.pad(bins, ((0, 8 - steps), (0, SEG - blocks)))
    rows = 3 * extent_x
    wide = extent_z + SEG
    struct = lambda *dims: jax.ShapeDtypeStruct(dims, F32)
    layer_rows = 3 * extent_y + 8
    full = lambda *dims: pl.BlockSpec(dims, lambda i: (0,) * len(dims))

    first_outs = [
        struct(rows + 16, wide),
        struct(rows + 8, wide),
        struct(rows + 8, SEG),
        jax.ShapeDtypeStruct((extent_z, segments), BF16),
    ]
    first_args = (displacement, segment_base, node, moduli, bins)
    first_specs = [full(*v.shape) for v in first_args]
    first_specs[3] = pl.BlockSpec((2, extent_x, 8, extent_z), lambda i: (0, 0, extent_y // 8 - 1, 0))
    up, down, far, hot = pl.pallas_call(
        first_body,
        grid=(1,),
        out_shape=first_outs,
        in_specs=first_specs,
        out_specs=[full(*v.shape) for v in first_outs],
        compiler_params=pltpu.CompilerParams(vmem_limit_bytes=60 * 1024 * 1024),
        cost_estimate=pl.CostEstimate(flops=1_000, bytes_accessed=1_000, transcendentals=0),
    )(*first_args)
    (turned,) = call(
        functools.partial(turn_body, extent_z),
        [jax.ShapeDtypeStruct((segments, extent_z), BF16)],
        specs=[WHOLE],
    )(node)
    (tile_places,) = call(
        tile_body, [jax.ShapeDtypeStruct((8, segments), jnp.int32)], specs=[SCALARS] + [WHOLE] * 3
    )(own_device[None].astype(jnp.int32), element_tile, node, hot)
    heat = jnp.zeros((blocks, SEG), F32)
    rim = moduli
    for step in range(steps):
        lower = cycled(up, "bin", 1)
        upper = cycled(down, "bin", -1)
        others = jnp.stack([cycled(far, "bin", shift) for shift in range(2, bin_count - 1)])
        first, last = step == 0, step == steps - 1
        (inner,) = call(
            inner_body,
            [struct(*shape)],
            [pltpu.VMEM((extent_x, 9, extent_y, extent_z), F32), pltpu.VMEM((extent_x + 1, 6, extent_y, extent_z), F32)],
            [WHOLE] * 2,
        )(displacement, moduli)
        if first:
            of_bins = [bins[:steps, :blocks]]
            of_bins += [v[rows : rows + steps, extent_z : extent_z + blocks] for v in (lower, upper)]
            of_bins += [v[rows : rows + steps, :blocks] for v in others]
            all_bins = jnp.concatenate(of_bins, axis=1).astype(jnp.int32)
        layer = lambda at, count=3: pl.BlockSpec((count, 1, extent_y, extent_z), lambda i: (0, at, 0, 0))
        up_rows = layer_rows + (2 * extent_y if first else 0)
        layer_args = [flags, displacement, displacement, lower, upper, inner, others]
        layer_specs = [SCALARS, layer(0), layer(extent_x - 1), full(*lower.shape), full(*upper.shape)]
        layer_specs += [pl.BlockSpec(memory_space=pl.ANY)] * 2
        if first:
            layer_args.append(moduli)
            layer_specs.append(layer(extent_x - 1, 2))
        to_front, to_back = pl.pallas_call(
            functools.partial(layer_body, first),
            grid=(1,),
            out_shape=[struct(up_rows, extent_z), struct(layer_rows, extent_z)],
            in_specs=layer_specs,
            out_specs=[full(up_rows, extent_z), full(layer_rows, extent_z)],
            compiler_params=pltpu.CompilerParams(vmem_limit_bytes=VMEM_BYTES),
            cost_estimate=pl.CostEstimate(flops=1_000, bytes_accessed=1_000, transcendentals=0),
        )(*layer_args)
        back = shifted(to_front, "dom", 1)
        near_blocks = 2 * blocks
        far_blocks = blocks * (bin_count - 2)
        pair_scratch = lambda count: [
            pltpu.VMEM((count + 1, 3, SEG, SEG), F32),
            pltpu.SMEM((bin_count * (count + 2),), jnp.int32),
        ]
        (sums,) = call(
            functools.partial(near_body, bin_count),
            [struct(blocks, 4, 8, SEG)],
            pair_scratch(near_blocks),
            [SCALARS, WHOLE, WHOLE, pl.BlockSpec(memory_space=pl.ANY)],
        )(all_bins[step], far, lower, to_front)
        to_back, sums, back = lax.optimization_barrier((to_back, sums, back))
        front = shifted(to_back, "dom", -1)
        pair_args = [all_bins[step], far, upper, others, sums, node, turned, heat]
        if last:
            pair_args.append(tile_places)
        contact, heat = call(
            functools.partial(rest_body, bin_count, last),
            [struct(3 * extent_x * extent_y, extent_z), struct(8, TILE_DEV) if last else struct(blocks, SEG)],
            pair_scratch(far_blocks) + [pltpu.VMEM((8, segments), F32)],
            [SCALARS] + [WHOLE] * (len(pair_args) - 1),
        )(*pair_args)
        if last:
            heat, back, front = lax.optimization_barrier((heat, back, front))
        update_args = [flags, displacement, velocity, nodal_mass, inner, contact, up, down, lower, upper, back, front, rim]
        update_outs = [struct(*shape), struct(*shape)]
        if not last:
            update_args += [segment_base, node, hot]
            update_outs += [struct(rows, wide), struct(rows, wide), struct(rows, SEG)]
        if first:
            update_outs.append(struct(8, extent_y, extent_z))
        made = call(
            functools.partial(update_body, first, last),
            update_outs,
            [pltpu.VMEM((3, extent_x, extent_z), F32)] * 2 + [pltpu.VMEM((3, extent_y, extent_z), F32)] * 2,
            [SCALARS] + [WHOLE] * (len(update_args) - 1),
        )(*update_args)
        displacement, velocity = made[:2]
        if not last:
            up, down, far = made[2:5]
        if first:
            rim = made[-1]
    tile_heat = heat[1] + shifted(heat[0], "dom", -1) + shifted(heat[2], "dom", 1)
    return displacement, velocity, tile_heat


def solution(mesh):
    placed = (
        P(None, "dom", "bin", None),
        P(None, "dom", "bin", None),
        P(None, "dom", "bin", None),
        P("dom", "bin", None),
        P(("dom", "bin")),
        P(None, ("dom", "bin")),
        P(None, ("dom", "bin"), None),
        P("dom", "bin", None),
    )
    return jax.shard_map(
        per_device,
        mesh=mesh,
        in_specs=placed,
        out_specs=(P(None, "dom", "bin", None), P(None, "dom", "bin", None), P(("dom", "bin"))),
        check_vma=False,
    )
```

profile of v0, /device:TPU:18, one launch (start us, length us, event | category | flops | bytes accessed | tf_op | source)
XLA Modules:
  0.0 109.5 jit_solution(18305295871114568804)
XLA Ops:
  0.6 0.8 convert_element_type.15
  1.4 0.6 pad.4.bins_ref
  2.0 3.2 %shard_map.104 = (f32[40,640]{1,0:T(8,128)}, f32[32,640]{1,0:T(8,128)}, f32[32,128]{1,0:T(8,128)}, bf16[512,1024]{1,0:T(8,128)(2,1)}) custom-call(f32[3,8,16,512]{3,2,1,0:T(8,128)} %refs_1_.3, f32[3,1024]{1,0:T(4,128)} %refs_13_.5, s32[8,128]{1,0:T(8,128)} %bitcast.20, f32[2,8,16,512]{3,2,1,0:T(8,128)} %moduli_ref.9, f32[8,128]{1,0:T(8,128)} %pad.4.bins_ref), custom_call_target="tpu_custom_call" | custom-call | flops 1000 | bytes 1000 | tf_op jit(solution)/shard_map/pallas_call | solution.py:473
  5.2 1.7 %collective-permute-start.1 = (f32[32,640]{1,0:T(8,128)}, f32[32,640]{1,0:T(8,128)S(1)}, u32[]{:S(2)}, u32[]{:S(2)}) collective-permute-start(f32[32,640]{1,0:T(8,128)} %get-tuple-element.57.refs_7_), channel_id=1, source_target_pairs={{0,3},{1,0},{2,1},{3,2},{4,7},{5,4},{6,5},{7,6},{8,11},{9,8},{10,9... | collective-permute-start | bytes 245768 | tf_op jit(solution)/shard_map/ppermute | solution.py:31
  7.0 1.5 %collective-permute-start.2 = (f32[32,128]{1,0:T(8,128)}, f32[32,128]{1,0:T(8,128)S(1)}, u32[]{:S(2)}, u32[]{:S(2)}) collective-permute-start(f32[32,128]{1,0:T(8,128)} %get-tuple-element.58.own_ref.refs_1_), channel_id=1, source_target_pairs={{0,2},{1,3},{2,0},{3,1},{4,6},{5,7},{6,4},{7,5},{8,10},{9,11},{10,... | collective-permute-start | bytes 49160 | tf_op jit(solution)/shard_map/ppermute | solution.py:31
  8.6 2.2 %shard_map.103.refs_5_.refs_4_ = f32[3,8,16,512]{3,2,1,0:T(8,128)S(1)} custom-call(f32[3,8,16,512]{3,2,1,0:T(8,128)S(1)} %copy-done.1, f32[2,8,16,512]{3,2,1,0:T(8,128)S(1)} %copy-done), custom_call_target="tpu_custom_call" | custom-call | flops 1000 | bytes 1000 | tf_op jit(solution)/shard_map/pallas_call | solution.py:497
  10.7 0.5 collective-permute-done.2
  11.3 0.6 shard_map.105
  11.9 3.6 %collective-permute-start.3 = (f32[88,512]{1,0:T(8,128)S(1)}, f32[88,512]{1,0:T(8,128)S(1)}, u32[]{:S(2)}, u32[]{:S(2)}) collective-permute-start(f32[88,512]{1,0:T(8,128)S(1)} %get-tuple-element.60._), channel_id=1, source_target_pairs={{0,4},{4,8},{8,12},{12,16},{16,20},{20,24},{24,28},{1,5},{5,9},{9,... | collective-permute-start | bytes 540680 | tf_op jit(solution)/shard_map/ppermute | solution.py:26
  15.6 3.6 %shard_map.106.refs_4_ = f32[8,4,8,128]{3,2,1,0:T(8,128)S(1)} custom-call(s32[32]{0:T(128)S(1)} %get-tuple-element.115.bins_ref.refs_0_, f32[32,128]{1,0:T(8,128)S(1)} %copy-done.19, f32[40,640]{1,0:T(8,128)S(1)} %collective-permute-done.refs_3_.lower_ref.refs_8_, f32[88,512]{1,0:T(8,128)S(1)} %get-tuple-element.60._), custom_call_target="tpu_custom_call" | custom-call | flops 1000 | bytes 1000 | tf_op jit(solution)/shard_map/pallas_call | solution.py:532
  19.2 0.8 collective-permute-done.3.refs_10_
  20.0 3.5 %collective-permute-start.4 = (f32[56,512]{1,0:T(8,128)S(1)}, f32[56,512]{1,0:T(8,128)S(1)}, u32[]{:S(2)}, u32[]{:S(2)}) collective-permute-start(f32[56,512]{1,0:T(8,128)S(1)} %get-tuple-element.64), channel_id=1, source_target_pairs={{4,0},{8,4},{12,8},{16,12},{20,16},{24,20},{28,24},{5,1},{9,5},{13... | collective-permute-start | bytes 344072 | tf_op jit(solution)/shard_map/ppermute | solution.py:26
  23.5 0.3 shard_map.107.refs_6_
  23.9 4.9 %shard_map.108 = (f32[384,512]{1,0:T(8,128)S(1)}, f32[8,128]{1,0:T(8,128)S(1)}) custom-call(s32[32]{0:T(128)S(1)} %get-tuple-element.115.bins_ref.refs_0_, f32[32,128]{1,0:T(8,128)S(1)} %copy-done.19, f32[32,640]{1,0:T(8,128)S(1)} %copy-done.13, f32[1,32,128]{2,1,0:T(8,128)S(1)} %bitcast.31, f32[8,4,8,128]{3,2,1,0:T(8,128)S(1)} %shard_map.106.refs_4_, ...), custom_call_target="tpu_custom_call" | custom-call | flops 1000 | bytes 1000 | tf_op jit(solution)/shard_map/pallas_call | solution.py:543
  28.9 2.5 %shard_map.109 = (f32[3,8,16,512]{3,2,1,0:T(8,128)S(1)}, f32[3,8,16,512]{3,2,1,0:T(8,128)S(1)}, f32[24,640]{1,0:T(8,128)S(1)}, f32[24,640]{1,0:T(8,128)S(1)}, f3...) custom-call(f32[2]{0:T(128)S(1)} %add_convert_fusion.refs_0_, f32[3,8,16,512]{3,2,1,0:T(8,128)S(1)} %copy-done.1, ...), custom_call_target="tpu_custom_call" | custom-call | flops 1000 | bytes 1000 | tf_op jit(solution)/shard_map/pallas_call | solution.py:558
  31.4 0.5 collective-permute-start.7
  31.9 0.8 collective-permute-start.6
  32.7 2.2 %shard_map.110.refs_5_.refs_4_ = f32[3,8,16,512]{3,2,1,0:T(8,128)S(1)} custom-call(f32[3,8,16,512]{3,2,1,0:T(8,128)S(1)} %get-tuple-element.66.disp_ref.refs_1_.refs_2_, f32[2,8,16,512]{3,2,1,0:T(8,128)S(1)} %copy-done), custom_call_target="tpu_custom_call" | custom-call | flops 1000 | bytes 1000 | tf_op jit(solution)/shard_map/pallas_call | solution.py:497
  34.9 0.8 collective-permute-done.6
  35.6 0.6 shard_map.111
  36.2 3.1 %collective-permute-start.8 = (f32[56,512]{1,0:T(8,128)S(1)}, f32[56,512]{1,0:T(8,128)S(1)}, u32[]{:S(2)}, u32[]{:S(2)}) collective-permute-start(f32[56,512]{1,0:T(8,128)S(1)} %get-tuple-element.72._), channel_id=1, source_target_pairs={{0,4},{4,8},{8,12},{12,16},{16,20},{20,24},{24,28},{1,5},{5,9},{9,... | collective-permute-start | bytes 344072 | tf_op jit(solution)/shard_map/ppermute | solution.py:26
  39.3 3.9 %shard_map.112.refs_4_ = f32[8,4,8,128]{3,2,1,0:T(8,128)S(1)} custom-call(s32[32]{0:T(128)S(1)} %get-tuple-element.114.bins_ref.refs_0_, f32[24,128]{1,0:T(8,128)S(1)} %get-tuple-element.68.own_ref.refs_1_, f32[24,640]{1,0:T(8,128)S(1)} %collective-permute-done.7.refs_3_.lower_ref.refs_8_, f32[56,512]{1,0:T(8,128)S(1)} %get-tuple-element.72._), custom_call_target="tpu_custom_call" | custom-call | flops 1000 | bytes 1000 | tf_op jit(solution)/shard_map/pallas_call | solution.py:532
  43.2 3.4 %collective-permute-start.9 = (f32[56,512]{1,0:T(8,128)S(1)}, f32[56,512]{1,0:T(8,128)S(1)}, u32[]{:S(2)}, u32[]{:S(2)}) collective-permute-start(f32[56,512]{1,0:T(8,128)S(1)} %get-tuple-element.77), channel_id=1, source_target_pairs={{4,0},{8,4},{12,8},{16,12},{20,16},{24,20},{28,24},{5,1},{9,5},{13... | collective-permute-start | bytes 344072 | tf_op jit(solution)/shard_map/ppermute | solution.py:26
  46.6 4.9 %shard_map.113 = (f32[384,512]{1,0:T(8,128)S(1)}, f32[8,128]{1,0:T(8,128)S(1)}) custom-call(s32[32]{0:T(128)S(1)} %get-tuple-element.114.bins_ref.refs_0_, f32[24,128]{1,0:T(8,128)S(1)} %get-tuple-element.68.own_ref.refs_1_, f32[24,640]{1,0:T(8,128)S(1)} %collective-permute-done.5.refs_4_.refs_2_.refs_9_, f32[1,24,128]{2,1,0:T(8,128)S(1)} %bitcast.35, ...), custom_call_target="tpu_custom_call" | custom-call | flops 1000 | bytes 1000 | tf_op jit(solution)/shard_map/pallas_call | solution.py:543
  51.5 2.4 %shard_map.114 = (f32[3,8,16,512]{3,2,1,0:T(8,128)S(1)}, f32[3,8,16,512]{3,2,1,0:T(8,128)S(1)}, f32[24,640]{1,0:T(8,128)S(1)}, f32[24,640]{1,0:T(8,128)S(1)}, f32[24,128]{1,0:T(8,128)S(1)}) custom-call(f32[2]{0:T(128)S(1)} %add_convert_fusion.refs_0_, f32[3,8,16,512]{3,2,1,0:T(8,128)S(1)} %get-tuple-element.66.disp_ref.refs_1_.refs_2_, ...), custom_call_target="tpu_custom_call" | custom-call | flops 1000 | bytes 1000 | tf_op jit(solution)/shard_map/pallas_call | solution.py:558
  54.0 0.5 collective-permute-start.12
  54.5 0.9 collective-permute-start.11
  55.4 2.2 %shard_map.115.refs_5_.refs_4_ = f32[3,8,16,512]{3,2,1,0:T(8,128)S(1)} custom-call(f32[3,8,16,512]{3,2,1,0:T(8,128)S(1)} %get-tuple-element.79.disp_ref.refs_1_.refs_2_, f32[2,8,16,512]{3,2,1,0:T(8,128)S(1)} %copy-done), custom_call_target="tpu_custom_call" | custom-call | flops 1000 | bytes 1000 | tf_op jit(solution)/shard_map/pallas_call | solution.py:497
  57.6 0.6 collective-permute-done.11
  58.2 0.6 shard_map.116
  58.8 3.5 %collective-permute-start.13 = (f32[56,512]{1,0:T(8,128)S(1)}, f32[56,512]{1,0:T(8,128)S(1)}, u32[]{:S(2)}, u32[]{:S(2)}) collective-permute-start(f32[56,512]{1,0:T(8,128)S(1)} %get-tuple-element.85._), channel_id=1, source_target_pairs={{0,4},{4,8},{8,12},{12,16},{16,20},{20,24},{24,28},{1,5},{5,9},{9,... | collective-permute-start | bytes 344072 | tf_op jit(solution)/shard_map/ppermute | solution.py:26
  62.3 3.9 %shard_map.117.refs_4_ = f32[8,4,8,128]{3,2,1,0:T(8,128)S(1)} custom-call(s32[32]{0:T(128)S(1)} %get-tuple-element.113.bins_ref.refs_0_, f32[24,128]{1,0:T(8,128)S(1)} %get-tuple-element.81.own_ref.refs_1_, f32[24,640]{1,0:T(8,128)S(1)} %collective-permute-done.12.refs_3_.lower_ref.refs_8_, f32[56,512]{1,0:T(8,128)S(1)} %get-tuple-element.85._), custom_call_target="tpu_custom_call" | custom-call | flops 1000 | bytes 1000 | tf_op jit(solution)/shard_map/pallas_call | solution.py:532
  66.2 3.5 %collective-permute-start.14 = (f32[56,512]{1,0:T(8,128)S(1)}, f32[56,512]{1,0:T(8,128)S(1)}, u32[]{:S(2)}, u32[]{:S(2)}) collective-permute-start(f32[56,512]{1,0:T(8,128)S(1)} %get-tuple-element.90), channel_id=1, source_target_pairs={{4,0},{8,4},{12,8},{16,12},{20,16},{24,20},{28,24},{5,1},{9,5},{13... | collective-permute-start | bytes 344072 | tf_op jit(solution)/shard_map/ppermute | solution.py:26
  69.7 4.6 %shard_map.118 = (f32[384,512]{1,0:T(8,128)S(1)}, f32[8,128]{1,0:T(8,128)S(1)}) custom-call(s32[32]{0:T(128)S(1)} %get-tuple-element.113.bins_ref.refs_0_, f32[24,128]{1,0:T(8,128)S(1)} %get-tuple-element.81.own_ref.refs_1_, f32[24,640]{1,0:T(8,128)S(1)} %collective-permute-done.10.refs_4_.refs_2_.refs_9_, f32[1,24,128]{2,1,0:T(8,128)S(1)} %bitcast.37, ...), custom_call_target="tpu_custom_call" | custom-call | flops 1000 | bytes 1000 | tf_op jit(solution)/shard_map/pallas_call | solution.py:543
  74.3 2.4 %shard_map.119 = (f32[3,8,16,512]{3,2,1,0:T(8,128)S(1)}, f32[3,8,16,512]{3,2,1,0:T(8,128)S(1)}, f32[24,640]{1,0:T(8,128)S(1)}, f32[24,640]{1,0:T(8,128)S(1)}, f32[24,128]{1,0:T(8,128)S(1)}) custom-call(f32[2]{0:T(128)S(1)} %add_convert_fusion.refs_0_, f32[3,8,16,512]{3,2,1,0:T(8,128)S(1)} %get-tuple-element.79.disp_ref.refs_1_.refs_2_, ...), custom_call_target="tpu_custom_call" | custom-call | flops 1000 | bytes 1000 | tf_op jit(solution)/shard_map/pallas_call | solution.py:558
  76.8 0.5 collective-permute-start.17
  77.3 1.3 %collective-permute-start.16 = (f32[24,128]{1,0:T(8,128)S(1)}, f32[24,128]{1,0:T(8,128)S(1)}, u32[]{:S(2)}, u32[]{:S(2)}) collective-permute-start(f32[24,128]{1,0:T(8,128)S(1)} %get-tuple-element.93.own_ref.refs_1_), channel_id=1, source_target_pairs={{0,2},{1,3},{2,0},{3,1},{4,6},{5,7},{6,4},{7,5},{8,10},{9,11},{10,... | collective-permute-start | bytes 36872 | tf_op jit(solution)/shard_map/ppermute | solution.py:31
  78.7 2.2 %shard_map.120.refs_5_.refs_4_ = f32[3,8,16,512]{3,2,1,0:T(8,128)S(1)} custom-call(f32[3,8,16,512]{3,2,1,0:T(8,128)S(1)} %get-tuple-element.91.disp_ref.refs_1_.refs_2_, f32[2,8,16,512]{3,2,1,0:T(8,128)S(1)} %copy-done), custom_call_target="tpu_custom_call" | custom-call | flops 1000 | bytes 1000 | tf_op jit(solution)/shard_map/pallas_call | solution.py:497
  81.2 1.2 %shard_map.121 = (f32[56,512]{1,0:T(8,128)S(1)}, f32[56,512]{1,0:T(8,128)}) custom-call(f32[2]{0:T(128)S(1)} %add_convert_fusion.refs_0_, f32[3,8,16,512]{3,2,1,0:T(8,128)S(1)} %get-tuple-element.91.disp_ref.refs_1_.refs_2_, f32[3,8,16,512]{3,2,1,0:T(8,128)S(1)} %get-tuple-element.91.disp_ref.refs_1_.refs_2_, ...), custom_call_target="tpu_custom_call" | custom-call | flops 1000 | bytes 1000 | tf_op jit(solution)/shard_map/pallas_call | solution.py:516
  82.4 3.6 %collective-permute-start.18 = (f32[56,512]{1,0:T(8,128)S(1)}, f32[56,512]{1,0:T(8,128)S(1)}, u32[]{:S(2)}, u32[]{:S(2)}) collective-permute-start(f32[56,512]{1,0:T(8,128)S(1)} %get-tuple-element.97._), channel_id=1, source_target_pairs={{0,4},{4,8},{8,12},{12,16},{16,20},{20,24},{24,28},{1,5},{5,9},{9,... | collective-permute-start | bytes 344072 | tf_op jit(solution)/shard_map/ppermute | solution.py:26
  86.0 3.6 %shard_map.122.refs_4_ = f32[8,4,8,128]{3,2,1,0:T(8,128)S(1)} custom-call(s32[32]{0:T(128)S(1)} %get-tuple-element.112.bins_ref.refs_0_, f32[24,128]{1,0:T(8,128)S(1)} %get-tuple-element.93.own_ref.refs_1_, f32[24,640]{1,0:T(8,128)S(1)} %collective-permute-done.17.refs_3_.lower_ref.refs_8_, f32[56,512]{1,0:T(8,128)S(1)} %get-tuple-element.97._), custom_call_target="tpu_custom_call" | custom-call | flops 1000 | bytes 1000 | tf_op jit(solution)/shard_map/pallas_call | solution.py:532
  89.6 3.5 %collective-permute-start.19 = (f32[56,512]{1,0:T(8,128)}, f32[56,512]{1,0:T(8,128)}, u32[]{:S(2)}, u32[]{:S(2)}) collective-permute-start(f32[56,512]{1,0:T(8,128)} %get-tuple-element.103), channel_id=1, source_target_pairs={{4,0},{8,4},{12,8},{16,12},{20,16},{24,20},{28,24},{5,1},{9,5},{13... | collective-permute-start | bytes 344072 | tf_op jit(solution)/shard_map/ppermute | solution.py:26
  93.1 0.5 shard_map.123.refs_8_
  93.8 5.3 %shard_map.124 = (f32[384,512]{1,0:T(8,128)S(1)}, f32[8,256]{1,0:T(8,128)S(1)}) custom-call(s32[32]{0:T(128)S(1)} %copy-done.27, f32[24,128]{1,0:T(8,128)S(1)} %copy-done.25, f32[24,640]{1,0:T(8,128)S(1)} %collective-permute-done.15.refs_4_.refs_2_.refs_9_, f32[1,24,128]{2,1,0:T(8,128)S(1)} %bitcast.33, f32[8,4,8,128]{3,2,1,0:T(8,128)S(1)} %shard_map.122.refs_4_, ...), custom_call_target="tpu_custom_call" | custom-call | flops 1000 | bytes 1000 | tf_op jit(solution)/shard_map/pallas_call | solution.py:543
  99.1 2.4 %collective-permute-start.20 = (f32[256]{0:T(256)S(1)}, f32[256]{0:T(256)S(1)}, u32[]{:S(2)}, u32[]{:S(2)}) collective-permute-start(f32[256]{0:T(256)S(1)} %bitcast.42), channel_id=1, source_target_pairs={{4,0},{8,4},{12,8},{16,12},{20,16},{24,20},{28,24},{5,1},{9,5},{13... | collective-permute-start | bytes 3080 | tf_op jit(solution)/shard_map/ppermute | solution.py:26
  101.5 4.3 %collective-permute-start.21 = (f32[256]{0:T(256)S(1)}, f32[256]{0:T(256)S(1)}, u32[]{:S(2)}, u32[]{:S(2)}) collective-permute-start(f32[256]{0:T(256)S(1)} %bitcast.41), channel_id=1, source_target_pairs={{0,4},{4,8},{8,12},{12,16},{16,20},{20,24},{24,28},{1,5},{5,9},{9,... | collective-permute-start | bytes 3080 | tf_op jit(solution)/shard_map/ppermute | solution.py:26
  105.9 3.1 %shard_map.125 = (f32[3,8,16,512]{3,2,1,0:T(8,128)}, f32[3,8,16,512]{3,2,1,0:T(8,128)}) custom-call(f32[2]{0:T(128)S(1)} %add_convert_fusion.refs_0_, f32[3,8,16,512]{3,2,1,0:T(8,128)S(1)} %get-tuple-element.91.disp_ref.refs_1_.refs_2_, f32[3,8,16,512]{3,2,1,0:T(8,128)S(1)} %copy-done.11, f32[8,16,512]{2,1,0:T(8,128)S(1)} %copy-done.6, ...), custom_call_target="tpu_custom_call" | custom-call | flops 1000 | bytes 1000 | tf_op jit(solution)/shard_map/pallas_call | solution.py:558
  109.0 0.6 add_add_fusion
  (86 shorter events, 1.0 us)
Async XLA Ops:
  0.6 7.9 %copy-start.1 = (f32[3,8,16,512]{3,2,1,0:T(8,128)S(1)}, f32[3,8,16,512]{3,2,1,0:T(8,128)}, u32[]{:S(2)}) copy-start(f32[3,8,16,512]{3,2,1,0:T(8,128)} %refs_1_.3) | copy-start | bytes 2359300
  2.0 6.6 %copy-start = (f32[2,8,16,512]{3,2,1,0:T(8,128)S(1)}, f32[2,8,16,512]{3,2,1,0:T(8,128)}, u32[]{:S(2)}) copy-start(f32[2,8,16,512]{3,2,1,0:T(8,128)} %moduli_ref.9) | copy-start | bytes 1572868
  5.2 6.1 %collective-permute-start = (f32[40,640]{1,0:T(8,128)}, f32[40,640]{1,0:T(8,128)S(1)}, u32[]{:S(2)}, u32[]{:S(2)}) collective-permute-start(f32[40,640]{1,0:T(8,128)} %get-tuple-element.56.refs_6_), channel_id=1, source_target_pairs={{0,1},{1,2},{2,3},{3,0},{4,5},{5,6},{6,7},{7,4},{8,9},{9,10},{10,1... | collective-permute-start | bytes 307208 | tf_op jit(solution)/shard_map/ppermute | solution.py:31
  5.2 6.1 %collective-permute-start.1 = (f32[32,640]{1,0:T(8,128)}, f32[32,640]{1,0:T(8,128)S(1)}, u32[]{:S(2)}, u32[]{:S(2)}) collective-permute-start(f32[32,640]{1,0:T(8,128)} %get-tuple-element.57.refs_7_), channel_id=1, source_target_pairs={{0,3},{1,0},{2,1},{3,2},{4,7},{5,4},{6,5},{7,6},{8,11},{9,8},{10,9... | collective-permute-start | bytes 245768 | tf_op jit(solution)/shard_map/ppermute | solution.py:31
  7.0 4.3 %collective-permute-start.2 = (f32[32,128]{1,0:T(8,128)}, f32[32,128]{1,0:T(8,128)S(1)}, u32[]{:S(2)}, u32[]{:S(2)}) collective-permute-start(f32[32,128]{1,0:T(8,128)} %get-tuple-element.58.own_ref.refs_1_), channel_id=1, source_target_pairs={{0,2},{1,3},{2,0},{3,1},{4,6},{5,7},{6,4},{7,5},{8,10},{9,11},{10,... | collective-permute-start | bytes 49160 | tf_op jit(solution)/shard_map/ppermute | solution.py:31
  11.9 3.7 %copy-start.19 = (f32[32,128]{1,0:T(8,128)S(1)}, f32[32,128]{1,0:T(8,128)}, u32[]{:S(2)}) copy-start(f32[32,128]{1,0:T(8,128)} %get-tuple-element.58.own_ref.refs_1_) | copy-start | bytes 49156
  11.9 8.1 %collective-permute-start.3 = (f32[88,512]{1,0:T(8,128)S(1)}, f32[88,512]{1,0:T(8,128)S(1)}, u32[]{:S(2)}, u32[]{:S(2)}) collective-permute-start(f32[88,512]{1,0:T(8,128)S(1)} %get-tuple-element.60._), channel_id=1, source_target_pairs={{0,4},{4,8},{8,12},{12,16},{16,20},{20,24},{24,28},{1,5},{5,9},{9,... | collective-permute-start | bytes 540680 | tf_op jit(solution)/shard_map/ppermute | solution.py:26
  15.6 70.4 %copy-start.26 = (s32[32]{0:T(128)}, s32[32]{0:T(128)S(1)}, u32[]{:S(2)}) copy-start(s32[32]{0:T(128)S(1)} %get-tuple-element.112.bins_ref.refs_0_) | copy-start | bytes 388
  15.6 7.9 %copy-start.14 = (s32[1024]{0:T(1024)S(1)}, s32[1024]{0:T(1024)}, u32[]{:S(2)}) copy-start(s32[1024]{0:T(1024)} %param.12) | copy-start | bytes 12292
  15.6 13.2 %copy-start.18 = (f32[32,640]{1,0:T(8,128)S(1)}, f32[32,640]{1,0:T(8,128)}, u32[]{:S(2)}) copy-start(f32[32,640]{1,0:T(8,128)} %get-tuple-element.57.refs_7_) | copy-start | bytes 245764
  20.0 3.8 %copy-start.13 = (f32[32,640]{1,0:T(8,128)S(1)}, f32[32,640]{1,0:T(8,128)}, u32[]{:S(2)}) copy-start(f32[32,640]{1,0:T(8,128)} %copy-done.12) | copy-start | bytes 245764
  20.0 8.8 %copy-start.2 = (bf16[512,1024]{1,0:T(8,128)(2,1)S(1)}, bf16[512,1024]{1,0:T(8,128)(2,1)}, u32[]{:S(2)}) copy-start(bf16[512,1024]{1,0:T(8,128)(2,1)} %get-tuple-element.65.refs_15_.hot_ref) | copy-start | bytes 3145732
  20.0 8.8 %collective-permute-start.4 = (f32[56,512]{1,0:T(8,128)S(1)}, f32[56,512]{1,0:T(8,128)S(1)}, u32[]{:S(2)}, u32[]{:S(2)}) collective-permute-start(f32[56,512]{1,0:T(8,128)S(1)} %get-tuple-element.64), channel_id=1, source_target_pairs={{4,0},{8,4},{12,8},{16,12},{20,16},{24,20},{28,24},{5,1},{9,5},{13... | collective-permute-start | bytes 344072 | tf_op jit(solution)/shard_map/ppermute | solution.py:26
  23.8 5.0 %copy-start.9 = (f32[3,8,16,512]{3,2,1,0:T(8,128)S(1)}, f32[3,8,16,512]{3,2,1,0:T(8,128)}, u32[]{:S(2)}) copy-start(f32[3,8,16,512]{3,2,1,0:T(8,128)} %refs_2_.3) | copy-start | bytes 2359300
  23.9 5.0 %copy-start.5 = (f32[8,16,512]{2,1,0:T(8,128)S(1)}, f32[8,16,512]{2,1,0:T(8,128)}, u32[]{:S(2)}) copy-start(f32[8,16,512]{2,1,0:T(8,128)} %refs_3_.7) | copy-start | bytes 786436
  23.9 5.0 %copy-start.15 = (f32[3,1024]{1,0:T(4,128)S(1)}, f32[3,1024]{1,0:T(4,128)}, u32[]{:S(2)}) copy-start(f32[3,1024]{1,0:T(4,128)} %refs_13_.5) | copy-start | bytes 36868
  23.9 5.0 %copy-start.17 = (f32[40,640]{1,0:T(8,128)S(1)}, f32[40,640]{1,0:T(8,128)}, u32[]{:S(2)}) copy-start(f32[40,640]{1,0:T(8,128)} %get-tuple-element.56.refs_6_) | copy-start | bytes 307204
  31.3 43.0 %copy-start.7 = (f32[8,16,512]{2,1,0:T(8,128)}, f32[8,16,512]{2,1,0:T(8,128)S(1)}, u32[]{:S(2)}) copy-start(f32[8,16,512]{2,1,0:T(8,128)S(1)} %get-tuple-element.78.refs_12_) | copy-start | bytes 786436
  31.4 4.3 %collective-permute-start.5 = (f32[24,640]{1,0:T(8,128)S(1)}, f32[24,640]{1,0:T(8,128)S(1)}, u32[]{:S(2)}, u32[]{:S(2)}) collective-permute-start(f32[24,640]{1,0:T(8,128)S(1)} %get-tuple-element.69.refs_7_), channel_id=1, source_target_pairs={{0,3},{1,0},{2,1},{3,2},{4,7},{5,4},{6,5},{7,6},{8,11},{9,8},{10,9... | collective-permute-start | bytes 184328 | tf_op jit(solution)/shard_map/ppermute | solution.py:31
  31.4 4.2 %collective-permute-start.7 = (f32[24,640]{1,0:T(8,128)S(1)}, f32[24,640]{1,0:T(8,128)S(1)}, u32[]{:S(2)}, u32[]{:S(2)}) collective-permute-start(f32[24,640]{1,0:T(8,128)S(1)} %get-tuple-element.70.refs_6_), channel_id=1, source_target_pairs={{0,1},{1,2},{2,3},{3,0},{4,5},{5,6},{6,7},{7,4},{8,9},{9,10},{10,1... | collective-permute-start | bytes 184328 | tf_op jit(solution)/shard_map/ppermute | solution.py:31
  31.9 3.7 %collective-permute-start.6 = (f32[24,128]{1,0:T(8,128)S(1)}, f32[24,128]{1,0:T(8,128)S(1)}, u32[]{:S(2)}, u32[]{:S(2)}) collective-permute-start(f32[24,128]{1,0:T(8,128)S(1)} %get-tuple-element.68.own_ref.refs_1_), channel_id=1, source_target_pairs={{0,2},{1,3},{2,0},{3,1},{4,6},{5,7},{6,4},{7,5},{8,10},{9,11},{10,... | collective-permute-start | bytes 36872 | tf_op jit(solution)/shard_map/ppermute | solution.py:31
  36.2 7.0 %collective-permute-start.8 = (f32[56,512]{1,0:T(8,128)S(1)}, f32[56,512]{1,0:T(8,128)S(1)}, u32[]{:S(2)}, u32[]{:S(2)}) collective-permute-start(f32[56,512]{1,0:T(8,128)S(1)} %get-tuple-element.72._), channel_id=1, source_target_pairs={{0,4},{4,8},{8,12},{12,16},{16,20},{20,24},{24,28},{1,5},{5,9},{9,... | collective-permute-start | bytes 344072 | tf_op jit(solution)/shard_map/ppermute | solution.py:26
  43.2 8.3 %collective-permute-start.9 = (f32[56,512]{1,0:T(8,128)S(1)}, f32[56,512]{1,0:T(8,128)S(1)}, u32[]{:S(2)}, u32[]{:S(2)}) collective-permute-start(f32[56,512]{1,0:T(8,128)S(1)} %get-tuple-element.77), channel_id=1, source_target_pairs={{4,0},{8,4},{12,8},{16,12},{20,16},{24,20},{28,24},{5,1},{9,5},{13... | collective-permute-start | bytes 344072 | tf_op jit(solution)/shard_map/ppermute | solution.py:26
  53.9 4.3 %collective-permute-start.10 = (f32[24,640]{1,0:T(8,128)S(1)}, f32[24,640]{1,0:T(8,128)S(1)}, u32[]{:S(2)}, u32[]{:S(2)}) collective-permute-start(f32[24,640]{1,0:T(8,128)S(1)} %get-tuple-element.82.refs_7_), channel_id=1, source_target_pairs={{0,3},{1,0},{2,1},{3,2},{4,7},{5,4},{6,5},{7,6},{8,11},{9,8},{10,9... | collective-permute-start | bytes 184328 | tf_op jit(solution)/shard_map/ppermute | solution.py:31
  54.0 4.2 %collective-permute-start.12 = (f32[24,640]{1,0:T(8,128)S(1)}, f32[24,640]{1,0:T(8,128)S(1)}, u32[]{:S(2)}, u32[]{:S(2)}) collective-permute-start(f32[24,640]{1,0:T(8,128)S(1)} %get-tuple-element.83.refs_6_), channel_id=1, source_target_pairs={{0,1},{1,2},{2,3},{3,0},{4,5},{5,6},{6,7},{7,4},{8,9},{9,10},{10,1... | collective-permute-start | bytes 184328 | tf_op jit(solution)/shard_map/ppermute | solution.py:31
  54.5 3.7 %collective-permute-start.11 = (f32[24,128]{1,0:T(8,128)S(1)}, f32[24,128]{1,0:T(8,128)S(1)}, u32[]{:S(2)}, u32[]{:S(2)}) collective-permute-start(f32[24,128]{1,0:T(8,128)S(1)} %get-tuple-element.81.own_ref.refs_1_), channel_id=1, source_target_pairs={{0,2},{1,3},{2,0},{3,1},{4,6},{5,7},{6,4},{7,5},{8,10},{9,11},{10,... | collective-permute-start | bytes 36872 | tf_op jit(solution)/shard_map/ppermute | solution.py:31
  58.8 7.5 %collective-permute-start.13 = (f32[56,512]{1,0:T(8,128)S(1)}, f32[56,512]{1,0:T(8,128)S(1)}, u32[]{:S(2)}, u32[]{:S(2)}) collective-permute-start(f32[56,512]{1,0:T(8,128)S(1)} %get-tuple-element.85._), channel_id=1, source_target_pairs={{0,4},{4,8},{8,12},{12,16},{16,20},{20,24},{24,28},{1,5},{5,9},{9,... | collective-permute-start | bytes 344072 | tf_op jit(solution)/shard_map/ppermute | solution.py:26
  66.2 8.0 %collective-permute-start.14 = (f32[56,512]{1,0:T(8,128)S(1)}, f32[56,512]{1,0:T(8,128)S(1)}, u32[]{:S(2)}, u32[]{:S(2)}) collective-permute-start(f32[56,512]{1,0:T(8,128)S(1)} %get-tuple-element.90), channel_id=1, source_target_pairs={{4,0},{8,4},{12,8},{16,12},{20,16},{24,20},{28,24},{5,1},{9,5},{13... | collective-permute-start | bytes 344072 | tf_op jit(solution)/shard_map/ppermute | solution.py:26
  76.7 4.1 %copy-start.10 = (f32[3,8,16,512]{3,2,1,0:T(8,128)}, f32[3,8,16,512]{3,2,1,0:T(8,128)S(1)}, u32[]{:S(2)}) copy-start(f32[3,8,16,512]{3,2,1,0:T(8,128)S(1)} %get-tuple-element.92.refs_2_) | copy-start | bytes 2359300
  76.8 4.1 %copy-start.20 = (f32[24,640]{1,0:T(8,128)}, f32[24,640]{1,0:T(8,128)S(1)}, u32[]{:S(2)}) copy-start(f32[24,640]{1,0:T(8,128)S(1)} %get-tuple-element.95.refs_6_) | copy-start | bytes 184324
  76.8 4.1 %copy-start.22 = (f32[24,640]{1,0:T(8,128)}, f32[24,640]{1,0:T(8,128)S(1)}, u32[]{:S(2)}) copy-start(f32[24,640]{1,0:T(8,128)S(1)} %get-tuple-element.94.refs_7_) | copy-start | bytes 184324
  76.8 9.2 %copy-start.24 = (f32[24,128]{1,0:T(8,128)}, f32[24,128]{1,0:T(8,128)S(1)}, u32[]{:S(2)}) copy-start(f32[24,128]{1,0:T(8,128)S(1)} %get-tuple-element.93.own_ref.refs_1_) | copy-start | bytes 36868
  76.8 4.4 %collective-permute-start.15 = (f32[24,640]{1,0:T(8,128)S(1)}, f32[24,640]{1,0:T(8,128)S(1)}, u32[]{:S(2)}, u32[]{:S(2)}) collective-permute-start(f32[24,640]{1,0:T(8,128)S(1)} %get-tuple-element.94.refs_7_), channel_id=1, source_target_pairs={{0,3},{1,0},{2,1},{3,2},{4,7},{5,4},{6,5},{7,6},{8,11},{9,8},{10,9... | collective-permute-start | bytes 184328 | tf_op jit(solution)/shard_map/ppermute | solution.py:31
  76.8 4.3 %collective-permute-start.17 = (f32[24,640]{1,0:T(8,128)S(1)}, f32[24,640]{1,0:T(8,128)S(1)}, u32[]{:S(2)}, u32[]{:S(2)}) collective-permute-start(f32[24,640]{1,0:T(8,128)S(1)} %get-tuple-element.95.refs_6_), channel_id=1, source_target_pairs={{0,1},{1,2},{2,3},{3,0},{4,5},{5,6},{6,7},{7,4},{8,9},{9,10},{10,1... | collective-permute-start | bytes 184328 | tf_op jit(solution)/shard_map/ppermute | solution.py:31
  77.3 3.8 %collective-permute-start.16 = (f32[24,128]{1,0:T(8,128)S(1)}, f32[24,128]{1,0:T(8,128)S(1)}, u32[]{:S(2)}, u32[]{:S(2)}) collective-permute-start(f32[24,128]{1,0:T(8,128)S(1)} %get-tuple-element.93.own_ref.refs_1_), channel_id=1, source_target_pairs={{0,2},{1,3},{2,0},{3,1},{4,6},{5,7},{6,4},{7,5},{8,10},{9,11},{10,... | collective-permute-start | bytes 36872 | tf_op jit(solution)/shard_map/ppermute | solution.py:31
  80.9 1.5 %copy-start.3 = (f32[3,8,16,512]{3,2,1,0:T(8,128)}, f32[3,8,16,512]{3,2,1,0:T(8,128)S(1)}, u32[]{:S(2)}) copy-start(f32[3,8,16,512]{3,2,1,0:T(8,128)S(1)} %shard_map.120.refs_5_.refs_4_) | copy-start | bytes 2359300
  82.4 10.7 %copy-start.16 = (s32[8,16,512]{2,1,0:T(8,128)S(1)}, s32[8,16,512]{2,1,0:T(8,128)}, u32[]{:S(2)}) copy-start(s32[8,16,512]{2,1,0:T(8,128)} %tiles_ref.1) | copy-start | bytes 786436
  82.4 7.2 %collective-permute-start.18 = (f32[56,512]{1,0:T(8,128)S(1)}, f32[56,512]{1,0:T(8,128)S(1)}, u32[]{:S(2)}, u32[]{:S(2)}) collective-permute-start(f32[56,512]{1,0:T(8,128)S(1)} %get-tuple-element.97._), channel_id=1, source_target_pairs={{0,4},{4,8},{8,12},{12,16},{16,20},{20,24},{24,28},{1,5},{5,9},{9,... | collective-permute-start | bytes 344072 | tf_op jit(solution)/shard_map/ppermute | solution.py:26
  89.6 9.5 %collective-permute-start.19 = (f32[56,512]{1,0:T(8,128)}, f32[56,512]{1,0:T(8,128)}, u32[]{:S(2)}, u32[]{:S(2)}) collective-permute-start(f32[56,512]{1,0:T(8,128)} %get-tuple-element.103), channel_id=1, source_target_pairs={{4,0},{8,4},{12,8},{16,12},{20,16},{24,20},{28,24},{5,1},{9,5},{13... | collective-permute-start | bytes 344072 | tf_op jit(solution)/shard_map/ppermute | solution.py:26
  93.1 0.7 copy-start.25
  93.1 12.7 %copy-start.11 = (f32[3,8,16,512]{3,2,1,0:T(8,128)S(1)}, f32[3,8,16,512]{3,2,1,0:T(8,128)}, u32[]{:S(2)}) copy-start(f32[3,8,16,512]{3,2,1,0:T(8,128)} %copy-done.10) | copy-start | bytes 2359300
  93.1 12.7 %copy-start.21 = (f32[24,640]{1,0:T(8,128)S(1)}, f32[24,640]{1,0:T(8,128)}, u32[]{:S(2)}) copy-start(f32[24,640]{1,0:T(8,128)} %copy-done.20) | copy-start | bytes 184324
  93.1 12.7 %copy-start.23 = (f32[24,640]{1,0:T(8,128)S(1)}, f32[24,640]{1,0:T(8,128)}, u32[]{:S(2)}) copy-start(f32[24,640]{1,0:T(8,128)} %copy-done.22) | copy-start | bytes 184324
  93.6 12.2 %copy-start.4 = (f32[3,8,16,512]{3,2,1,0:T(8,128)S(1)}, f32[3,8,16,512]{3,2,1,0:T(8,128)}, u32[]{:S(2)}) copy-start(f32[3,8,16,512]{3,2,1,0:T(8,128)} %copy-done.3) | copy-start | bytes 2359300
  93.8 12.1 %copy-start.6 = (f32[8,16,512]{2,1,0:T(8,128)S(1)}, f32[8,16,512]{2,1,0:T(8,128)}, u32[]{:S(2)}) copy-start(f32[8,16,512]{2,1,0:T(8,128)} %refs_3_.7) | copy-start | bytes 786436
  93.8 12.1 %copy-start.8 = (f32[8,16,512]{2,1,0:T(8,128)S(1)}, f32[8,16,512]{2,1,0:T(8,128)}, u32[]{:S(2)}) copy-start(f32[8,16,512]{2,1,0:T(8,128)} %copy-done.7) | copy-start | bytes 786436
  99.1 9.9 %collective-permute-start.20 = (f32[256]{0:T(256)S(1)}, f32[256]{0:T(256)S(1)}, u32[]{:S(2)}, u32[]{:S(2)}) collective-permute-start(f32[256]{0:T(256)S(1)} %bitcast.42), channel_id=1, source_target_pairs={{4,0},{8,4},{12,8},{16,12},{20,16},{24,20},{28,24},{5,1},{9,5},{13... | collective-permute-start | bytes 3080 | tf_op jit(solution)/shard_map/ppermute | solution.py:26
  101.5 7.4 %collective-permute-start.21 = (f32[256]{0:T(256)S(1)}, f32[256]{0:T(256)S(1)}, u32[]{:S(2)}, u32[]{:S(2)}) collective-permute-start(f32[256]{0:T(256)S(1)} %bitcast.41), channel_id=1, source_target_pairs={{0,4},{4,8},{8,12},{12,16},{16,20},{20,24},{24,28},{1,5},{5,9},{9,... | collective-permute-start | bytes 3080 | tf_op jit(solution)/shard_map/ppermute | solution.py:26
  (2 other events, 1.3 us)
where the time goes:
time: 110 us
  Pallas kernels  60.6 us (55%)
  starting transfers between devices  42.2 us (38%)
  waiting for transfers between devices  3.02 us (3%)
  other arithmetic  1.48 us (1%)
  between operations  1.29 us (1%)
    ppermute x10, starting transfers between devices, shifted(): lax.ppermute(value, axis, [(source, source + steps) for source in range(f...  34.2 us
    pallas_call x4, Pallas kernels, per_device(): call(functools.partial(rest_body, bin_count, last), [struct(3 * extent_x...  19.6 us
    pallas_call x4, Pallas kernels, per_device(): call(functools.partial(near_body, bin_count), [struct(blocks, 4, 8, SEG)]...  15 us
    pallas_call x4, Pallas kernels, per_device(): call(functools.partial(update_body, first, last), update_outs, [pltpu.VME...  10.4 us
    pallas_call x4, Pallas kernels, per_device(): call(inner_body, [struct(*shape)], [pltpu.VMEM((extent_x, 9, extent_y, ex...  8.68 us
    ppermute x12, starting transfers between devices, cycled(): lax.ppermute(value, axis, [(source, (source + steps) % count) for source...  7.93 us
    pallas_call x1, Pallas kernels, per_device(): pl.pallas_call(first_body, grid=(1,), out_shape=first_outs, in_specs=firs...  3.2 us
    pallas_call x4, Pallas kernels, per_device(): pl.pallas_call(functools.partial(layer_body, first), grid=(1,), out_shape...  2.91 us
  transfers between devices with their start and end apart: 22, of which 5 were waited for; matrix products, arithmetic and copies ran while one was open for 0% of the time, Pallas kernels for 43%

commit v1 on v0

--- a/solution.py
+++ b/solution.py
@@ -20,10 +20,13 @@
 NT = (((1,), (1,)), ((), ()))
 
 
-def shifted(value, axis, steps):
+def swapped(value, axis, odd):
     count = lax.axis_size(axis)
-    first, last = (max(0, -steps), min(count, count - steps))
-    return lax.ppermute(value, axis, [(source, source + steps) for source in range(first, last)])
+    first = 1 if odd else 0
+    partner = list(range(count))
+    for i in range(first, count - 1, 2):
+        partner[i], partner[i + 1] = i + 1, i
+    return lax.ppermute(value, axis, list(enumerate(partner)))
 
 
 def cycled(value, axis, steps):
@@ -99,40 +102,47 @@
     store_messages(disp_ref, base_ref, node_ref, hot_ref[...], up_ref, down_ref, far_ref)
     rows = 3 * extent_x
     store_column(moduli_ref, moduli_ref.shape[2] - 1, up_ref, rows)
-    bins = bins_ref[...]
+    steps, blocks = bins_ref.shape
+    bins = bins_ref[...].astype(F32)
     zeros = jnp.zeros((8, SEG), F32)
-    up_ref[rows : rows + 8, extent_z:] = bins
     up_ref[rows + 8 : rows + 16, extent_z:] = zeros
     down_ref[rows : rows + 8, 0:extent_z] = jnp.zeros((8, extent_z), F32)
-    down_ref[rows : rows + 8, extent_z:] = bins
-    far_ref[rows : rows + 8, :] = bins
+    for ref, lane in ((up_ref, extent_z), (down_ref, extent_z), (far_ref, 0)):
+        ref[rows : rows + 8, lane : lane + SEG] = zeros
+        ref[rows : rows + steps, lane : lane + blocks] = bins
 
 
 def layer_body(with_moduli, *refs):
     flag_ref, first_ref, last_ref, lower_ref, upper_ref = refs[:5]
     if with_moduli:
-        moduli_ref, up_ref, down_ref = refs[7:]
+        moduli_ref, even_ref, odd_ref = refs[7:]
     else:
-        up_ref, down_ref = refs[7:]
+        even_ref, odd_ref = refs[7:]
     extent_y, extent_z = first_ref.shape[2:]
     main = 3 * extent_y
     extent_x = lower_ref.shape[0] // (5 if with_moduli else 3)
-    has_lower, has_upper = flag_ref[0], flag_ref[1]
-    for x, source_ref, target_ref in ((0, first_ref, down_ref), (extent_x - 1, last_ref, up_ref)):
-        for p in range(3):
-            target_ref[p * extent_y : (p + 1) * extent_y, :] = source_ref[p, 0]
+    has_lower, has_upper, is_odd = flag_ref[0], flag_ref[1], flag_ref[4] > 0.5
+    for p in range(3):
+        low, high = first_ref[p, 0], last_ref[p, 0]
+        even_ref[p * extent_y : (p + 1) * extent_y, :] = jnp.where(is_odd, low, high)
+        odd_ref[p * extent_y : (p + 1) * extent_y, :] = jnp.where(is_odd, high, low)
+    edges = []
+    for x in (0, extent_x - 1):
         at = [p * extent_x + x for p in range(3)]
         above = [upper_ref[i : i + 1, 0:extent_z] * has_upper for i in at]
         below = [lower_ref[i : i + 1, 0:extent_z] * has_lower for i in at]
-        if with_moduli and x > 0:
+        if with_moduli:
             at = [(3 + m) * extent_x + x for m in range(2)]
             rest = [lower_ref[i : i + 1, 0:extent_z] * has_lower for i in at]
         else:
             rest = [jnp.zeros((2, extent_z), F32)]
-        target_ref[main : main + 8, :] = jnp.concatenate(above + below + rest, axis=0)
+        edges.append(jnp.concatenate(above + below + rest, axis=0))
+    even_ref[main : main + 8, :] = jnp.where(is_odd, edges[0], edges[1])
+    odd_ref[main : main + 8, :] = jnp.where(is_odd, edges[1], edges[0])
     if with_moduli:
         for m in range(2):
-            up_ref[main + 8 + m * extent_y : main + 8 + (m + 1) * extent_y, :] = moduli_ref[m, 0]
+            for target_ref in (even_ref, odd_ref):
+                target_ref[main + 8 + m * extent_y : main + 8 + (m + 1) * extent_y, :] = moduli_ref[m, 0]
 
 
 def pair_sums(bins_ref, own_ref, sources, begin, bin_count, sums_of, store, spread, listed):
@@ -197,7 +207,7 @@
 def rest_body(bin_count, last, *refs):
     bins_ref, own_ref, upper_ref, far_ref, sums_ref, node_ref, hot_ref, heat_ref = refs[:8]
     if last:
-        tile_ref, contact_ref, partial_ref, spread, listed, push = refs[8:]
+        tile_ref, flag_ref, contact_ref, partial_ref, spread, listed, push = refs[8:]
     else:
         contact_ref, total_ref, spread, listed, push = refs[8:]
     extent_z = contact_ref.shape[1]
@@ -232,9 +242,11 @@
     placed = jnp.where(at_side, flat, 0.0)
     high, low = split_two(placed)
     lowest = (placed - high.astype(F32) - low.astype(F32)).astype(BF16)
-    partial_ref[...] = sum(
-        lax.dot_general(piece, hot_slot, NT, preferred_element_type=F32) for piece in (high, low, lowest)
-    )
+    made = sum(lax.dot_general(piece, hot_slot, NT, preferred_element_type=F32) for piece in (high, low, lowest))
+    is_odd = flag_ref[4] > 0.5
+    to_even = jnp.where(is_odd, made[0:1], made[2:3])
+    to_odd = jnp.where(is_odd, made[2:3], made[0:1])
+    partial_ref[...] = jnp.concatenate([to_even, made[1:2], to_odd, made[3:]], axis=0)
 
 
 def turn_body(extent_z, node_ref, out_ref):
@@ -350,7 +362,7 @@
     refs = list(refs)
     take = lambda count: [refs.pop(0) for _ in range(count)]
     flag_ref, disp_ref, vel_ref, mass_ref, inner_ref, contact_ref = take(6)
-    own_up_ref, own_down_ref, lower_ref, upper_ref, back_ref, front_ref, rim_ref = take(7)
+    own_up_ref, own_down_ref, lower_ref, upper_ref, even_ref, odd_ref, rim_ref = take(7)
     if not last:
         base_ref, node_ref, hot_ref = take(3)
     new_disp_ref, new_vel_ref = take(2)
@@ -360,10 +372,19 @@
         moduli_ref, rim_ref = rim_ref, take(1)[0]
     (side_low, side_high, face_low, face_high) = take(4)
     _, extent_x, extent_y, extent_z = disp_ref.shape
-    has_lower, has_upper = flag_ref[0], flag_ref[1]
+    has_lower, has_upper, has_back, has_front = [flag_ref[i] for i in range(4)]
+    is_odd = flag_ref[4] > 0.5
     place = lax.broadcasted_iota(jnp.int32, (8, extent_z), 0)
     all_but_last = lax.broadcasted_iota(jnp.int32, (extent_y, extent_z), 0) < extent_y - 1
     main = 3 * extent_y
+
+    def back(begin, count):
+        rows = slice(begin, begin + count)
+        return jnp.where(is_odd, even_ref[rows, :], odd_ref[rows, :]) * has_back
+
+    def front(begin, count):
+        rows = slice(begin, begin + count)
+        return jnp.where(is_odd, odd_ref[rows, :], even_ref[rows, :]) * has_front
 
     def ring(tile, above, below):
         return jnp.concatenate([tile, jnp.where(place == 0, above, jnp.where(place == 7, below, 0.0))], axis=0)
@@ -372,9 +393,9 @@
         for m in range(2):
             at = slice((3 + m) * extent_x, (4 + m) * extent_x)
             begin = main + 8 + m * extent_y
-            of_back = back_ref[begin : begin + extent_y, :]
+            of_back = back(begin, extent_y)
             high = ring(own_up_ref[at, 0:extent_z], 0.0, of_back[extent_y - 1 :])
-            low = ring(lower_ref[at, 0:extent_z] * has_lower, 0.0, back_ref[main + 6 + m : main + 7 + m, :])
+            low = ring(lower_ref[at, 0:extent_z] * has_lower, 0.0, back(main + 6 + m, 1))
             rim_ref[m] = high * SCALE
             rim_ref[2 + m] = low * SCALE
             rim_ref[4 + m] = jnp.where(all_but_last, of_back * SCALE, 0.0)
@@ -386,7 +407,7 @@
             at = main + extra + p if row is None else p * extent_y + row
             tile = tile_ref[p * extent_x : (p + 1) * extent_x, 0:extent_z]
             tile = tile if weight is None else tile * weight
-            made.append(ring(tile, front_ref[at : at + 1, :], back_ref[at : at + 1, :]))
+            made.append(ring(tile, front(at, 1), back(at, 1)))
         return made
 
     def side(near, far, at, sign, target):
@@ -418,10 +439,10 @@
             plain = (of_x - of_y) + behind_row(of_x + of_y)
             target[p] = spread_z(plain, of_z + behind_row(of_z))
 
-    layer_of = lambda ref: [ref[p * extent_y : (p + 1) * extent_y, :] for p in range(3)]
+    layer_of = lambda side_of: [side_of(p * extent_y, extent_y) for p in range(3)]
     own_layer = lambda x: [disp_ref[p, x] for p in range(3)]
-    face(layer_of(back_ref), own_layer(0), 4, 1.0, face_low)
-    face(own_layer(extent_x - 1), layer_of(front_ref), 6, -1.0, face_high)
+    face(layer_of(back), own_layer(0), 4, 1.0, face_low)
+    face(own_layer(extent_x - 1), layer_of(front), 6, -1.0, face_high)
 
     for x in range(extent_x):
         step_mass = TIME_STEP / mass_ref[x]
@@ -450,11 +471,12 @@
     blocks = segments // SEG
     bin_count = lax.axis_size("bin")
     bin_at = lax.axis_index("bin")
-    own_device = lax.axis_index("dom") * bin_count + bin_at
-    flags = jnp.stack([bin_at > 0, bin_at < bin_count - 1]).astype(F32)
+    dom_at, dom_count = lax.axis_index("dom"), lax.axis_size("dom")
+    own_device = dom_at * bin_count + bin_at
+    checks = (bin_at > 0, bin_at < bin_count - 1, dom_at > 0, dom_at < dom_count - 1, dom_at % 2 == 1)
+    flags = jnp.stack(checks).astype(F32)
     node = segment_node.reshape(blocks, SEG)
-    bins = contact_bin[:, :, 0].astype(F32)
-    bins = jnp.pad(bins, ((0, 8 - steps), (0, SEG - blocks)))
+    bins = contact_bin[:, :, 0]
     rows = 3 * extent_x
     wide = extent_z + SEG
     struct = lambda *dims: jax.ShapeDtypeStruct(dims, F32)
@@ -501,28 +523,28 @@
             [WHOLE] * 2,
         )(displacement, moduli)
         if first:
-            of_bins = [bins[:steps, :blocks]]
+            of_bins = [bins.astype(F32)]
             of_bins += [v[rows : rows + steps, extent_z : extent_z + blocks] for v in (lower, upper)]
             of_bins += [v[rows : rows + steps, :blocks] for v in others]
             all_bins = jnp.concatenate(of_bins, axis=1).astype(jnp.int32)
         layer = lambda at, count=3: pl.BlockSpec((count, 1, extent_y, extent_z), lambda i: (0, at, 0, 0))
-        up_rows = layer_rows + (2 * extent_y if first else 0)
+        send_rows = layer_rows + (2 * extent_y if first else 0)
         layer_args = [flags, displacement, displacement, lower, upper, inner, others]
         layer_specs = [SCALARS, layer(0), layer(extent_x - 1), full(*lower.shape), full(*upper.shape)]
         layer_specs += [pl.BlockSpec(memory_space=pl.ANY)] * 2
         if first:
             layer_args.append(moduli)
             layer_specs.append(layer(extent_x - 1, 2))
-        to_front, to_back = pl.pallas_call(
+        to_even, to_odd = pl.pallas_call(
             functools.partial(layer_body, first),
             grid=(1,),
-            out_shape=[struct(up_rows, extent_z), struct(layer_rows, extent_z)],
+            out_shape=[struct(send_rows, extent_z)] * 2,
             in_specs=layer_specs,
-            out_specs=[full(up_rows, extent_z), full(layer_rows, extent_z)],
+            out_specs=[full(send_rows, extent_z)] * 2,
             compiler_params=pltpu.CompilerParams(vmem_limit_bytes=VMEM_BYTES),
             cost_estimate=pl.CostEstimate(flops=1_000, bytes_accessed=1_000, transcendentals=0),
         )(*layer_args)
-        back = shifted(to_front, "dom", 1)
+        of_even = swapped(to_even, "dom", False)
         near_blocks = 2 * blocks
         far_blocks = blocks * (bin_count - 2)
         pair_scratch = lambda count: [
@@ -534,21 +556,22 @@
             [struct(blocks, 4, 8, SEG)],
             pair_scratch(near_blocks),
             [SCALARS, WHOLE, WHOLE, pl.BlockSpec(memory_space=pl.ANY)],
-        )(all_bins[step], far, lower, to_front)
-        to_back, sums, back = lax.optimization_barrier((to_back, sums, back))
-        front = shifted(to_back, "dom", -1)
+        )(all_bins[step], far, lower, to_even)
+        to_odd, sums, of_even = lax.optimization_barrier((to_odd, sums, of_even))
+        of_odd = swapped(to_odd, "dom", True)
         pair_args = [all_bins[step], far, upper, others, sums, node, turned, heat]
         if last:
-            pair_args.append(tile_places)
+            pair_args += [tile_places, flags]
         contact, heat = call(
             functools.partial(rest_body, bin_count, last),
             [struct(3 * extent_x * extent_y, extent_z), struct(8, TILE_DEV) if last else struct(blocks, SEG)],
             pair_scratch(far_blocks) + [pltpu.VMEM((8, segments), F32)],
-            [SCALARS] + [WHOLE] * (len(pair_args) - 1),
+            [SCALARS] + [WHOLE] * (len(pair_args) - 2) + [SCALARS if last else WHOLE],
         )(*pair_args)
         if last:
-            heat, back, front = lax.optimization_barrier((heat, back, front))
-        update_args = [flags, displacement, velocity, nodal_mass, inner, contact, up, down, lower, upper, back, front, rim]
+            heat, of_even, of_odd = lax.optimization_barrier((heat, of_even, of_odd))
+        update_args = [flags, displacement, velocity, nodal_mass, inner, contact, up, down, lower, upper]
+        update_args += [of_even, of_odd, rim]
         update_outs = [struct(*shape), struct(*shape)]
         if not last:
             update_args += [segment_base, node, hot]
@@ -566,7 +589,11 @@
             up, down, far = made[2:5]
         if first:
             rim = made[-1]
-    tile_heat = heat[1] + shifted(heat[0], "dom", -1) + shifted(heat[2], "dom", 1)
+    odd_weight = jnp.where(dom_at % 2 == 1, flags[3], flags[2])
+    from_even, from_odd = swapped(heat[0], "dom", False), swapped(heat[2], "dom", True)
+    if dom_count % 2:
+        from_even = from_even * flags[3]
+    tile_heat = heat[1] + from_even + from_odd * odd_weight
     return displacement, velocity, tile_heat
 
 

time: 110 us -> 108 us (0.982)
  the two profiles are of different devices: /device:TPU:18 before, /device:TPU:0 now
where the time goes in v1:
time: 108 us; the launch traced here: 107 us
  Pallas kernels  60.7 us (56%)
  starting transfers between devices  30.8 us (29%)
  local copies, waits for them, and re-layouts  8.54 us (8%)
  waiting for transfers between devices  3.13 us (3%)
  between operations  2.66 us (2%)
    ppermute x10, starting transfers between devices, swapped(): return lax.ppermute(value, axis, list(enumerate(partner)))  22.4 us
    pallas_call x4, Pallas kernels, per_device(): call(functools.partial(rest_body, bin_count, last), [struct(3 * extent_x...  19.2 us
    pallas_call x4, Pallas kernels, per_device(): call(functools.partial(near_body, bin_count), [struct(blocks, 4, 8, SEG)]...  15.4 us
    pallas_call x4, Pallas kernels, per_device(): call(functools.partial(update_body, first, last), update_outs, [pltpu.VME...  10.4 us
    pallas_call x4, Pallas kernels, per_device(): call(inner_body, [struct(*shape)], [pltpu.VMEM((extent_x, 9, extent_y, ex...  8.68 us
    ppermute x12, starting transfers between devices, cycled(): lax.ppermute(value, axis, [(source, (source + steps) % count) for source...  8.46 us
    unnamed x74, local copies, waits for them, and re-layouts  7.75 us
    pallas_call x1, Pallas kernels, per_device(): pl.pallas_call(first_body, grid=(1,), out_shape=first_outs, in_specs=firs...  3.25 us
  transfers between devices with their start and end apart: 22, of which 4 were waited for; matrix products, arithmetic and copies ran while one was open for 1% of the time, Pallas kernels for 44%

profile of v1, /device:TPU:0, one launch (start us, length us, event | category | flops | bytes accessed | tf_op | source)
XLA Modules:
  0.0 106.5 jit_solution(11294011818358148198)
XLA Ops:
  0.6 3.3 %shard_map.104 = (f32[40,640]{1,0:T(8,128)}, f32[32,640]{1,0:T(8,128)}, f32[32,128]{1,0:T(8,128)}, bf16[512,1024]{1,0:T(8,128)(2,1)}) custom-call(f32[3,8,16,512]{3,2,1,0:T(8,128)} %refs_1_.3, f32[3,1024]{1,0:T(4,128)} %refs_13_.5, s32[8,128]{1,0:T(8,128)} %bitcast.25, f32[2,8,16,512]{3,2,1,0:T(8,128)} %moduli_ref.9, s32[4,8]{1,0:T(4,128)} %bitcast.43), custom_call_target="tpu_custom_call" | custom-call | flops 1000 | bytes 1000 | tf_op jit(solution)/shard_map/pallas_call | solution.py:495
  4.4 2.0 %collective-permute-start.1 = (f32[32,640]{1,0:T(8,128)}, f32[32,640]{1,0:T(8,128)S(1)}, u32[]{:S(2)}, u32[]{:S(2)}) collective-permute-start(f32[32,640]{1,0:T(8,128)} %get-tuple-element.57.refs_7_), channel_id=1, source_target_pairs={{0,3},{1,0},{2,1},{3,2},{4,7},{5,4},{6,5},{7,6},{8,11},{9,8},{10,9... | collective-permute-start | bytes 245768 | tf_op jit(solution)/shard_map/ppermute | solution.py:34
  6.4 2.3 %collective-permute-start.2 = (f32[32,128]{1,0:T(8,128)}, f32[32,128]{1,0:T(8,128)S(1)}, u32[]{:S(2)}, u32[]{:S(2)}) collective-permute-start(f32[32,128]{1,0:T(8,128)} %get-tuple-element.58.own_ref.refs_1_), channel_id=1, source_target_pairs={{0,2},{1,3},{2,0},{3,1},{4,6},{5,7},{6,4},{7,5},{8,10},{9,11},{10,... | collective-permute-start | bytes 49160 | tf_op jit(solution)/shard_map/ppermute | solution.py:34
  8.6 2.2 %shard_map.103.refs_5_.refs_4_ = f32[3,8,16,512]{3,2,1,0:T(8,128)S(1)} custom-call(f32[3,8,16,512]{3,2,1,0:T(8,128)S(1)} %copy-done.1, f32[2,8,16,512]{3,2,1,0:T(8,128)S(1)} %copy-done), custom_call_target="tpu_custom_call" | custom-call | flops 1000 | bytes 1000 | tf_op jit(solution)/shard_map/pallas_call | solution.py:519
  10.8 0.7 copy-done.36
  11.7 0.6 shard_map.105
  12.3 1.6 %collective-permute-start.3 = (f32[88,512]{1,0:T(8,128)S(1)}, f32[88,512]{1,0:T(8,128)S(1)}, u32[]{:S(2)}, u32[]{:S(2)}) collective-permute-start(f32[88,512]{1,0:T(8,128)S(1)} %get-tuple-element.60._), channel_id=1, source_target_pairs={{0,4},{4,0},{8,12},{12,8},{16,20},{20,16},{24,28},{28,24},{1,5},{5... | collective-permute-start | bytes 540680 | tf_op jit(solution)/shard_map/ppermute | solution.py:29
  14.0 3.6 %shard_map.106.refs_4_ = f32[8,4,8,128]{3,2,1,0:T(8,128)S(1)} custom-call(s32[32]{0:T(128)S(1)} %get-tuple-element.115.bins_ref.refs_0_, f32[32,128]{1,0:T(8,128)S(1)} %copy-done.27, f32[40,640]{1,0:T(8,128)S(1)} %collective-permute-done.refs_3_.lower_ref.refs_8_, f32[88,512]{1,0:T(8,128)S(1)} %get-tuple-element.60._), custom_call_target="tpu_custom_call" | custom-call | flops 1000 | bytes 1000 | tf_op jit(solution)/shard_map/pallas_call | solution.py:554
  17.6 0.6 collective-permute-done.3.refs_10_
  18.2 0.8 collective-permute-start.4
  19.4 4.6 %shard_map.108 = (f32[384,512]{1,0:T(8,128)S(1)}, f32[8,128]{1,0:T(8,128)S(1)}) custom-call(s32[32]{0:T(128)S(1)} %get-tuple-element.115.bins_ref.refs_0_, f32[32,128]{1,0:T(8,128)S(1)} %copy-done.27, f32[32,640]{1,0:T(8,128)S(1)} %copy-done.17, f32[1,32,128]{2,1,0:T(8,128)S(1)} %bitcast.36, f32[8,4,8,128]{3,2,1,0:T(8,128)S(1)} %shard_map.106.refs_4_, ...), custom_call_target="tpu_custom_call" | custom-call | flops 1000 | bytes 1000 | tf_op jit(solution)/shard_map/pallas_call | solution.py:565
  24.1 2.5 %shard_map.109 = (f32[3,8,16,512]{3,2,1,0:T(8,128)S(1)}, f32[3,8,16,512]{3,2,1,0:T(8,128)S(1)}, f32[24,640]{1,0:T(8,128)S(1)}, f32[24,640]{1,0:T(8,128)S(1)}, f3...) custom-call(f32[5]{0:T(128)S(1)} %convert_element_type.9.refs_0_.refs_9_, f32[3,8,16,512]{3,2,1,0:T(8,128)S(1)} %copy-done.1, ...), custom_call_target="tpu_custom_call" | custom-call | flops 1000 | bytes 1000 | tf_op jit(solution)/shard_map/pallas_call | solution.py:581
  27.1 1.1 %collective-permute-start.6 = (f32[24,128]{1,0:T(8,128)S(1)}, f32[24,128]{1,0:T(8,128)S(1)}, u32[]{:S(2)}, u32[]{:S(2)}) collective-permute-start(f32[24,128]{1,0:T(8,128)S(1)} %get-tuple-element.68.own_ref.refs_1_), channel_id=1, source_target_pairs={{0,2},{1,3},{2,0},{3,1},{4,6},{5,7},{6,4},{7,5},{8,10},{9,11},{10,... | collective-permute-start | bytes 36872 | tf_op jit(solution)/shard_map/ppermute | solution.py:34
  28.2 2.2 %shard_map.110.refs_5_.refs_4_ = f32[3,8,16,512]{3,2,1,0:T(8,128)S(1)} custom-call(f32[3,8,16,512]{3,2,1,0:T(8,128)S(1)} %get-tuple-element.66.disp_ref.refs_1_.refs_2_, f32[2,8,16,512]{3,2,1,0:T(8,128)S(1)} %copy-done), custom_call_target="tpu_custom_call" | custom-call | flops 1000 | bytes 1000 | tf_op jit(solution)/shard_map/pallas_call | solution.py:519
  30.9 0.6 shard_map.111
  31.4 4.6 %collective-permute-start.8 = (f32[56,512]{1,0:T(8,128)S(1)}, f32[56,512]{1,0:T(8,128)S(1)}, u32[]{:S(2)}, u32[]{:S(2)}) collective-permute-start(f32[56,512]{1,0:T(8,128)S(1)} %get-tuple-element.72._), channel_id=1, source_target_pairs={{0,4},{4,0},{8,12},{12,8},{16,20},{20,16},{24,28},{28,24},{1,5},{5... | collective-permute-start | bytes 344072 | tf_op jit(solution)/shard_map/ppermute | solution.py:29
  36.1 4.1 %shard_map.112.refs_4_ = f32[8,4,8,128]{3,2,1,0:T(8,128)S(1)} custom-call(s32[32]{0:T(128)S(1)} %get-tuple-element.114.bins_ref.refs_0_, f32[24,128]{1,0:T(8,128)S(1)} %get-tuple-element.68.own_ref.refs_1_, f32[24,640]{1,0:T(8,128)S(1)} %collective-permute-done.7.refs_3_.lower_ref.refs_8_, f32[56,512]{1,0:T(8,128)S(1)} %get-tuple-element.72._), custom_call_target="tpu_custom_call" | custom-call | flops 1000 | bytes 1000 | tf_op jit(solution)/shard_map/pallas_call | solution.py:554
  40.2 0.8 collective-permute-start.9
  41.1 4.7 %shard_map.113 = (f32[384,512]{1,0:T(8,128)S(1)}, f32[8,128]{1,0:T(8,128)S(1)}) custom-call(s32[32]{0:T(128)S(1)} %get-tuple-element.114.bins_ref.refs_0_, f32[24,128]{1,0:T(8,128)S(1)} %get-tuple-element.68.own_ref.refs_1_, f32[24,640]{1,0:T(8,128)S(1)} %collective-permute-done.5.refs_4_.refs_2_.refs_9_, f32[1,24,128]{2,1,0:T(8,128)S(1)} %bitcast.40, ...), custom_call_target="tpu_custom_call" | custom-call | flops 1000 | bytes 1000 | tf_op jit(solution)/shard_map/pallas_call | solution.py:565
  45.8 2.4 %shard_map.114 = (f32[3,8,16,512]{3,2,1,0:T(8,128)S(1)}, f32[3,8,16,512]{3,2,1,0:T(8,128)S(1)}, f32[24,640]{1,0:T(8,128)S(1)}, f32[24,640]{1,0:T(8,128)S(1)}, f32[24,128]{1,0:T(8,128)S(1)}) custom-call(f32[5]{0:T(128)S(1)} %convert_element_type.9.refs_0_.refs_9_, f32[3,8,16,512]{3,2,1,0:T(8,128)S(1)} %get-tuple-element.66.disp_ref.refs_1_.refs_2_, ...), custom_call_target="tpu_custom_call" | custom-call | flops 1000 | bytes 1000 | tf_op jit(solution)/shard_map/pallas_call | solution.py:581
  49.3 2.2 %shard_map.115.refs_5_.refs_4_ = f32[3,8,16,512]{3,2,1,0:T(8,128)S(1)} custom-call(f32[3,8,16,512]{3,2,1,0:T(8,128)S(1)} %get-tuple-element.79.disp_ref.refs_1_.refs_2_, f32[2,8,16,512]{3,2,1,0:T(8,128)S(1)} %copy-done), custom_call_target="tpu_custom_call" | custom-call | flops 1000 | bytes 1000 | tf_op jit(solution)/shard_map/pallas_call | solution.py:519
  51.4 1.0 collective-permute-done.11
  52.5 0.6 shard_map.116
  53.0 4.7 %collective-permute-start.13 = (f32[56,512]{1,0:T(8,128)S(1)}, f32[56,512]{1,0:T(8,128)S(1)}, u32[]{:S(2)}, u32[]{:S(2)}) collective-permute-start(f32[56,512]{1,0:T(8,128)S(1)} %get-tuple-element.85._), channel_id=1, source_target_pairs={{0,4},{4,0},{8,12},{12,8},{16,20},{20,16},{24,28},{28,24},{1,5},{5... | collective-permute-start | bytes 344072 | tf_op jit(solution)/shard_map/ppermute | solution.py:29
  57.7 4.1 %shard_map.117.refs_4_ = f32[8,4,8,128]{3,2,1,0:T(8,128)S(1)} custom-call(s32[32]{0:T(128)S(1)} %get-tuple-element.113.bins_ref.refs_0_, f32[24,128]{1,0:T(8,128)S(1)} %get-tuple-element.81.own_ref.refs_1_, f32[24,640]{1,0:T(8,128)S(1)} %collective-permute-done.12.refs_3_.lower_ref.refs_8_, f32[56,512]{1,0:T(8,128)S(1)} %get-tuple-element.85._), custom_call_target="tpu_custom_call" | custom-call | flops 1000 | bytes 1000 | tf_op jit(solution)/shard_map/pallas_call | solution.py:554
  61.9 0.7 collective-permute-start.14
  62.6 4.7 %shard_map.118 = (f32[384,512]{1,0:T(8,128)S(1)}, f32[8,128]{1,0:T(8,128)S(1)}) custom-call(s32[32]{0:T(128)S(1)} %get-tuple-element.113.bins_ref.refs_0_, f32[24,128]{1,0:T(8,128)S(1)} %get-tuple-element.81.own_ref.refs_1_, f32[24,640]{1,0:T(8,128)S(1)} %collective-permute-done.10.refs_4_.refs_2_.refs_9_, f32[1,24,128]{2,1,0:T(8,128)S(1)} %bitcast.42, ...), custom_call_target="tpu_custom_call" | custom-call | flops 1000 | bytes 1000 | tf_op jit(solution)/shard_map/pallas_call | solution.py:565
  67.3 2.4 %shard_map.119 = (f32[3,8,16,512]{3,2,1,0:T(8,128)S(1)}, f32[3,8,16,512]{3,2,1,0:T(8,128)S(1)}, f32[24,640]{1,0:T(8,128)S(1)}, f32[24,640]{1,0:T(8,128)S(1)}, f32[24,128]{1,0:T(8,128)S(1)}) custom-call(f32[5]{0:T(128)S(1)} %convert_element_type.9.refs_0_.refs_9_, f32[3,8,16,512]{3,2,1,0:T(8,128)S(1)} %get-tuple-element.79.disp_ref.refs_1_.refs_2_, ...), custom_call_target="tpu_custom_call" | custom-call | flops 1000 | bytes 1000 | tf_op jit(solution)/shard_map/pallas_call | solution.py:581
  70.8 2.2 %shard_map.120.refs_5_.refs_4_ = f32[3,8,16,512]{3,2,1,0:T(8,128)S(1)} custom-call(f32[3,8,16,512]{3,2,1,0:T(8,128)S(1)} %get-tuple-element.91.disp_ref.refs_1_.refs_2_, f32[2,8,16,512]{3,2,1,0:T(8,128)S(1)} %copy-done), custom_call_target="tpu_custom_call" | custom-call | flops 1000 | bytes 1000 | tf_op jit(solution)/shard_map/pallas_call | solution.py:519
  73.0 1.0 collective-permute-done.16
  74.0 1.2 %shard_map.121 = (f32[56,512]{1,0:T(8,128)S(1)}, f32[56,512]{1,0:T(8,128)}) custom-call(f32[5]{0:T(128)S(1)} %convert_element_type.9.refs_0_.refs_9_, f32[3,8,16,512]{3,2,1,0:T(8,128)S(1)} %get-tuple-element.91.disp_ref.refs_1_.refs_2_, f32[3,8,16,512]{3,2,1,0:T(8,128)S(1)} %get-tuple-element.91.disp_ref.refs_1_.refs_2_, ...), custom_call_target="tpu_custom_call" | custom-call | flops 1000 | bytes 1000 | tf_op jit(solution)/shard_map/pallas_call | solution.py:538
  75.3 3.3 %collective-permute-start.18 = (f32[56,512]{1,0:T(8,128)S(1)}, f32[56,512]{1,0:T(8,128)S(1)}, u32[]{:S(2)}, u32[]{:S(2)}) collective-permute-start(f32[56,512]{1,0:T(8,128)S(1)} %get-tuple-element.97._), channel_id=1, source_target_pairs={{0,4},{4,0},{8,12},{12,8},{16,20},{20,16},{24,28},{28,24},{1,5},{5... | collective-permute-start | bytes 344072 | tf_op jit(solution)/shard_map/ppermute | solution.py:29
  78.6 3.6 %shard_map.122.refs_4_ = f32[8,4,8,128]{3,2,1,0:T(8,128)S(1)} custom-call(s32[32]{0:T(128)S(1)} %get-tuple-element.112.bins_ref.refs_0_, f32[24,128]{1,0:T(8,128)S(1)} %get-tuple-element.93.own_ref.refs_1_, f32[24,640]{1,0:T(8,128)S(1)} %collective-permute-done.17.refs_3_.lower_ref.refs_8_, f32[56,512]{1,0:T(8,128)S(1)} %get-tuple-element.97._), custom_call_target="tpu_custom_call" | custom-call | flops 1000 | bytes 1000 | tf_op jit(solution)/shard_map/pallas_call | solution.py:554
  82.2 2.2 %collective-permute-start.19 = (f32[56,512]{1,0:T(8,128)}, f32[56,512]{1,0:T(8,128)}, u32[]{:S(2)}, u32[]{:S(2)}) collective-permute-start(f32[56,512]{1,0:T(8,128)} %get-tuple-element.103), channel_id=1, source_target_pairs={{0,0},{4,8},{8,4},{12,16},{16,12},{20,24},{24,20},{28,28},{1,1},{5... | collective-permute-start | bytes 344072 | tf_op jit(solution)/shard_map/ppermute | solution.py:29
  84.4 0.5 shard_map.123.refs_8_
  85.1 1.0 copy-done.19
  86.0 5.3 %shard_map.124 = (f32[384,512]{1,0:T(8,128)S(1)}, f32[8,256]{1,0:T(8,128)S(1)}) custom-call(s32[32]{0:T(128)S(1)} %get-tuple-element.112.bins_ref.refs_0_, f32[24,128]{1,0:T(8,128)S(1)} %copy-done.33, f32[24,640]{1,0:T(8,128)S(1)} %collective-permute-done.15.refs_4_.refs_2_.refs_9_, f32[1,24,128]{2,1,0:T(8,128)S(1)} %bitcast.38, ...), custom_call_target="tpu_custom_call" | custom-call | flops 1000 | bytes 1000 | tf_op jit(solution)/shard_map/pallas_call | solution.py:565
  91.3 0.9 copy-done.14
  92.3 3.1 %collective-permute-start.20 = (f32[256]{0:T(256)S(1)}, f32[256]{0:T(256)S(1)}, u32[]{:S(2)}, u32[]{:S(2)}) collective-permute-start(f32[256]{0:T(256)S(1)} %bitcast.47), channel_id=1, source_target_pairs={{0,4},{4,0},{8,12},{12,8},{16,20},{20,16},{24,28},{28,24},{1,5},{5... | collective-permute-start | bytes 3080 | tf_op jit(solution)/shard_map/ppermute | solution.py:29
  95.4 0.6 collective-permute-start.21
  96.0 0.7 fusion.1
  98.1 1.1 %copy-done.13 = f32[3,8,16,512]{3,2,1,0:T(8,128)S(1)} copy-done((f32[3,8,16,512]{3,2,1,0:T(8,128)S(1)}, f32[3,8,16,512]{3,2,1,0:T(8,128)}, u32[]{:S(2)}) %copy-start.13) | copy-done | bytes 786456
  99.2 1.1 %copy-done.15 = f32[384,512]{1,0:T(8,128)S(1)} copy-done((f32[384,512]{1,0:T(8,128)S(1)}, f32[384,512]{1,0:T(8,128)}, u32[]{:S(2)}) %copy-start.15) | copy-done | bytes 786456
  100.3 0.9 copy-done.24
  101.2 0.8 copy-done.29
  102.1 0.8 copy-done.31
  102.9 3.1 %shard_map.125 = (f32[3,8,16,512]{3,2,1,0:T(8,128)}, f32[3,8,16,512]{3,2,1,0:T(8,128)}) custom-call(f32[5]{0:T(128)S(1)} %convert_element_type.9.refs_0_.refs_9_, f32[3,8,16,512]{3,2,1,0:T(8,128)S(1)} %get-tuple-element.91.disp_ref.refs_1_.refs_2_, f32[3,8,16,512]{3,2,1,0:T(8,128)S(1)} %copy-done.13, f32[8,16,512]{2,1,0:T(8,128)S(1)} %copy-done.8, ...), custom_call_target="tpu_custom_call" | custom-call | flops 1000 | bytes 1000 | tf_op jit(solution)/shard_map/pallas_call | solution.py:581
  106.0 0.6 multiply_add_fusion
  (105 shorter events, 4.4 us)
Async XLA Ops:
  0.6 8.0 %copy-start.1 = (f32[3,8,16,512]{3,2,1,0:T(8,128)S(1)}, f32[3,8,16,512]{3,2,1,0:T(8,128)}, u32[]{:S(2)}) copy-start(f32[3,8,16,512]{3,2,1,0:T(8,128)} %refs_1_.3) | copy-start | bytes 2359300
  0.6 8.0 %copy-start = (f32[2,8,16,512]{3,2,1,0:T(8,128)S(1)}, f32[2,8,16,512]{3,2,1,0:T(8,128)}, u32[]{:S(2)}) copy-start(f32[2,8,16,512]{3,2,1,0:T(8,128)} %moduli_ref.9) | copy-start | bytes 1572868
  3.9 7.8 %collective-permute-start = (f32[40,640]{1,0:T(8,128)}, f32[40,640]{1,0:T(8,128)S(1)}, u32[]{:S(2)}, u32[]{:S(2)}) collective-permute-start(f32[40,640]{1,0:T(8,128)} %get-tuple-element.56.refs_6_), channel_id=1, source_target_pairs={{0,1},{1,2},{2,3},{3,0},{4,5},{5,6},{6,7},{7,4},{8,9},{9,10},{10,1... | collective-permute-start | bytes 307208 | tf_op jit(solution)/shard_map/ppermute | solution.py:34
  4.4 7.3 %collective-permute-start.1 = (f32[32,640]{1,0:T(8,128)}, f32[32,640]{1,0:T(8,128)S(1)}, u32[]{:S(2)}, u32[]{:S(2)}) collective-permute-start(f32[32,640]{1,0:T(8,128)} %get-tuple-element.57.refs_7_), channel_id=1, source_target_pairs={{0,3},{1,0},{2,1},{3,2},{4,7},{5,4},{6,5},{7,6},{8,11},{9,8},{10,9... | collective-permute-start | bytes 245768 | tf_op jit(solution)/shard_map/ppermute | solution.py:34
  6.4 5.3 %collective-permute-start.2 = (f32[32,128]{1,0:T(8,128)}, f32[32,128]{1,0:T(8,128)S(1)}, u32[]{:S(2)}, u32[]{:S(2)}) collective-permute-start(f32[32,128]{1,0:T(8,128)} %get-tuple-element.58.own_ref.refs_1_), channel_id=1, source_target_pairs={{0,2},{1,3},{2,0},{3,1},{4,6},{5,7},{6,4},{7,5},{8,10},{9,11},{10,... | collective-permute-start | bytes 49160 | tf_op jit(solution)/shard_map/ppermute | solution.py:34
  10.8 1.5 %copy-start.3 = (f32[3,8,16,512]{3,2,1,0:T(8,128)}, f32[3,8,16,512]{3,2,1,0:T(8,128)S(1)}, u32[]{:S(2)}) copy-start(f32[3,8,16,512]{3,2,1,0:T(8,128)S(1)} %shard_map.103.refs_5_.refs_4_) | copy-start | bytes 2359300
  11.7 12.3 %copy-start.11 = (f32[3,8,16,512]{3,2,1,0:T(8,128)S(1)}, f32[3,8,16,512]{3,2,1,0:T(8,128)}, u32[]{:S(2)}) copy-start(f32[3,8,16,512]{3,2,1,0:T(8,128)} %refs_2_.3) | copy-start | bytes 2359300
  12.3 1.7 %copy-start.27 = (f32[32,128]{1,0:T(8,128)S(1)}, f32[32,128]{1,0:T(8,128)}, u32[]{:S(2)}) copy-start(f32[32,128]{1,0:T(8,128)} %get-tuple-element.58.own_ref.refs_1_) | copy-start | bytes 49156
  12.3 5.9 %collective-permute-start.3 = (f32[88,512]{1,0:T(8,128)S(1)}, f32[88,512]{1,0:T(8,128)S(1)}, u32[]{:S(2)}, u32[]{:S(2)}) collective-permute-start(f32[88,512]{1,0:T(8,128)S(1)} %get-tuple-element.60._), channel_id=1, source_target_pairs={{0,4},{4,0},{8,12},{12,8},{16,20},{20,16},{24,28},{28,24},{1,5},{5... | collective-permute-start | bytes 540680 | tf_op jit(solution)/shard_map/ppermute | solution.py:29
  14.0 5.0 %copy-start.20 = (s32[1024]{0:T(1024)S(1)}, s32[1024]{0:T(1024)}, u32[]{:S(2)}) copy-start(s32[1024]{0:T(1024)} %param.12) | copy-start | bytes 12292
  14.0 10.0 %copy-start.26 = (f32[32,640]{1,0:T(8,128)S(1)}, f32[32,640]{1,0:T(8,128)}, u32[]{:S(2)}) copy-start(f32[32,640]{1,0:T(8,128)} %get-tuple-element.57.refs_7_) | copy-start | bytes 245764
  18.2 1.2 %copy-start.17 = (f32[32,640]{1,0:T(8,128)S(1)}, f32[32,640]{1,0:T(8,128)}, u32[]{:S(2)}) copy-start(f32[32,640]{1,0:T(8,128)} %copy-done.16) | copy-start | bytes 245764
  18.2 5.8 %copy-start.2 = (bf16[512,1024]{1,0:T(8,128)(2,1)S(1)}, bf16[512,1024]{1,0:T(8,128)(2,1)}, u32[]{:S(2)}) copy-start(bf16[512,1024]{1,0:T(8,128)(2,1)} %get-tuple-element.65.refs_15_.hot_ref) | copy-start | bytes 3145732
  18.2 5.8 %collective-permute-start.4 = (f32[88,512]{1,0:T(8,128)S(1)}, f32[88,512]{1,0:T(8,128)S(1)}, u32[]{:S(2)}, u32[]{:S(2)}) collective-permute-start(f32[88,512]{1,0:T(8,128)S(1)} %get-tuple-element.64), channel_id=1, source_target_pairs={{0,0},{4,8},{8,4},{12,16},{16,12},{20,24},{24,20},{28,28},{1,1},{5... | collective-permute-start | bytes 540680 | tf_op jit(solution)/shard_map/ppermute | solution.py:29
  19.4 4.7 %copy-start.4 = (f32[3,8,16,512]{3,2,1,0:T(8,128)S(1)}, f32[3,8,16,512]{3,2,1,0:T(8,128)}, u32[]{:S(2)}) copy-start(f32[3,8,16,512]{3,2,1,0:T(8,128)} %copy-done.3) | copy-start | bytes 2359300
  19.4 4.7 %copy-start.7 = (f32[8,16,512]{2,1,0:T(8,128)S(1)}, f32[8,16,512]{2,1,0:T(8,128)}, u32[]{:S(2)}) copy-start(f32[8,16,512]{2,1,0:T(8,128)} %refs_3_.7) | copy-start | bytes 786436
  19.4 4.7 %copy-start.21 = (f32[3,1024]{1,0:T(4,128)S(1)}, f32[3,1024]{1,0:T(4,128)}, u32[]{:S(2)}) copy-start(f32[3,1024]{1,0:T(4,128)} %refs_13_.5) | copy-start | bytes 36868
  19.4 4.7 %copy-start.25 = (f32[40,640]{1,0:T(8,128)S(1)}, f32[40,640]{1,0:T(8,128)}, u32[]{:S(2)}) copy-start(f32[40,640]{1,0:T(8,128)} %get-tuple-element.56.refs_6_) | copy-start | bytes 307204
  26.6 40.7 %copy-start.9 = (f32[8,16,512]{2,1,0:T(8,128)}, f32[8,16,512]{2,1,0:T(8,128)S(1)}, u32[]{:S(2)}) copy-start(f32[8,16,512]{2,1,0:T(8,128)S(1)} %get-tuple-element.78.refs_12_) | copy-start | bytes 786436
  26.6 4.3 %collective-permute-start.5 = (f32[24,640]{1,0:T(8,128)S(1)}, f32[24,640]{1,0:T(8,128)S(1)}, u32[]{:S(2)}, u32[]{:S(2)}) collective-permute-start(f32[24,640]{1,0:T(8,128)S(1)} %get-tuple-element.69.refs_7_), channel_id=1, source_target_pairs={{0,3},{1,0},{2,1},{3,2},{4,7},{5,4},{6,5},{7,6},{8,11},{9,8},{10,9... | collective-permute-start | bytes 184328 | tf_op jit(solution)/shard_map/ppermute | solution.py:34
  26.6 4.2 %collective-permute-start.7 = (f32[24,640]{1,0:T(8,128)S(1)}, f32[24,640]{1,0:T(8,128)S(1)}, u32[]{:S(2)}, u32[]{:S(2)}) collective-permute-start(f32[24,640]{1,0:T(8,128)S(1)} %get-tuple-element.70.refs_6_), channel_id=1, source_target_pairs={{0,1},{1,2},{2,3},{3,0},{4,5},{5,6},{6,7},{7,4},{8,9},{9,10},{10,1... | collective-permute-start | bytes 184328 | tf_op jit(solution)/shard_map/ppermute | solution.py:34
  27.1 3.7 %collective-permute-start.6 = (f32[24,128]{1,0:T(8,128)S(1)}, f32[24,128]{1,0:T(8,128)S(1)}, u32[]{:S(2)}, u32[]{:S(2)}) collective-permute-start(f32[24,128]{1,0:T(8,128)S(1)} %get-tuple-element.68.own_ref.refs_1_), channel_id=1, source_target_pairs={{0,2},{1,3},{2,0},{3,1},{4,6},{5,7},{6,4},{7,5},{8,10},{9,11},{10,... | collective-permute-start | bytes 36872 | tf_op jit(solution)/shard_map/ppermute | solution.py:34
  31.4 8.8 %collective-permute-start.8 = (f32[56,512]{1,0:T(8,128)S(1)}, f32[56,512]{1,0:T(8,128)S(1)}, u32[]{:S(2)}, u32[]{:S(2)}) collective-permute-start(f32[56,512]{1,0:T(8,128)S(1)} %get-tuple-element.72._), channel_id=1, source_target_pairs={{0,4},{4,0},{8,12},{12,8},{16,20},{20,16},{24,28},{28,24},{1,5},{5... | collective-permute-start | bytes 344072 | tf_op jit(solution)/shard_map/ppermute | solution.py:29
  40.2 5.5 %collective-permute-start.9 = (f32[56,512]{1,0:T(8,128)S(1)}, f32[56,512]{1,0:T(8,128)S(1)}, u32[]{:S(2)}, u32[]{:S(2)}) collective-permute-start(f32[56,512]{1,0:T(8,128)S(1)} %get-tuple-element.77), channel_id=1, source_target_pairs={{0,0},{4,8},{8,4},{12,16},{16,12},{20,24},{24,20},{28,28},{1,1},{5... | collective-permute-start | bytes 344072 | tf_op jit(solution)/shard_map/ppermute | solution.py:29
  48.2 4.3 %collective-permute-start.10 = (f32[24,640]{1,0:T(8,128)S(1)}, f32[24,640]{1,0:T(8,128)S(1)}, u32[]{:S(2)}, u32[]{:S(2)}) collective-permute-start(f32[24,640]{1,0:T(8,128)S(1)} %get-tuple-element.82.refs_7_), channel_id=1, source_target_pairs={{0,3},{1,0},{2,1},{3,2},{4,7},{5,4},{6,5},{7,6},{8,11},{9,8},{10,9... | collective-permute-start | bytes 184328 | tf_op jit(solution)/shard_map/ppermute | solution.py:34
  48.3 4.2 %collective-permute-start.12 = (f32[24,640]{1,0:T(8,128)S(1)}, f32[24,640]{1,0:T(8,128)S(1)}, u32[]{:S(2)}, u32[]{:S(2)}) collective-permute-start(f32[24,640]{1,0:T(8,128)S(1)} %get-tuple-element.83.refs_6_), channel_id=1, source_target_pairs={{0,1},{1,2},{2,3},{3,0},{4,5},{5,6},{6,7},{7,4},{8,9},{9,10},{10,1... | collective-permute-start | bytes 184328 | tf_op jit(solution)/shard_map/ppermute | solution.py:34
  48.8 3.7 %collective-permute-start.11 = (f32[24,128]{1,0:T(8,128)S(1)}, f32[24,128]{1,0:T(8,128)S(1)}, u32[]{:S(2)}, u32[]{:S(2)}) collective-permute-start(f32[24,128]{1,0:T(8,128)S(1)} %get-tuple-element.81.own_ref.refs_1_), channel_id=1, source_target_pairs={{0,2},{1,3},{2,0},{3,1},{4,6},{5,7},{6,4},{7,5},{8,10},{9,11},{10,... | collective-permute-start | bytes 36872 | tf_op jit(solution)/shard_map/ppermute | solution.py:34
  53.0 8.8 %collective-permute-start.13 = (f32[56,512]{1,0:T(8,128)S(1)}, f32[56,512]{1,0:T(8,128)S(1)}, u32[]{:S(2)}, u32[]{:S(2)}) collective-permute-start(f32[56,512]{1,0:T(8,128)S(1)} %get-tuple-element.85._), channel_id=1, source_target_pairs={{0,4},{4,0},{8,12},{12,8},{16,20},{20,16},{24,28},{28,24},{1,5},{5... | collective-permute-start | bytes 344072 | tf_op jit(solution)/shard_map/ppermute | solution.py:29
  61.9 5.4 %collective-permute-start.14 = (f32[56,512]{1,0:T(8,128)S(1)}, f32[56,512]{1,0:T(8,128)S(1)}, u32[]{:S(2)}, u32[]{:S(2)}) collective-permute-start(f32[56,512]{1,0:T(8,128)S(1)} %get-tuple-element.90), channel_id=1, source_target_pairs={{0,0},{4,8},{8,4},{12,16},{16,12},{20,24},{24,20},{28,28},{1,1},{5... | collective-permute-start | bytes 344072 | tf_op jit(solution)/shard_map/ppermute | solution.py:29
  67.2 2.5 %copy-start.34 = (f32[8,128]{1,0:T(8,128)}, f32[8,128]{1,0:T(8,128)S(1)}, u32[]{:S(2)}) copy-start(f32[8,128]{1,0:T(8,128)S(1)} %get-tuple-element.99.refs_7_) | copy-start | bytes 12292
  69.7 3.3 %copy-start.12 = (f32[3,8,16,512]{3,2,1,0:T(8,128)}, f32[3,8,16,512]{3,2,1,0:T(8,128)S(1)}, u32[]{:S(2)}) copy-start(f32[3,8,16,512]{3,2,1,0:T(8,128)S(1)} %get-tuple-element.92.refs_2_) | copy-start | bytes 2359300
  69.7 3.3 %copy-start.28 = (f32[24,640]{1,0:T(8,128)}, f32[24,640]{1,0:T(8,128)S(1)}, u32[]{:S(2)}) copy-start(f32[24,640]{1,0:T(8,128)S(1)} %get-tuple-element.95.refs_6_) | copy-start | bytes 184324
  69.8 3.3 %copy-start.30 = (f32[24,640]{1,0:T(8,128)}, f32[24,640]{1,0:T(8,128)S(1)}, u32[]{:S(2)}) copy-start(f32[24,640]{1,0:T(8,128)S(1)} %get-tuple-element.94.refs_7_) | copy-start | bytes 184324
  69.8 8.8 %copy-start.32 = (f32[24,128]{1,0:T(8,128)}, f32[24,128]{1,0:T(8,128)S(1)}, u32[]{:S(2)}) copy-start(f32[24,128]{1,0:T(8,128)S(1)} %get-tuple-element.93.own_ref.refs_1_) | copy-start | bytes 36868
  69.8 4.3 %collective-permute-start.15 = (f32[24,640]{1,0:T(8,128)S(1)}, f32[24,640]{1,0:T(8,128)S(1)}, u32[]{:S(2)}, u32[]{:S(2)}) collective-permute-start(f32[24,640]{1,0:T(8,128)S(1)} %get-tuple-element.94.refs_7_), channel_id=1, source_target_pairs={{0,3},{1,0},{2,1},{3,2},{4,7},{5,4},{6,5},{7,6},{8,11},{9,8},{10,9... | collective-permute-start | bytes 184328 | tf_op jit(solution)/shard_map/ppermute | solution.py:34
  69.8 4.2 %collective-permute-start.17 = (f32[24,640]{1,0:T(8,128)S(1)}, f32[24,640]{1,0:T(8,128)S(1)}, u32[]{:S(2)}, u32[]{:S(2)}) collective-permute-start(f32[24,640]{1,0:T(8,128)S(1)} %get-tuple-element.95.refs_6_), channel_id=1, source_target_pairs={{0,1},{1,2},{2,3},{3,0},{4,5},{5,6},{6,7},{7,4},{8,9},{9,10},{10,1... | collective-permute-start | bytes 184328 | tf_op jit(solution)/shard_map/ppermute | solution.py:34
  70.3 3.7 %collective-permute-start.16 = (f32[24,128]{1,0:T(8,128)S(1)}, f32[24,128]{1,0:T(8,128)S(1)}, u32[]{:S(2)}, u32[]{:S(2)}) collective-permute-start(f32[24,128]{1,0:T(8,128)S(1)} %get-tuple-element.93.own_ref.refs_1_), channel_id=1, source_target_pairs={{0,2},{1,3},{2,0},{3,1},{4,6},{5,7},{6,4},{7,5},{8,10},{9,11},{10,... | collective-permute-start | bytes 36872 | tf_op jit(solution)/shard_map/ppermute | solution.py:34
  73.0 2.2 %copy-start.5 = (f32[3,8,16,512]{3,2,1,0:T(8,128)}, f32[3,8,16,512]{3,2,1,0:T(8,128)S(1)}, u32[]{:S(2)}) copy-start(f32[3,8,16,512]{3,2,1,0:T(8,128)S(1)} %shard_map.120.refs_5_.refs_4_) | copy-start | bytes 2359300
  75.3 9.1 %copy-start.22 = (s32[8,16,512]{2,1,0:T(8,128)S(1)}, s32[8,16,512]{2,1,0:T(8,128)}, u32[]{:S(2)}) copy-start(s32[8,16,512]{2,1,0:T(8,128)} %tiles_ref.1) | copy-start | bytes 786436
  75.3 6.9 %collective-permute-start.18 = (f32[56,512]{1,0:T(8,128)S(1)}, f32[56,512]{1,0:T(8,128)S(1)}, u32[]{:S(2)}, u32[]{:S(2)}) collective-permute-start(f32[56,512]{1,0:T(8,128)S(1)} %get-tuple-element.97._), channel_id=1, source_target_pairs={{0,4},{4,0},{8,12},{12,8},{16,20},{20,16},{24,28},{28,24},{1,5},{5... | collective-permute-start | bytes 344072 | tf_op jit(solution)/shard_map/ppermute | solution.py:29
  82.2 2.7 %copy-start.18 = (f32[8,4,8,128]{3,2,1,0:T(8,128)}, f32[8,4,8,128]{3,2,1,0:T(8,128)S(1)}, u32[]{:S(2)}) copy-start(f32[8,4,8,128]{3,2,1,0:T(8,128)S(1)} %shard_map.122.refs_4_) | copy-start | bytes 393220
  82.2 2.7 %copy-start.23 = (f32[56,512]{1,0:T(8,128)}, f32[56,512]{1,0:T(8,128)S(1)}, u32[]{:S(2)}) copy-start(f32[56,512]{1,0:T(8,128)S(1)} %collective-permute-done.18.refs_10_) | copy-start | bytes 344068
  82.2 10.1 %collective-permute-start.19 = (f32[56,512]{1,0:T(8,128)}, f32[56,512]{1,0:T(8,128)}, u32[]{:S(2)}, u32[]{:S(2)}) collective-permute-start(f32[56,512]{1,0:T(8,128)} %get-tuple-element.103), channel_id=1, source_target_pairs={{0,0},{4,8},{8,4},{12,16},{16,12},{20,24},{24,20},{28,28},{1,1},{5... | collective-permute-start | bytes 344072 | tf_op jit(solution)/shard_map/ppermute | solution.py:29
  84.9 13.1 %copy-start.6 = (f32[3,8,16,512]{3,2,1,0:T(8,128)S(1)}, f32[3,8,16,512]{3,2,1,0:T(8,128)}, u32[]{:S(2)}) copy-start(f32[3,8,16,512]{3,2,1,0:T(8,128)} %copy-done.5) | copy-start | bytes 2359300
  86.0 12.0 %copy-start.8 = (f32[8,16,512]{2,1,0:T(8,128)S(1)}, f32[8,16,512]{2,1,0:T(8,128)}, u32[]{:S(2)}) copy-start(f32[8,16,512]{2,1,0:T(8,128)} %refs_3_.7) | copy-start | bytes 786436
  86.0 12.0 %copy-start.10 = (f32[8,16,512]{2,1,0:T(8,128)S(1)}, f32[8,16,512]{2,1,0:T(8,128)}, u32[]{:S(2)}) copy-start(f32[8,16,512]{2,1,0:T(8,128)} %copy-done.9) | copy-start | bytes 786436
  92.3 13.7 %collective-permute-start.20 = (f32[256]{0:T(256)S(1)}, f32[256]{0:T(256)S(1)}, u32[]{:S(2)}, u32[]{:S(2)}) collective-permute-start(f32[256]{0:T(256)S(1)} %bitcast.47), channel_id=1, source_target_pairs={{0,4},{4,0},{8,12},{12,8},{16,20},{20,16},{24,28},{28,24},{1,5},{5... | collective-permute-start | bytes 3080 | tf_op jit(solution)/shard_map/ppermute | solution.py:29
  95.4 10.6 %collective-permute-start.21 = (f32[256]{0:T(256)S(1)}, f32[256]{0:T(256)S(1)}, u32[]{:S(2)}, u32[]{:S(2)}) collective-permute-start(f32[256]{0:T(256)S(1)} %bitcast.46), channel_id=1, source_target_pairs={{0,0},{4,8},{8,4},{12,16},{16,12},{20,24},{24,20},{28,28},{1,1},{5... | collective-permute-start | bytes 3080 | tf_op jit(solution)/shard_map/ppermute | solution.py:29
  (11 other events, 9.6 us)

commit v2 on v1

--- a/solution.py
+++ b/solution.py
@@ -20,13 +20,16 @@
 NT = (((1,), (1,)), ((), ()))
 
 
-def swapped(value, axis, odd):
+def swapped(value, axis):
     count = lax.axis_size(axis)
-    first = 1 if odd else 0
-    partner = list(range(count))
-    for i in range(first, count - 1, 2):
-        partner[i], partner[i + 1] = i + 1, i
-    return lax.ppermute(value, axis, list(enumerate(partner)))
+    return lax.ppermute(value, axis, [(i, i ^ 1) for i in range(count)])
+
+
+def relayed(value, axis):
+    count = lax.axis_size(axis)
+    target = [i + 2 if i % 2 == 0 else i - 2 for i in range(count)]
+    target[count - 2], target[1] = count - 1, 0
+    return lax.ppermute(value, axis, list(enumerate(target)))
 
 
 def cycled(value, axis, steps):
@@ -95,7 +98,7 @@
     store_positions(disp_ref, base_ref, node_ref, hot, [(up_ref, extent_z), (down_ref, extent_z), (far_ref, 0)])
 
 
-def first_body(disp_ref, base_ref, node_ref, moduli_ref, bins_ref, up_ref, down_ref, far_ref, hot_ref):
+def first_body(_, disp_ref, base_ref, node_ref, moduli_ref, bins_ref, up_ref, down_ref, far_ref, hot_ref):
     _, extent_x, extent_y, extent_z = disp_ref.shape
     _, column = node_split(node_ref, extent_z)
     hot_ref[...] = one_hot_z(column, extent_z)
@@ -246,7 +249,7 @@
     is_odd = flag_ref[4] > 0.5
     to_even = jnp.where(is_odd, made[0:1], made[2:3])
     to_odd = jnp.where(is_odd, made[2:3], made[0:1])
-    partial_ref[...] = jnp.concatenate([to_even, made[1:2], to_odd, made[3:]], axis=0)
+    partial_ref[...] = jnp.concatenate([made[1:2], to_even, to_odd, made[3:]], axis=0)
 
 
 def turn_body(extent_z, node_ref, out_ref):
@@ -264,7 +267,7 @@
     tiles = tiles_ref[...].reshape(extent_x * extent_y, extent_z)
     device = lax.div(tiles, jnp.int32(TILE_DEV))
     slot = tiles - device * TILE_DEV
-    offset = (device - own_ref[0]).astype(F32).astype(BF16)
+    offset = (device.astype(F32) - own_ref[5]).astype(BF16)
     found = gather_nodes([offset], row, hot)
     side = jnp.where(found < -0.5, 0, jnp.where(found > 0.5, 2, 1))
     found_slot = gather_nodes([slot.astype(F32).astype(BF16)], row, hot).astype(jnp.int32)
@@ -473,8 +476,8 @@
     bin_at = lax.axis_index("bin")
     dom_at, dom_count = lax.axis_index("dom"), lax.axis_size("dom")
     own_device = dom_at * bin_count + bin_at
-    checks = (bin_at > 0, bin_at < bin_count - 1, dom_at > 0, dom_at < dom_count - 1, dom_at % 2 == 1)
-    flags = jnp.stack(checks).astype(F32)
+    checks = (bin_at > 0, bin_at < bin_count - 1, dom_at > 0, dom_at < dom_count - 1, (dom_at & 1) == 1)
+    flags = jnp.concatenate([jnp.stack(checks).astype(F32), own_device[None].astype(F32)])
     node = segment_node.reshape(blocks, SEG)
     bins = contact_bin[:, :, 0]
     rows = 3 * extent_x
@@ -489,9 +492,9 @@
         struct(rows + 8, SEG),
         jax.ShapeDtypeStruct((extent_z, segments), BF16),
     ]
-    first_args = (displacement, segment_base, node, moduli, bins)
-    first_specs = [full(*v.shape) for v in first_args]
-    first_specs[3] = pl.BlockSpec((2, extent_x, 8, extent_z), lambda i: (0, 0, extent_y // 8 - 1, 0))
+    first_args = (flags, displacement, segment_base, node, moduli, bins)
+    first_specs = [SCALARS] + [full(*v.shape) for v in first_args[1:]]
+    first_specs[4] = pl.BlockSpec((2, extent_x, 8, extent_z), lambda i: (0, 0, extent_y // 8 - 1, 0))
     up, down, far, hot = pl.pallas_call(
         first_body,
         grid=(1,),
@@ -508,7 +511,7 @@
     )(node)
     (tile_places,) = call(
         tile_body, [jax.ShapeDtypeStruct((8, segments), jnp.int32)], specs=[SCALARS] + [WHOLE] * 3
-    )(own_device[None].astype(jnp.int32), element_tile, node, hot)
+    )(flags, element_tile, node, hot)
     heat = jnp.zeros((blocks, SEG), F32)
     rim = moduli
     for step in range(steps):
@@ -523,7 +526,7 @@
             [WHOLE] * 2,
         )(displacement, moduli)
         if first:
-            of_bins = [bins.astype(F32)]
+            of_bins = [far[rows : rows + steps, :blocks]]
             of_bins += [v[rows : rows + steps, extent_z : extent_z + blocks] for v in (lower, upper)]
             of_bins += [v[rows : rows + steps, :blocks] for v in others]
             all_bins = jnp.concatenate(of_bins, axis=1).astype(jnp.int32)
@@ -544,7 +547,7 @@
             compiler_params=pltpu.CompilerParams(vmem_limit_bytes=VMEM_BYTES),
             cost_estimate=pl.CostEstimate(flops=1_000, bytes_accessed=1_000, transcendentals=0),
         )(*layer_args)
-        of_even = swapped(to_even, "dom", False)
+        relay = swapped(to_odd, "dom")
         near_blocks = 2 * blocks
         far_blocks = blocks * (bin_count - 2)
         pair_scratch = lambda count: [
@@ -556,9 +559,10 @@
             [struct(blocks, 4, 8, SEG)],
             pair_scratch(near_blocks),
             [SCALARS, WHOLE, WHOLE, pl.BlockSpec(memory_space=pl.ANY)],
-        )(all_bins[step], far, lower, to_even)
-        to_odd, sums, of_even = lax.optimization_barrier((to_odd, sums, of_even))
-        of_odd = swapped(to_odd, "dom", True)
+        )(all_bins[step], far, lower, to_odd)
+        to_even, sums, relay = lax.optimization_barrier((to_even, sums, relay))
+        of_odd = relayed(relay, "dom")
+        of_even = swapped(to_even, "dom")
         pair_args = [all_bins[step], far, upper, others, sums, node, turned, heat]
         if last:
             pair_args += [tile_places, flags]
@@ -589,11 +593,9 @@
             up, down, far = made[2:5]
         if first:
             rim = made[-1]
-    odd_weight = jnp.where(dom_at % 2 == 1, flags[3], flags[2])
-    from_even, from_odd = swapped(heat[0], "dom", False), swapped(heat[2], "dom", True)
-    if dom_count % 2:
-        from_even = from_even * flags[3]
-    tile_heat = heat[1] + from_even + from_odd * odd_weight
+    got = swapped(heat[1:3], "dom")
+    passed = relayed(got[1], "dom")
+    tile_heat = heat[0] + got[0] + passed
     return displacement, velocity, tile_heat
 
 

time: 108 us -> 98.4 us (0.911)
  local copies, waits for them, and re-layouts: 8.54 us -> 0.78 us
  waiting for transfers between devices: 3.13 us -> 10 us
  starting transfers between devices: 30.8 us -> 24.2 us
  between operations: 2.66 us -> 1.02 us
    ppermute x10 -> x14, starting transfers between devices: 22.4 us -> 14.7 us  [the longest x9 7.96 us: swapped(): return lax.ppermute(value, axis, [(i, i ^ 1) for i in range(count)])]
    ppermute x10 -> x14, waiting for transfers between devices: 0.63 us -> 7.79 us  [the longest x9 6.17 us: swapped(): return lax.ppermute(value, axis, [(i, i ^ 1) for i in range(count)])]
    unnamed x74 -> x24, local copies, waits for them, and re-layouts: 7.75 us -> 0.65 us
  transfers between devices with their start and end apart: 22 -> 26, of which waited for: 4 -> 11; matrix products, arithmetic and copies ran while one was open for 1% -> 0% of each run, Pallas kernels for 44% -> 49%
where the time goes in v2:
time: 98.4 us; the launch traced here: 97.7 us
  Pallas kernels  60.4 us (61%)
  starting transfers between devices  24.2 us (25%)
  waiting for transfers between devices  10 us (10%)
  other arithmetic  1.25 us (1%)
  between operations  1.02 us (1%)
    pallas_call x4, Pallas kernels, per_device(): call(functools.partial(rest_body, bin_count, last), [struct(3 * extent_x...  19.5 us
    pallas_call x4, Pallas kernels, per_device(): call(functools.partial(near_body, bin_count), [struct(blocks, 4, 8, SEG)]...  15.2 us
    pallas_call x4, Pallas kernels, per_device(): call(functools.partial(update_body, first, last), update_outs, [pltpu.VME...  10.2 us
    ppermute x12, starting transfers between devices, cycled(): lax.ppermute(value, axis, [(source, (source + steps) % count) for source...  9.47 us
    pallas_call x4, Pallas kernels, per_device(): call(inner_body, [struct(*shape)], [pltpu.VMEM((extent_x, 9, extent_y, ex...  8.68 us
    ppermute x9, starting transfers between devices, swapped(): return lax.ppermute(value, axis, [(i, i ^ 1) for i in range(count)])  7.96 us
    ppermute x5, starting transfers between devices, relayed(): return lax.ppermute(value, axis, list(enumerate(target)))  6.76 us
    ppermute x9, waiting for transfers between devices, swapped(): return lax.ppermute(value, axis, [(i, i ^ 1) for i in range(count)])  6.17 us
  transfers between devices with their start and end apart: 26, of which 11 were waited for; matrix products, arithmetic and copies ran while one was open for 0% of the time, Pallas kernels for 49%

profile of v2, /device:TPU:0, one launch (start us, length us, event | category | flops | bytes accessed | tf_op | source)
XLA Modules:
  0.0 97.7 jit_solution(15374844695717181107)
XLA Ops:
  0.8 0.6 pad_maximum_fusion._.refs_0_.own_ref.refs_9_
  1.4 3.2 %shard_map.104 = (f32[40,640]{1,0:T(8,128)}, f32[32,640]{1,0:T(8,128)}, f32[32,128]{1,0:T(8,128)}, bf16[512,1024]{1,0:T(8,128)(2,1)}) custom-call(f32[6]{0:T(128)} %pad_maximum_fusion._.refs_0_.own_ref.refs_9_, f32[3,8,16,512]{3,2,1,0:T(8,128)} %refs_1_.3, f32[3,1024]{1,0:T(4,128)} %refs_13_.5, s32[8,128]{1,0:T(8,128)} %bitcast.22, ...), custom_call_target="tpu_custom_call" | custom-call | flops 1000 | bytes 1000 | tf_op jit(solution)/shard_map/pallas_call | solution.py:498
  5.1 2.0 %collective-permute-start.1 = (f32[32,640]{1,0:T(8,128)}, f32[32,640]{1,0:T(8,128)S(1)}, u32[]{:S(2)}, u32[]{:S(2)}) collective-permute-start(f32[32,640]{1,0:T(8,128)} %get-tuple-element.58.refs_7_), channel_id=1, source_target_pairs={{0,3},{1,0},{2,1},{3,2},{4,7},{5,4},{6,5},{7,6},{8,11},{9,8},{10,9... | collective-permute-start | bytes 245768 | tf_op jit(solution)/shard_map/ppermute | solution.py:37
  7.1 2.3 %collective-permute-start.2 = (f32[32,128]{1,0:T(8,128)}, f32[32,128]{1,0:T(8,128)S(1)}, u32[]{:S(2)}, u32[]{:S(2)}) collective-permute-start(f32[32,128]{1,0:T(8,128)} %get-tuple-element.56.own_ref.refs_1_), channel_id=1, source_target_pairs={{0,2},{1,3},{2,0},{3,1},{4,6},{5,7},{6,4},{7,5},{8,10},{9,11},{10,... | collective-permute-start | bytes 49160 | tf_op jit(solution)/shard_map/ppermute | solution.py:37
  9.3 2.2 %shard_map.103.refs_5_.refs_4_ = f32[3,8,16,512]{3,2,1,0:T(8,128)S(1)} custom-call(f32[3,8,16,512]{3,2,1,0:T(8,128)S(1)} %copy-done.1, f32[2,8,16,512]{3,2,1,0:T(8,128)S(1)} %copy-done), custom_call_target="tpu_custom_call" | custom-call | flops 1000 | bytes 1000 | tf_op jit(solution)/shard_map/pallas_call | solution.py:522
  11.5 0.6 collective-permute-done.2
  12.1 0.6 copy-done.11
  12.7 0.6 shard_map.105
  13.3 1.6 %collective-permute-start.3 = (f32[88,512]{1,0:T(8,128)S(1)}, f32[88,512]{1,0:T(8,128)S(1)}, u32[]{:S(2)}, u32[]{:S(2)}) collective-permute-start(f32[88,512]{1,0:T(8,128)S(1)} %get-tuple-element.60._), channel_id=1, source_target_pairs={{0,4},{4,0},{8,12},{12,8},{16,20},{20,16},{24,28},{28,24},{1,5},{5... | collective-permute-start | bytes 540680 | tf_op jit(solution)/shard_map/ppermute | solution.py:25
  15.0 3.9 %shard_map.106.refs_4_ = f32[8,4,8,128]{3,2,1,0:T(8,128)S(1)} custom-call(s32[32]{0:T(128)S(1)} %get-tuple-element.114.bins_ref.refs_0_, f32[32,128]{1,0:T(8,128)S(1)} %copy-done.10, f32[40,640]{1,0:T(8,128)S(1)} %collective-permute-done.refs_3_.lower_ref.refs_8_, f32[88,512]{1,0:T(8,128)S(1)} %get-tuple-element.60._), custom_call_target="tpu_custom_call" | custom-call | flops 1000 | bytes 1000 | tf_op jit(solution)/shard_map/pallas_call | solution.py:557
  18.9 0.6 collective-permute-done.3
  19.5 1.5 %collective-permute-start.4 = (f32[88,512]{1,0:T(8,128)S(1)}, f32[88,512]{1,0:T(8,128)S(1)}, u32[]{:S(2)}, u32[]{:S(2)}) collective-permute-start(f32[88,512]{1,0:T(8,128)S(1)} %get-tuple-element.63), channel_id=1, source_target_pairs={{0,4},{4,0},{8,12},{12,8},{16,20},{20,16},{24,28},{28,24},{1,5},{5... | collective-permute-start | bytes 540680 | tf_op jit(solution)/shard_map/ppermute | solution.py:25
  21.0 1.6 %collective-permute-start.5 = (f32[88,512]{1,0:T(8,128)S(1)}, f32[88,512]{1,0:T(8,128)S(1)}, u32[]{:S(2)}, u32[]{:S(2)}) collective-permute-start(f32[88,512]{1,0:T(8,128)S(1)} %collective-permute-done.3), channel_id=1, source_target_pairs={{0,8},{4,0},{8,16},{12,4},{16,24},{20,12},{24,28},{28,20},{1,9},{5... | collective-permute-start | bytes 540680 | tf_op jit(solution)/shard_map/ppermute | solution.py:32
  23.0 5.0 %shard_map.108 = (f32[384,512]{1,0:T(8,128)S(1)}, f32[8,128]{1,0:T(8,128)S(1)}) custom-call(s32[32]{0:T(128)S(1)} %get-tuple-element.114.bins_ref.refs_0_, f32[32,128]{1,0:T(8,128)S(1)} %copy-done.10, f32[32,640]{1,0:T(8,128)S(1)} %collective-permute-done.1.refs_4_.refs_2_.refs_9_, f32[1,32,128]{2,1,0:T(8,128)S(1)} %bitcast.33, ...), custom_call_target="tpu_custom_call" | custom-call | flops 1000 | bytes 1000 | tf_op jit(solution)/shard_map/pallas_call | solution.py:569
  27.9 0.6 collective-permute-done.5.refs_11_
  28.6 2.5 %shard_map.109 = (f32[3,8,16,512]{3,2,1,0:T(8,128)S(1)}, f32[3,8,16,512]{3,2,1,0:T(8,128)S(1)}, f32[24,640]{1,0:T(8,128)S(1)}, f32[24,640]{1,0:T(8,128)S(1)}, f3...) custom-call(f32[6]{0:T(128)S(1)} %copy-done.11, f32[3,8,16,512]{3,2,1,0:T(8,128)S(1)} %copy-done.1, ...), custom_call_target="tpu_custom_call" | custom-call | flops 1000 | bytes 1000 | tf_op jit(solution)/shard_map/pallas_call | solution.py:585
  31.6 1.2 %collective-permute-start.7 = (f32[24,128]{1,0:T(8,128)S(1)}, f32[24,128]{1,0:T(8,128)S(1)}, u32[]{:S(2)}, u32[]{:S(2)}) collective-permute-start(f32[24,128]{1,0:T(8,128)S(1)} %get-tuple-element.68.own_ref.refs_1_), channel_id=1, source_target_pairs={{0,2},{1,3},{2,0},{3,1},{4,6},{5,7},{6,4},{7,5},{8,10},{9,11},{10,... | collective-permute-start | bytes 36872 | tf_op jit(solution)/shard_map/ppermute | solution.py:37
  32.8 2.2 %shard_map.110.refs_5_.refs_4_ = f32[3,8,16,512]{3,2,1,0:T(8,128)S(1)} custom-call(f32[3,8,16,512]{3,2,1,0:T(8,128)S(1)} %get-tuple-element.66.disp_ref.refs_1_.refs_2_, f32[2,8,16,512]{3,2,1,0:T(8,128)S(1)} %copy-done), custom_call_target="tpu_custom_call" | custom-call | flops 1000 | bytes 1000 | tf_op jit(solution)/shard_map/pallas_call | solution.py:522
  35.5 0.6 shard_map.111
  36.1 3.6 %shard_map.112.refs_4_ = f32[8,4,8,128]{3,2,1,0:T(8,128)S(1)} custom-call(s32[32]{0:T(128)S(1)} %get-tuple-element.113.bins_ref.refs_0_, f32[24,128]{1,0:T(8,128)S(1)} %get-tuple-element.68.own_ref.refs_1_, f32[24,640]{1,0:T(8,128)S(1)} %collective-permute-done.8.refs_3_.lower_ref.refs_8_, f32[56,512]{1,0:T(8,128)S(1)} %get-tuple-element.72._), custom_call_target="tpu_custom_call" | custom-call | flops 1000 | bytes 1000 | tf_op jit(solution)/shard_map/pallas_call | solution.py:557
  39.7 1.5 %collective-permute-done.9 = f32[56,512]{1,0:T(8,128)S(1)} collective-permute-done((f32[56,512]{1,0:T(8,128)S(1)}, f32[56,512]{1,0:T(8,128)S(1)}, u32[]{:S(2)}, u32[]{:S(2)}) %collective-permute-start.9) | collective-permute-done | bytes 114720 | tf_op jit(solution)/shard_map/ppermute | solution.py:25
  41.8 0.6 collective-permute-start.11
  42.4 4.6 %shard_map.113 = (f32[384,512]{1,0:T(8,128)S(1)}, f32[8,128]{1,0:T(8,128)S(1)}) custom-call(s32[32]{0:T(128)S(1)} %get-tuple-element.113.bins_ref.refs_0_, f32[24,128]{1,0:T(8,128)S(1)} %get-tuple-element.68.own_ref.refs_1_, f32[24,640]{1,0:T(8,128)S(1)} %collective-permute-done.6.refs_4_.refs_2_.refs_9_, f32[1,24,128]{2,1,0:T(8,128)S(1)} %bitcast.37, ...), custom_call_target="tpu_custom_call" | custom-call | flops 1000 | bytes 1000 | tf_op jit(solution)/shard_map/pallas_call | solution.py:569
  47.0 1.0 %collective-permute-done.11.refs_11_ = f32[56,512]{1,0:T(8,128)S(1)} collective-permute-done((f32[56,512]{1,0:T(8,128)S(1)}, f32[56,512]{1,0:T(8,128)S(1)}, u32[]{:S(2)}, u32[]{:S(2)}) %collective-permute-start.11) | collective-permute-done | bytes 114720 | tf_op jit(solution)/shard_map/ppermute | solution.py:32
  48.0 2.5 %shard_map.114 = (f32[3,8,16,512]{3,2,1,0:T(8,128)S(1)}, f32[3,8,16,512]{3,2,1,0:T(8,128)S(1)}, f32[24,640]{1,0:T(8,128)S(1)}, f32[24,640]{1,0:T(8,128)S(1)}, f32[24,128]{1,0:T(8,128)S(1)}) custom-call(f32[6]{0:T(128)S(1)} %copy-done.11, f32[3,8,16,512]{3,2,1,0:T(8,128)S(1)} %get-tuple-element.66.disp_ref.refs_1_.refs_2_, ...), custom_call_target="tpu_custom_call" | custom-call | flops 1000 | bytes 1000 | tf_op jit(solution)/shard_map/pallas_call | solution.py:585
  51.1 0.7 collective-permute-start.13
  51.8 2.2 %shard_map.115.refs_5_.refs_4_ = f32[3,8,16,512]{3,2,1,0:T(8,128)S(1)} custom-call(f32[3,8,16,512]{3,2,1,0:T(8,128)S(1)} %get-tuple-element.79.disp_ref.refs_1_.refs_2_, f32[2,8,16,512]{3,2,1,0:T(8,128)S(1)} %copy-done), custom_call_target="tpu_custom_call" | custom-call | flops 1000 | bytes 1000 | tf_op jit(solution)/shard_map/pallas_call | solution.py:522
  54.0 0.8 collective-permute-done.13
  54.8 0.6 shard_map.116
  55.9 3.6 %shard_map.117.refs_4_ = f32[8,4,8,128]{3,2,1,0:T(8,128)S(1)} custom-call(s32[32]{0:T(128)S(1)} %get-tuple-element.112.bins_ref.refs_0_, f32[24,128]{1,0:T(8,128)S(1)} %get-tuple-element.81.own_ref.refs_1_, f32[24,640]{1,0:T(8,128)S(1)} %collective-permute-done.14.refs_3_.lower_ref.refs_8_, f32[56,512]{1,0:T(8,128)S(1)} %get-tuple-element.85._), custom_call_target="tpu_custom_call" | custom-call | flops 1000 | bytes 1000 | tf_op jit(solution)/shard_map/pallas_call | solution.py:557
  59.5 0.9 collective-permute-done.15
  60.4 1.2 %collective-permute-start.16 = (f32[56,512]{1,0:T(8,128)S(1)}, f32[56,512]{1,0:T(8,128)S(1)}, u32[]{:S(2)}, u32[]{:S(2)}) collective-permute-start(f32[56,512]{1,0:T(8,128)S(1)} %get-tuple-element.89), channel_id=1, source_target_pairs={{0,4},{4,0},{8,12},{12,8},{16,20},{20,16},{24,28},{28,24},{1,5},{5... | collective-permute-start | bytes 344072 | tf_op jit(solution)/shard_map/ppermute | solution.py:25
  61.6 1.5 %collective-permute-start.17 = (f32[56,512]{1,0:T(8,128)S(1)}, f32[56,512]{1,0:T(8,128)S(1)}, u32[]{:S(2)}, u32[]{:S(2)}) collective-permute-start(f32[56,512]{1,0:T(8,128)S(1)} %collective-permute-done.15), channel_id=1, source_target_pairs={{0,8},{4,0},{8,16},{12,4},{16,24},{20,12},{24,28},{28,20},{1,9},{5... | collective-permute-start | bytes 344072 | tf_op jit(solution)/shard_map/ppermute | solution.py:32
  63.1 4.7 %shard_map.118 = (f32[384,512]{1,0:T(8,128)S(1)}, f32[8,128]{1,0:T(8,128)S(1)}) custom-call(s32[32]{0:T(128)S(1)} %get-tuple-element.112.bins_ref.refs_0_, f32[24,128]{1,0:T(8,128)S(1)} %get-tuple-element.81.own_ref.refs_1_, f32[24,640]{1,0:T(8,128)S(1)} %collective-permute-done.12.refs_4_.refs_2_.refs_9_, f32[1,24,128]{2,1,0:T(8,128)S(1)} %bitcast.39, ...), custom_call_target="tpu_custom_call" | custom-call | flops 1000 | bytes 1000 | tf_op jit(solution)/shard_map/pallas_call | solution.py:569
  67.9 2.5 %shard_map.119 = (f32[3,8,16,512]{3,2,1,0:T(8,128)S(1)}, f32[3,8,16,512]{3,2,1,0:T(8,128)S(1)}, f32[24,640]{1,0:T(8,128)S(1)}, f32[24,640]{1,0:T(8,128)S(1)}, f32[24,128]{1,0:T(8,128)S(1)}) custom-call(f32[6]{0:T(128)S(1)} %copy-done.11, f32[3,8,16,512]{3,2,1,0:T(8,128)S(1)} %get-tuple-element.79.disp_ref.refs_1_.refs_2_, ...), custom_call_target="tpu_custom_call" | custom-call | flops 1000 | bytes 1000 | tf_op jit(solution)/shard_map/pallas_call | solution.py:585
  70.9 1.2 %collective-permute-start.19 = (f32[24,128]{1,0:T(8,128)S(1)}, f32[24,128]{1,0:T(8,128)S(1)}, u32[]{:S(2)}, u32[]{:S(2)}) collective-permute-start(f32[24,128]{1,0:T(8,128)S(1)} %get-tuple-element.93.own_ref.refs_1_), channel_id=1, source_target_pairs={{0,2},{1,3},{2,0},{3,1},{4,6},{5,7},{6,4},{7,5},{8,10},{9,11},{10,... | collective-permute-start | bytes 36872 | tf_op jit(solution)/shard_map/ppermute | solution.py:37
  72.1 2.2 %shard_map.120.refs_5_.refs_4_ = f32[3,8,16,512]{3,2,1,0:T(8,128)S(1)} custom-call(f32[3,8,16,512]{3,2,1,0:T(8,128)S(1)} %get-tuple-element.91.disp_ref.refs_1_.refs_2_, f32[2,8,16,512]{3,2,1,0:T(8,128)S(1)} %copy-done), custom_call_target="tpu_custom_call" | custom-call | flops 1000 | bytes 1000 | tf_op jit(solution)/shard_map/pallas_call | solution.py:522
  74.6 0.6 shard_map.121
  75.2 1.0 collective-permute-start.21
  76.2 4.1 %shard_map.122.refs_4_ = f32[8,4,8,128]{3,2,1,0:T(8,128)S(1)} custom-call(s32[32]{0:T(128)S(1)} %get-tuple-element.111.bins_ref.refs_0_, f32[24,128]{1,0:T(8,128)S(1)} %get-tuple-element.93.own_ref.refs_1_, f32[24,640]{1,0:T(8,128)S(1)} %collective-permute-done.20.refs_3_.lower_ref.refs_8_, f32[56,512]{1,0:T(8,128)S(1)} %get-tuple-element.97._), custom_call_target="tpu_custom_call" | custom-call | flops 1000 | bytes 1000 | tf_op jit(solution)/shard_map/pallas_call | solution.py:557
  80.5 0.9 collective-permute-start.22
  81.4 1.4 %collective-permute-start.23 = (f32[56,512]{1,0:T(8,128)S(1)}, f32[56,512]{1,0:T(8,128)S(1)}, u32[]{:S(2)}, u32[]{:S(2)}) collective-permute-start(f32[56,512]{1,0:T(8,128)S(1)} %collective-permute-done.21), channel_id=1, source_target_pairs={{0,8},{4,0},{8,16},{12,4},{16,24},{20,12},{24,28},{28,20},{1,9},{5... | collective-permute-start | bytes 344072 | tf_op jit(solution)/shard_map/ppermute | solution.py:32
  82.8 1.1 %shard_map.123.refs_8_ = s32[8,1024]{1,0:T(8,128)S(1)} custom-call(f32[6]{0:T(128)S(1)} %copy-done.11, s32[8,16,512]{2,1,0:T(8,128)S(1)} %copy-done.7, s32[8,128]{1,0:T(8,128)S(1)} %bitcast.30, bf16[512,1024]{1,0:T(8,128)(2,1)S(1)} %copy-done.2), custom_call_target="tpu_custom_call" | custom-call | flops 1000 | bytes 1000 | tf_op jit(solution)/shard_map/pallas_call | solution.py:512
  83.9 5.1 %shard_map.124 = (f32[384,512]{1,0:T(8,128)S(1)}, f32[8,256]{1,0:T(8,128)S(1)}) custom-call(s32[32]{0:T(128)S(1)} %get-tuple-element.111.bins_ref.refs_0_, f32[24,128]{1,0:T(8,128)S(1)} %get-tuple-element.93.own_ref.refs_1_, f32[24,640]{1,0:T(8,128)S(1)} %collective-permute-done.18.refs_4_.refs_2_.refs_9_, f32[1,24,128]{2,1,0:T(8,128)S(1)} %bitcast.35, ...), custom_call_target="tpu_custom_call" | custom-call | flops 1000 | bytes 1000 | tf_op jit(solution)/shard_map/pallas_call | solution.py:569
  89.1 0.7 collective-permute-start.24
  89.8 3.0 %collective-permute-done.24 = f32[2,256]{1,0:T(2,128)S(1)} collective-permute-done((f32[2,256]{1,0:T(2,128)S(1)}, f32[2,256]{1,0:T(2,128)S(1)}, u32[]{:S(2)}, u32[]{:S(2)}) %collective-permute-start.24) | collective-permute-done | bytes 2080 | tf_op jit(solution)/shard_map/ppermute | solution.py:25
  92.7 1.7 %collective-permute-start.25 = (f32[256]{0:T(256)S(1)}, f32[256]{0:T(256)S(1)}, u32[]{:S(2)}, u32[]{:S(2)}) collective-permute-start(f32[256]{0:T(256)S(1)} %bitcast.42), channel_id=1, source_target_pairs={{0,8},{4,0},{8,16},{12,4},{16,24},{20,12},{24,28},{28,20},{1,9},{5... | collective-permute-start | bytes 3080 | tf_op jit(solution)/shard_map/ppermute | solution.py:32
  94.4 2.7 %shard_map.125 = (f32[3,8,16,512]{3,2,1,0:T(8,128)}, f32[3,8,16,512]{3,2,1,0:T(8,128)}) custom-call(f32[6]{0:T(128)S(1)} %copy-done.11, f32[3,8,16,512]{3,2,1,0:T(8,128)S(1)} %get-tuple-element.91.disp_ref.refs_1_.refs_2_, f32[3,8,16,512]{3,2,1,0:T(8,128)S(1)} %get-tuple-element.92.refs_2_, f32[8,16,512]{2,1,0:T(8,128)S(1)} %copy-done.3, ...), custom_call_target="tpu_custom_call" | custom-call | flops 1000 | bytes 1000 | tf_op jit(solution)/shard_map/pallas_call | solution.py:585
  (64 shorter events, 5.4 us)
Async XLA Ops:
  0.6 8.7 %copy-start.1 = (f32[3,8,16,512]{3,2,1,0:T(8,128)S(1)}, f32[3,8,16,512]{3,2,1,0:T(8,128)}, u32[]{:S(2)}) copy-start(f32[3,8,16,512]{3,2,1,0:T(8,128)} %refs_1_.3) | copy-start | bytes 2359300
  1.4 8.0 %copy-start = (f32[2,8,16,512]{3,2,1,0:T(8,128)S(1)}, f32[2,8,16,512]{3,2,1,0:T(8,128)}, u32[]{:S(2)}) copy-start(f32[2,8,16,512]{3,2,1,0:T(8,128)} %moduli_ref.9) | copy-start | bytes 1572868
  4.6 7.5 %collective-permute-start = (f32[40,640]{1,0:T(8,128)}, f32[40,640]{1,0:T(8,128)S(1)}, u32[]{:S(2)}, u32[]{:S(2)}) collective-permute-start(f32[40,640]{1,0:T(8,128)} %get-tuple-element.57.refs_6_), channel_id=1, source_target_pairs={{0,1},{1,2},{2,3},{3,0},{4,5},{5,6},{6,7},{7,4},{8,9},{9,10},{10,1... | collective-permute-start | bytes 307208 | tf_op jit(solution)/shard_map/ppermute | solution.py:37
  5.1 7.1 %collective-permute-start.1 = (f32[32,640]{1,0:T(8,128)}, f32[32,640]{1,0:T(8,128)S(1)}, u32[]{:S(2)}, u32[]{:S(2)}) collective-permute-start(f32[32,640]{1,0:T(8,128)} %get-tuple-element.58.refs_7_), channel_id=1, source_target_pairs={{0,3},{1,0},{2,1},{3,2},{4,7},{5,4},{6,5},{7,6},{8,11},{9,8},{10,9... | collective-permute-start | bytes 245768 | tf_op jit(solution)/shard_map/ppermute | solution.py:37
  7.1 4.4 %copy-start.10 = (f32[32,128]{1,0:T(8,128)S(1)}, f32[32,128]{1,0:T(8,128)}, u32[]{:S(2)}) copy-start(f32[32,128]{1,0:T(8,128)} %get-tuple-element.56.own_ref.refs_1_) | copy-start | bytes 49156
  7.1 5.1 %collective-permute-start.2 = (f32[32,128]{1,0:T(8,128)}, f32[32,128]{1,0:T(8,128)S(1)}, u32[]{:S(2)}, u32[]{:S(2)}) collective-permute-start(f32[32,128]{1,0:T(8,128)} %get-tuple-element.56.own_ref.refs_1_), channel_id=1, source_target_pairs={{0,2},{1,3},{2,0},{3,1},{4,6},{5,7},{6,4},{7,5},{8,10},{9,11},{10,... | collective-permute-start | bytes 49160 | tf_op jit(solution)/shard_map/ppermute | solution.py:37
  12.1 0.6 copy-start.11
  13.3 6.2 %collective-permute-start.3 = (f32[88,512]{1,0:T(8,128)S(1)}, f32[88,512]{1,0:T(8,128)S(1)}, u32[]{:S(2)}, u32[]{:S(2)}) collective-permute-start(f32[88,512]{1,0:T(8,128)S(1)} %get-tuple-element.60._), channel_id=1, source_target_pairs={{0,4},{4,0},{8,12},{12,8},{16,20},{20,16},{24,28},{28,24},{1,5},{5... | collective-permute-start | bytes 540680 | tf_op jit(solution)/shard_map/ppermute | solution.py:25
  15.0 7.6 %copy-start.5 = (s32[1024]{0:T(1024)S(1)}, s32[1024]{0:T(1024)}, u32[]{:S(2)}) copy-start(s32[1024]{0:T(1024)} %param.12) | copy-start | bytes 12292
  19.5 9.1 %copy-start.2 = (bf16[512,1024]{1,0:T(8,128)(2,1)S(1)}, bf16[512,1024]{1,0:T(8,128)(2,1)}, u32[]{:S(2)}) copy-start(bf16[512,1024]{1,0:T(8,128)(2,1)} %get-tuple-element.65.refs_15_.hot_ref) | copy-start | bytes 3145732
  19.5 8.5 %collective-permute-start.4 = (f32[88,512]{1,0:T(8,128)S(1)}, f32[88,512]{1,0:T(8,128)S(1)}, u32[]{:S(2)}, u32[]{:S(2)}) collective-permute-start(f32[88,512]{1,0:T(8,128)S(1)} %get-tuple-element.63), channel_id=1, source_target_pairs={{0,4},{4,0},{8,12},{12,8},{16,20},{20,16},{24,28},{28,24},{1,5},{5... | collective-permute-start | bytes 540680 | tf_op jit(solution)/shard_map/ppermute | solution.py:25
  21.0 7.6 %collective-permute-start.5 = (f32[88,512]{1,0:T(8,128)S(1)}, f32[88,512]{1,0:T(8,128)S(1)}, u32[]{:S(2)}, u32[]{:S(2)}) collective-permute-start(f32[88,512]{1,0:T(8,128)S(1)} %collective-permute-done.3), channel_id=1, source_target_pairs={{0,8},{4,0},{8,16},{12,4},{16,24},{20,12},{24,28},{28,20},{1,9},{5... | collective-permute-start | bytes 540680 | tf_op jit(solution)/shard_map/ppermute | solution.py:32
  22.9 5.6 %copy-start.4 = (f32[3,8,16,512]{3,2,1,0:T(8,128)S(1)}, f32[3,8,16,512]{3,2,1,0:T(8,128)}, u32[]{:S(2)}) copy-start(f32[3,8,16,512]{3,2,1,0:T(8,128)} %refs_2_.3) | copy-start | bytes 2359300
  22.9 5.6 %copy-start.3 = (f32[8,16,512]{2,1,0:T(8,128)S(1)}, f32[8,16,512]{2,1,0:T(8,128)}, u32[]{:S(2)}) copy-start(f32[8,16,512]{2,1,0:T(8,128)} %refs_3_.7) | copy-start | bytes 786436
  22.9 5.6 %copy-start.6 = (f32[3,1024]{1,0:T(4,128)S(1)}, f32[3,1024]{1,0:T(4,128)}, u32[]{:S(2)}) copy-start(f32[3,1024]{1,0:T(4,128)} %refs_13_.5) | copy-start | bytes 36868
  22.9 5.6 %copy-start.8 = (f32[40,640]{1,0:T(8,128)S(1)}, f32[40,640]{1,0:T(8,128)}, u32[]{:S(2)}) copy-start(f32[40,640]{1,0:T(8,128)} %get-tuple-element.57.refs_6_) | copy-start | bytes 307204
  23.0 5.6 %copy-start.9 = (f32[32,640]{1,0:T(8,128)S(1)}, f32[32,640]{1,0:T(8,128)}, u32[]{:S(2)}) copy-start(f32[32,640]{1,0:T(8,128)} %get-tuple-element.58.refs_7_) | copy-start | bytes 245764
  31.1 4.4 %collective-permute-start.6 = (f32[24,640]{1,0:T(8,128)S(1)}, f32[24,640]{1,0:T(8,128)S(1)}, u32[]{:S(2)}, u32[]{:S(2)}) collective-permute-start(f32[24,640]{1,0:T(8,128)S(1)} %get-tuple-element.69.refs_7_), channel_id=1, source_target_pairs={{0,3},{1,0},{2,1},{3,2},{4,7},{5,4},{6,5},{7,6},{8,11},{9,8},{10,9... | collective-permute-start | bytes 184328 | tf_op jit(solution)/shard_map/ppermute | solution.py:37
  31.1 4.3 %collective-permute-start.8 = (f32[24,640]{1,0:T(8,128)S(1)}, f32[24,640]{1,0:T(8,128)S(1)}, u32[]{:S(2)}, u32[]{:S(2)}) collective-permute-start(f32[24,640]{1,0:T(8,128)S(1)} %get-tuple-element.70.refs_6_), channel_id=1, source_target_pairs={{0,1},{1,2},{2,3},{3,0},{4,5},{5,6},{6,7},{7,4},{8,9},{9,10},{10,1... | collective-permute-start | bytes 184328 | tf_op jit(solution)/shard_map/ppermute | solution.py:37
  31.6 3.8 %collective-permute-start.7 = (f32[24,128]{1,0:T(8,128)S(1)}, f32[24,128]{1,0:T(8,128)S(1)}, u32[]{:S(2)}, u32[]{:S(2)}) collective-permute-start(f32[24,128]{1,0:T(8,128)S(1)} %get-tuple-element.68.own_ref.refs_1_), channel_id=1, source_target_pairs={{0,2},{1,3},{2,0},{3,1},{4,6},{5,7},{6,4},{7,5},{8,10},{9,11},{10,... | collective-permute-start | bytes 36872 | tf_op jit(solution)/shard_map/ppermute | solution.py:37
  36.0 5.2 %collective-permute-start.9 = (f32[56,512]{1,0:T(8,128)S(1)}, f32[56,512]{1,0:T(8,128)S(1)}, u32[]{:S(2)}, u32[]{:S(2)}) collective-permute-start(f32[56,512]{1,0:T(8,128)S(1)} %get-tuple-element.72._), channel_id=1, source_target_pairs={{0,4},{4,0},{8,12},{12,8},{16,20},{20,16},{24,28},{28,24},{1,5},{5... | collective-permute-start | bytes 344072 | tf_op jit(solution)/shard_map/ppermute | solution.py:25
  41.3 5.7 %collective-permute-start.10 = (f32[56,512]{1,0:T(8,128)S(1)}, f32[56,512]{1,0:T(8,128)S(1)}, u32[]{:S(2)}, u32[]{:S(2)}) collective-permute-start(f32[56,512]{1,0:T(8,128)S(1)} %get-tuple-element.76), channel_id=1, source_target_pairs={{0,4},{4,0},{8,12},{12,8},{16,20},{20,16},{24,28},{28,24},{1,5},{5... | collective-permute-start | bytes 344072 | tf_op jit(solution)/shard_map/ppermute | solution.py:25
  41.8 6.2 %collective-permute-start.11 = (f32[56,512]{1,0:T(8,128)S(1)}, f32[56,512]{1,0:T(8,128)S(1)}, u32[]{:S(2)}, u32[]{:S(2)}) collective-permute-start(f32[56,512]{1,0:T(8,128)S(1)} %collective-permute-done.9), channel_id=1, source_target_pairs={{0,8},{4,0},{8,16},{12,4},{16,24},{20,12},{24,28},{28,20},{1,9},{5... | collective-permute-start | bytes 344072 | tf_op jit(solution)/shard_map/ppermute | solution.py:32
  50.5 4.3 %collective-permute-start.12 = (f32[24,640]{1,0:T(8,128)S(1)}, f32[24,640]{1,0:T(8,128)S(1)}, u32[]{:S(2)}, u32[]{:S(2)}) collective-permute-start(f32[24,640]{1,0:T(8,128)S(1)} %get-tuple-element.82.refs_7_), channel_id=1, source_target_pairs={{0,3},{1,0},{2,1},{3,2},{4,7},{5,4},{6,5},{7,6},{8,11},{9,8},{10,9... | collective-permute-start | bytes 184328 | tf_op jit(solution)/shard_map/ppermute | solution.py:37
  50.6 4.2 %collective-permute-start.14 = (f32[24,640]{1,0:T(8,128)S(1)}, f32[24,640]{1,0:T(8,128)S(1)}, u32[]{:S(2)}, u32[]{:S(2)}) collective-permute-start(f32[24,640]{1,0:T(8,128)S(1)} %get-tuple-element.83.refs_6_), channel_id=1, source_target_pairs={{0,1},{1,2},{2,3},{3,0},{4,5},{5,6},{6,7},{7,4},{8,9},{9,10},{10,1... | collective-permute-start | bytes 184328 | tf_op jit(solution)/shard_map/ppermute | solution.py:37
  51.1 3.7 %collective-permute-start.13 = (f32[24,128]{1,0:T(8,128)S(1)}, f32[24,128]{1,0:T(8,128)S(1)}, u32[]{:S(2)}, u32[]{:S(2)}) collective-permute-start(f32[24,128]{1,0:T(8,128)S(1)} %get-tuple-element.81.own_ref.refs_1_), channel_id=1, source_target_pairs={{0,2},{1,3},{2,0},{3,1},{4,6},{5,7},{6,4},{7,5},{8,10},{9,11},{10,... | collective-permute-start | bytes 36872 | tf_op jit(solution)/shard_map/ppermute | solution.py:37
  55.4 5.0 %collective-permute-start.15 = (f32[56,512]{1,0:T(8,128)S(1)}, f32[56,512]{1,0:T(8,128)S(1)}, u32[]{:S(2)}, u32[]{:S(2)}) collective-permute-start(f32[56,512]{1,0:T(8,128)S(1)} %get-tuple-element.85._), channel_id=1, source_target_pairs={{0,4},{4,0},{8,12},{12,8},{16,20},{20,16},{24,28},{28,24},{1,5},{5... | collective-permute-start | bytes 344072 | tf_op jit(solution)/shard_map/ppermute | solution.py:25
  60.4 7.5 %collective-permute-start.16 = (f32[56,512]{1,0:T(8,128)S(1)}, f32[56,512]{1,0:T(8,128)S(1)}, u32[]{:S(2)}, u32[]{:S(2)}) collective-permute-start(f32[56,512]{1,0:T(8,128)S(1)} %get-tuple-element.89), channel_id=1, source_target_pairs={{0,4},{4,0},{8,12},{12,8},{16,20},{20,16},{24,28},{28,24},{1,5},{5... | collective-permute-start | bytes 344072 | tf_op jit(solution)/shard_map/ppermute | solution.py:25
  61.6 6.3 %collective-permute-start.17 = (f32[56,512]{1,0:T(8,128)S(1)}, f32[56,512]{1,0:T(8,128)S(1)}, u32[]{:S(2)}, u32[]{:S(2)}) collective-permute-start(f32[56,512]{1,0:T(8,128)S(1)} %collective-permute-done.15), channel_id=1, source_target_pairs={{0,8},{4,0},{8,16},{12,4},{16,24},{20,12},{24,28},{28,20},{1,9},{5... | collective-permute-start | bytes 344072 | tf_op jit(solution)/shard_map/ppermute | solution.py:32
  70.4 4.3 %collective-permute-start.18 = (f32[24,640]{1,0:T(8,128)S(1)}, f32[24,640]{1,0:T(8,128)S(1)}, u32[]{:S(2)}, u32[]{:S(2)}) collective-permute-start(f32[24,640]{1,0:T(8,128)S(1)} %get-tuple-element.94.refs_7_), channel_id=1, source_target_pairs={{0,3},{1,0},{2,1},{3,2},{4,7},{5,4},{6,5},{7,6},{8,11},{9,8},{10,9... | collective-permute-start | bytes 184328 | tf_op jit(solution)/shard_map/ppermute | solution.py:37
  70.4 4.2 %collective-permute-start.20 = (f32[24,640]{1,0:T(8,128)S(1)}, f32[24,640]{1,0:T(8,128)S(1)}, u32[]{:S(2)}, u32[]{:S(2)}) collective-permute-start(f32[24,640]{1,0:T(8,128)S(1)} %get-tuple-element.95.refs_6_), channel_id=1, source_target_pairs={{0,1},{1,2},{2,3},{3,0},{4,5},{5,6},{6,7},{7,4},{8,9},{9,10},{10,1... | collective-permute-start | bytes 184328 | tf_op jit(solution)/shard_map/ppermute | solution.py:37
  70.9 3.7 %collective-permute-start.19 = (f32[24,128]{1,0:T(8,128)S(1)}, f32[24,128]{1,0:T(8,128)S(1)}, u32[]{:S(2)}, u32[]{:S(2)}) collective-permute-start(f32[24,128]{1,0:T(8,128)S(1)} %get-tuple-element.93.own_ref.refs_1_), channel_id=1, source_target_pairs={{0,2},{1,3},{2,0},{3,1},{4,6},{5,7},{6,4},{7,5},{8,10},{9,11},{10,... | collective-permute-start | bytes 36872 | tf_op jit(solution)/shard_map/ppermute | solution.py:37
  75.2 7.6 %copy-start.7 = (s32[8,16,512]{2,1,0:T(8,128)S(1)}, s32[8,16,512]{2,1,0:T(8,128)}, u32[]{:S(2)}) copy-start(s32[8,16,512]{2,1,0:T(8,128)} %tiles_ref.1) | copy-start | bytes 786436
  75.2 5.2 %collective-permute-start.21 = (f32[56,512]{1,0:T(8,128)S(1)}, f32[56,512]{1,0:T(8,128)S(1)}, u32[]{:S(2)}, u32[]{:S(2)}) collective-permute-start(f32[56,512]{1,0:T(8,128)S(1)} %get-tuple-element.97._), channel_id=1, source_target_pairs={{0,4},{4,0},{8,12},{12,8},{16,20},{20,16},{24,28},{28,24},{1,5},{5... | collective-permute-start | bytes 344072 | tf_op jit(solution)/shard_map/ppermute | solution.py:25
  80.5 8.6 %collective-permute-start.22 = (f32[56,512]{1,0:T(8,128)S(1)}, f32[56,512]{1,0:T(8,128)S(1)}, u32[]{:S(2)}, u32[]{:S(2)}) collective-permute-start(f32[56,512]{1,0:T(8,128)S(1)} %get-tuple-element.102), channel_id=1, source_target_pairs={{0,4},{4,0},{8,12},{12,8},{16,20},{20,16},{24,28},{28,24},{1,5},{5... | collective-permute-start | bytes 344072 | tf_op jit(solution)/shard_map/ppermute | solution.py:25
  81.4 7.6 %collective-permute-start.23 = (f32[56,512]{1,0:T(8,128)S(1)}, f32[56,512]{1,0:T(8,128)S(1)}, u32[]{:S(2)}, u32[]{:S(2)}) collective-permute-start(f32[56,512]{1,0:T(8,128)S(1)} %collective-permute-done.21), channel_id=1, source_target_pairs={{0,8},{4,0},{8,16},{12,4},{16,24},{20,12},{24,28},{28,20},{1,9},{5... | collective-permute-start | bytes 344072 | tf_op jit(solution)/shard_map/ppermute | solution.py:32
  89.1 3.7 %collective-permute-start.24 = (f32[2,256]{1,0:T(2,128)S(1)}, f32[2,256]{1,0:T(2,128)S(1)}, u32[]{:S(2)}, u32[]{:S(2)}) collective-permute-start(f32[2,256]{1,0:T(2,128)S(1)} %slice.49), channel_id=1, source_target_pairs={{0,4},{4,0},{8,12},{12,8},{16,20},{20,16},{24,28},{28,24},{1,5},{5... | collective-permute-start | bytes 6152 | tf_op jit(solution)/shard_map/ppermute | solution.py:25
  92.7 4.4 %collective-permute-start.25 = (f32[256]{0:T(256)S(1)}, f32[256]{0:T(256)S(1)}, u32[]{:S(2)}, u32[]{:S(2)}) collective-permute-start(f32[256]{0:T(256)S(1)} %bitcast.42), channel_id=1, source_target_pairs={{0,8},{4,0},{8,16},{12,4},{16,24},{20,12},{24,28},{28,20},{1,9},{5... | collective-permute-start | bytes 3080 | tf_op jit(solution)/shard_map/ppermute | solution.py:32

commit v3 on v2

--- a/solution.py
+++ b/solution.py
@@ -561,8 +561,8 @@
             [SCALARS, WHOLE, WHOLE, pl.BlockSpec(memory_space=pl.ANY)],
         )(all_bins[step], far, lower, to_odd)
         to_even, sums, relay = lax.optimization_barrier((to_even, sums, relay))
+        of_even = swapped(to_even, "dom")
         of_odd = relayed(relay, "dom")
-        of_even = swapped(to_even, "dom")
         pair_args = [all_bins[step], far, upper, others, sums, node, turned, heat]
         if last:
             pair_args += [tile_places, flags]
@@ -594,6 +594,7 @@
         if first:
             rim = made[-1]
     got = swapped(heat[1:3], "dom")
+    got, velocity = lax.optimization_barrier((got, velocity))
     passed = relayed(got[1], "dom")
     tile_heat = heat[0] + got[0] + passed
     return displacement, velocity, tile_heat

time: 98.4 us -> 97.9 us (level)
    ppermute x5, waiting for transfers between devices: 1.62 us -> 3.79 us  [relayed(): return lax.ppermute(value, axis, list(enumerate(target)))]
    ppermute x9, waiting for transfers between devices: 6.17 us -> 4.31 us  [swapped(): return lax.ppermute(value, axis, [(i, i ^ 1) for i in range(count)])]
  transfers between devices with their start and end apart: 26 -> 26, of which waited for: 11 -> 11; matrix products, arithmetic and copies ran while one was open for 0% -> 0% of each run, Pallas kernels for 49% -> 48%
where the time goes in v3:
time: 97.9 us; the launch traced here: 97.7 us
  Pallas kernels  60 us (61%)
  starting transfers between devices  24.5 us (25%)
  waiting for transfers between devices  10.1 us (10%)
  other arithmetic  1.25 us (1%)
  between operations  1.03 us (1%)
    pallas_call x4, Pallas kernels, per_device(): call(functools.partial(rest_body, bin_count, last), [struct(3 * extent_x...  19.3 us
    pallas_call x4, Pallas kernels, per_device(): call(functools.partial(near_body, bin_count), [struct(blocks, 4, 8, SEG)]...  14.9 us
    pallas_call x4, Pallas kernels, per_device(): call(functools.partial(update_body, first, last), update_outs, [pltpu.VME...  10.2 us
    ppermute x12, starting transfers between devices, cycled(): lax.ppermute(value, axis, [(source, (source + steps) % count) for source...  9.52 us
    pallas_call x4, Pallas kernels, per_device(): call(inner_body, [struct(*shape)], [pltpu.VMEM((extent_x, 9, extent_y, ex...  8.68 us
    ppermute x5, starting transfers between devices, relayed(): return lax.ppermute(value, axis, list(enumerate(target)))  7.58 us
    ppermute x9, starting transfers between devices, swapped(): return lax.ppermute(value, axis, [(i, i ^ 1) for i in range(count)])  7.42 us
    ppermute x9, waiting for transfers between devices, swapped(): return lax.ppermute(value, axis, [(i, i ^ 1) for i in range(count)])  4.31 us
  transfers between devices with their start and end apart: 26, of which 11 were waited for; matrix products, arithmetic and copies ran while one was open for 0% of the time, Pallas kernels for 48%

profile of v3, /device:TPU:0, one launch (start us, length us, event | category | flops | bytes accessed | tf_op | source)
XLA Modules:
  0.0 97.7 jit_solution(13476344489369475577)
XLA Ops:
  0.8 0.6 pad_maximum_fusion._.refs_0_.own_ref.refs_9_
  1.4 3.2 %shard_map.104 = (f32[40,640]{1,0:T(8,128)}, f32[32,640]{1,0:T(8,128)}, f32[32,128]{1,0:T(8,128)}, bf16[512,1024]{1,0:T(8,128)(2,1)}) custom-call(f32[6]{0:T(128)} %pad_maximum_fusion._.refs_0_.own_ref.refs_9_, f32[3,8,16,512]{3,2,1,0:T(8,128)} %refs_1_.3, f32[3,1024]{1,0:T(4,128)} %refs_13_.5, s32[8,128]{1,0:T(8,128)} %bitcast.22, ...), custom_call_target="tpu_custom_call" | custom-call | flops 1000 | bytes 1000 | tf_op jit(solution)/shard_map/pallas_call | solution.py:498
  5.1 2.0 %collective-permute-start.1 = (f32[32,640]{1,0:T(8,128)}, f32[32,640]{1,0:T(8,128)S(1)}, u32[]{:S(2)}, u32[]{:S(2)}) collective-permute-start(f32[32,640]{1,0:T(8,128)} %get-tuple-element.60.refs_7_), channel_id=1, source_target_pairs={{0,3},{1,0},{2,1},{3,2},{4,7},{5,4},{6,5},{7,6},{8,11},{9,8},{10,9... | collective-permute-start | bytes 245768 | tf_op jit(solution)/shard_map/ppermute | solution.py:37
  7.1 2.3 %collective-permute-start.2 = (f32[32,128]{1,0:T(8,128)}, f32[32,128]{1,0:T(8,128)S(1)}, u32[]{:S(2)}, u32[]{:S(2)}) collective-permute-start(f32[32,128]{1,0:T(8,128)} %get-tuple-element.58.own_ref.refs_1_), channel_id=1, source_target_pairs={{0,2},{1,3},{2,0},{3,1},{4,6},{5,7},{6,4},{7,5},{8,10},{9,11},{10,... | collective-permute-start | bytes 49160 | tf_op jit(solution)/shard_map/ppermute | solution.py:37
  9.3 2.2 %shard_map.103.refs_5_.refs_4_ = f32[3,8,16,512]{3,2,1,0:T(8,128)S(1)} custom-call(f32[3,8,16,512]{3,2,1,0:T(8,128)S(1)} %copy-done.1, f32[2,8,16,512]{3,2,1,0:T(8,128)S(1)} %copy-done), custom_call_target="tpu_custom_call" | custom-call | flops 1000 | bytes 1000 | tf_op jit(solution)/shard_map/pallas_call | solution.py:522
  11.5 0.6 collective-permute-done.2
  12.1 0.6 copy-done.11
  12.7 0.6 shard_map.105
  13.3 1.6 %collective-permute-start.3 = (f32[88,512]{1,0:T(8,128)S(1)}, f32[88,512]{1,0:T(8,128)S(1)}, u32[]{:S(2)}, u32[]{:S(2)}) collective-permute-start(f32[88,512]{1,0:T(8,128)S(1)} %get-tuple-element.62._), channel_id=1, source_target_pairs={{0,4},{4,0},{8,12},{12,8},{16,20},{20,16},{24,28},{28,24},{1,5},{5... | collective-permute-start | bytes 540680 | tf_op jit(solution)/shard_map/ppermute | solution.py:25
  15.0 3.6 %shard_map.106.refs_4_ = f32[8,4,8,128]{3,2,1,0:T(8,128)S(1)} custom-call(s32[32]{0:T(128)S(1)} %get-tuple-element.118.bins_ref.refs_0_, f32[32,128]{1,0:T(8,128)S(1)} %copy-done.10, f32[40,640]{1,0:T(8,128)S(1)} %collective-permute-done.refs_3_.lower_ref.refs_8_, f32[88,512]{1,0:T(8,128)S(1)} %get-tuple-element.62._), custom_call_target="tpu_custom_call" | custom-call | flops 1000 | bytes 1000 | tf_op jit(solution)/shard_map/pallas_call | solution.py:557
  18.6 0.9 collective-permute-done.3
  19.5 1.5 %collective-permute-start.4 = (f32[88,512]{1,0:T(8,128)S(1)}, f32[88,512]{1,0:T(8,128)S(1)}, u32[]{:S(2)}, u32[]{:S(2)}) collective-permute-start(f32[88,512]{1,0:T(8,128)S(1)} %get-tuple-element.65), channel_id=1, source_target_pairs={{0,4},{4,0},{8,12},{12,8},{16,20},{20,16},{24,28},{28,24},{1,5},{5... | collective-permute-start | bytes 540680 | tf_op jit(solution)/shard_map/ppermute | solution.py:25
  21.0 1.6 %collective-permute-start.5 = (f32[88,512]{1,0:T(8,128)S(1)}, f32[88,512]{1,0:T(8,128)S(1)}, u32[]{:S(2)}, u32[]{:S(2)}) collective-permute-start(f32[88,512]{1,0:T(8,128)S(1)} %collective-permute-done.3), channel_id=1, source_target_pairs={{0,8},{4,0},{8,16},{12,4},{16,24},{20,12},{24,28},{28,20},{1,9},{5... | collective-permute-start | bytes 540680 | tf_op jit(solution)/shard_map/ppermute | solution.py:32
  23.0 4.6 %shard_map.108 = (f32[384,512]{1,0:T(8,128)S(1)}, f32[8,128]{1,0:T(8,128)S(1)}) custom-call(s32[32]{0:T(128)S(1)} %get-tuple-element.118.bins_ref.refs_0_, f32[32,128]{1,0:T(8,128)S(1)} %copy-done.10, f32[32,640]{1,0:T(8,128)S(1)} %collective-permute-done.1.refs_4_.refs_2_.refs_9_, f32[1,32,128]{2,1,0:T(8,128)S(1)} %bitcast.33, ...), custom_call_target="tpu_custom_call" | custom-call | flops 1000 | bytes 1000 | tf_op jit(solution)/shard_map/pallas_call | solution.py:569
  27.6 0.9 collective-permute-done.5.refs_11_
  28.6 2.5 %shard_map.109 = (f32[3,8,16,512]{3,2,1,0:T(8,128)S(1)}, f32[3,8,16,512]{3,2,1,0:T(8,128)S(1)}, f32[24,640]{1,0:T(8,128)S(1)}, f32[24,640]{1,0:T(8,128)S(1)}, f3...) custom-call(f32[6]{0:T(128)S(1)} %copy-done.11, f32[3,8,16,512]{3,2,1,0:T(8,128)S(1)} %copy-done.1, ...), custom_call_target="tpu_custom_call" | custom-call | flops 1000 | bytes 1000 | tf_op jit(solution)/shard_map/pallas_call | solution.py:585
  31.6 1.0 %collective-permute-start.7 = (f32[24,128]{1,0:T(8,128)S(1)}, f32[24,128]{1,0:T(8,128)S(1)}, u32[]{:S(2)}, u32[]{:S(2)}) collective-permute-start(f32[24,128]{1,0:T(8,128)S(1)} %get-tuple-element.70.own_ref.refs_1_), channel_id=1, source_target_pairs={{0,2},{1,3},{2,0},{3,1},{4,6},{5,7},{6,4},{7,5},{8,10},{9,11},{10,... | collective-permute-start | bytes 36872 | tf_op jit(solution)/shard_map/ppermute | solution.py:37
  32.7 2.2 %shard_map.110.refs_5_.refs_4_ = f32[3,8,16,512]{3,2,1,0:T(8,128)S(1)} custom-call(f32[3,8,16,512]{3,2,1,0:T(8,128)S(1)} %get-tuple-element.68.disp_ref.refs_1_.refs_2_, f32[2,8,16,512]{3,2,1,0:T(8,128)S(1)} %copy-done), custom_call_target="tpu_custom_call" | custom-call | flops 1000 | bytes 1000 | tf_op jit(solution)/shard_map/pallas_call | solution.py:522
  35.3 0.6 shard_map.111
  36.0 3.6 %shard_map.112.refs_4_ = f32[8,4,8,128]{3,2,1,0:T(8,128)S(1)} custom-call(s32[32]{0:T(128)S(1)} %get-tuple-element.117.bins_ref.refs_0_, f32[24,128]{1,0:T(8,128)S(1)} %get-tuple-element.70.own_ref.refs_1_, f32[24,640]{1,0:T(8,128)S(1)} %collective-permute-done.8.refs_3_.lower_ref.refs_8_, f32[56,512]{1,0:T(8,128)S(1)} %get-tuple-element.74._), custom_call_target="tpu_custom_call" | custom-call | flops 1000 | bytes 1000 | tf_op jit(solution)/shard_map/pallas_call | solution.py:557
  39.6 1.4 %collective-permute-done.9 = f32[56,512]{1,0:T(8,128)S(1)} collective-permute-done((f32[56,512]{1,0:T(8,128)S(1)}, f32[56,512]{1,0:T(8,128)S(1)}, u32[]{:S(2)}, u32[]{:S(2)}) %collective-permute-start.9) | collective-permute-done | bytes 114720 | tf_op jit(solution)/shard_map/ppermute | solution.py:25
  41.0 1.0 %collective-permute-start.10 = (f32[56,512]{1,0:T(8,128)S(1)}, f32[56,512]{1,0:T(8,128)S(1)}, u32[]{:S(2)}, u32[]{:S(2)}) collective-permute-start(f32[56,512]{1,0:T(8,128)S(1)} %get-tuple-element.78), channel_id=1, source_target_pairs={{0,4},{4,0},{8,12},{12,8},{16,20},{20,16},{24,28},{28,24},{1,5},{5... | collective-permute-start | bytes 344072 | tf_op jit(solution)/shard_map/ppermute | solution.py:25
  42.0 1.0 %collective-permute-start.11 = (f32[56,512]{1,0:T(8,128)S(1)}, f32[56,512]{1,0:T(8,128)S(1)}, u32[]{:S(2)}, u32[]{:S(2)}) collective-permute-start(f32[56,512]{1,0:T(8,128)S(1)} %collective-permute-done.9), channel_id=1, source_target_pairs={{0,8},{4,0},{8,16},{12,4},{16,24},{20,12},{24,28},{28,20},{1,9},{5... | collective-permute-start | bytes 344072 | tf_op jit(solution)/shard_map/ppermute | solution.py:32
  43.0 5.0 %shard_map.113 = (f32[384,512]{1,0:T(8,128)S(1)}, f32[8,128]{1,0:T(8,128)S(1)}) custom-call(s32[32]{0:T(128)S(1)} %get-tuple-element.117.bins_ref.refs_0_, f32[24,128]{1,0:T(8,128)S(1)} %get-tuple-element.70.own_ref.refs_1_, f32[24,640]{1,0:T(8,128)S(1)} %collective-permute-done.6.refs_4_.refs_2_.refs_9_, f32[1,24,128]{2,1,0:T(8,128)S(1)} %bitcast.37, ...), custom_call_target="tpu_custom_call" | custom-call | flops 1000 | bytes 1000 | tf_op jit(solution)/shard_map/pallas_call | solution.py:569
  48.0 2.5 %shard_map.114 = (f32[3,8,16,512]{3,2,1,0:T(8,128)S(1)}, f32[3,8,16,512]{3,2,1,0:T(8,128)S(1)}, f32[24,640]{1,0:T(8,128)S(1)}, f32[24,640]{1,0:T(8,128)S(1)}, f32[24,128]{1,0:T(8,128)S(1)}) custom-call(f32[6]{0:T(128)S(1)} %copy-done.11, f32[3,8,16,512]{3,2,1,0:T(8,128)S(1)} %get-tuple-element.68.disp_ref.refs_1_.refs_2_, ...), custom_call_target="tpu_custom_call" | custom-call | flops 1000 | bytes 1000 | tf_op jit(solution)/shard_map/pallas_call | solution.py:585
  51.1 0.9 collective-permute-start.13
  52.0 2.2 %shard_map.115.refs_5_.refs_4_ = f32[3,8,16,512]{3,2,1,0:T(8,128)S(1)} custom-call(f32[3,8,16,512]{3,2,1,0:T(8,128)S(1)} %get-tuple-element.81.disp_ref.refs_1_.refs_2_, f32[2,8,16,512]{3,2,1,0:T(8,128)S(1)} %copy-done), custom_call_target="tpu_custom_call" | custom-call | flops 1000 | bytes 1000 | tf_op jit(solution)/shard_map/pallas_call | solution.py:522
  54.1 0.6 collective-permute-done.13
  54.8 0.6 shard_map.116
  55.4 0.7 collective-permute-start.15
  56.1 4.1 %shard_map.117.refs_4_ = f32[8,4,8,128]{3,2,1,0:T(8,128)S(1)} custom-call(s32[32]{0:T(128)S(1)} %get-tuple-element.116.bins_ref.refs_0_, f32[24,128]{1,0:T(8,128)S(1)} %get-tuple-element.83.own_ref.refs_1_, f32[24,640]{1,0:T(8,128)S(1)} %collective-permute-done.14.refs_3_.lower_ref.refs_8_, f32[56,512]{1,0:T(8,128)S(1)} %get-tuple-element.87._), custom_call_target="tpu_custom_call" | custom-call | flops 1000 | bytes 1000 | tf_op jit(solution)/shard_map/pallas_call | solution.py:557
  60.4 0.7 collective-permute-start.16
  61.1 1.4 %collective-permute-start.17 = (f32[56,512]{1,0:T(8,128)S(1)}, f32[56,512]{1,0:T(8,128)S(1)}, u32[]{:S(2)}, u32[]{:S(2)}) collective-permute-start(f32[56,512]{1,0:T(8,128)S(1)} %collective-permute-done.15), channel_id=1, source_target_pairs={{0,8},{4,0},{8,16},{12,4},{16,24},{20,12},{24,28},{28,20},{1,9},{5... | collective-permute-start | bytes 344072 | tf_op jit(solution)/shard_map/ppermute | solution.py:32
  62.5 4.7 %shard_map.118 = (f32[384,512]{1,0:T(8,128)S(1)}, f32[8,128]{1,0:T(8,128)S(1)}) custom-call(s32[32]{0:T(128)S(1)} %get-tuple-element.116.bins_ref.refs_0_, f32[24,128]{1,0:T(8,128)S(1)} %get-tuple-element.83.own_ref.refs_1_, f32[24,640]{1,0:T(8,128)S(1)} %collective-permute-done.12.refs_4_.refs_2_.refs_9_, f32[1,24,128]{2,1,0:T(8,128)S(1)} %bitcast.39, ...), custom_call_target="tpu_custom_call" | custom-call | flops 1000 | bytes 1000 | tf_op jit(solution)/shard_map/pallas_call | solution.py:569
  67.2 2.5 %shard_map.119 = (f32[3,8,16,512]{3,2,1,0:T(8,128)S(1)}, f32[3,8,16,512]{3,2,1,0:T(8,128)S(1)}, f32[24,640]{1,0:T(8,128)S(1)}, f32[24,640]{1,0:T(8,128)S(1)}, f32[24,128]{1,0:T(8,128)S(1)}) custom-call(f32[6]{0:T(128)S(1)} %copy-done.11, f32[3,8,16,512]{3,2,1,0:T(8,128)S(1)} %get-tuple-element.81.disp_ref.refs_1_.refs_2_, ...), custom_call_target="tpu_custom_call" | custom-call | flops 1000 | bytes 1000 | tf_op jit(solution)/shard_map/pallas_call | solution.py:585
  70.3 1.2 %collective-permute-start.19 = (f32[24,128]{1,0:T(8,128)S(1)}, f32[24,128]{1,0:T(8,128)S(1)}, u32[]{:S(2)}, u32[]{:S(2)}) collective-permute-start(f32[24,128]{1,0:T(8,128)S(1)} %get-tuple-element.95.own_ref.refs_1_), channel_id=1, source_target_pairs={{0,2},{1,3},{2,0},{3,1},{4,6},{5,7},{6,4},{7,5},{8,10},{9,11},{10,... | collective-permute-start | bytes 36872 | tf_op jit(solution)/shard_map/ppermute | solution.py:37
  71.5 2.2 %shard_map.120.refs_5_.refs_4_ = f32[3,8,16,512]{3,2,1,0:T(8,128)S(1)} custom-call(f32[3,8,16,512]{3,2,1,0:T(8,128)S(1)} %get-tuple-element.93.disp_ref.refs_1_.refs_2_, f32[2,8,16,512]{3,2,1,0:T(8,128)S(1)} %copy-done), custom_call_target="tpu_custom_call" | custom-call | flops 1000 | bytes 1000 | tf_op jit(solution)/shard_map/pallas_call | solution.py:522
  74.6 0.7 collective-permute-start.21
  75.3 3.6 %shard_map.122.refs_4_ = f32[8,4,8,128]{3,2,1,0:T(8,128)S(1)} custom-call(s32[32]{0:T(128)S(1)} %get-tuple-element.115.bins_ref.refs_0_, f32[24,128]{1,0:T(8,128)S(1)} %get-tuple-element.95.own_ref.refs_1_, f32[24,640]{1,0:T(8,128)S(1)} %collective-permute-done.20.refs_3_.lower_ref.refs_8_, f32[56,512]{1,0:T(8,128)S(1)} %get-tuple-element.99._), custom_call_target="tpu_custom_call" | custom-call | flops 1000 | bytes 1000 | tf_op jit(solution)/shard_map/pallas_call | solution.py:557
  78.8 1.0 %collective-permute-done.21 = f32[56,512]{1,0:T(8,128)S(1)} collective-permute-done((f32[56,512]{1,0:T(8,128)S(1)}, f32[56,512]{1,0:T(8,128)S(1)}, u32[]{:S(2)}, u32[]{:S(2)}) %collective-permute-start.21) | collective-permute-done | bytes 114720 | tf_op jit(solution)/shard_map/ppermute | solution.py:25
  79.8 1.0 %collective-permute-start.22 = (f32[56,512]{1,0:T(8,128)S(1)}, f32[56,512]{1,0:T(8,128)S(1)}, u32[]{:S(2)}, u32[]{:S(2)}) collective-permute-start(f32[56,512]{1,0:T(8,128)S(1)} %get-tuple-element.104), channel_id=1, source_target_pairs={{0,4},{4,0},{8,12},{12,8},{16,20},{20,16},{24,28},{28,24},{1,5},{5... | collective-permute-start | bytes 344072 | tf_op jit(solution)/shard_map/ppermute | solution.py:25
  80.9 2.9 %collective-permute-start.23 = (f32[56,512]{1,0:T(8,128)S(1)}, f32[56,512]{1,0:T(8,128)S(1)}, u32[]{:S(2)}, u32[]{:S(2)}) collective-permute-start(f32[56,512]{1,0:T(8,128)S(1)} %collective-permute-done.21), channel_id=1, source_target_pairs={{0,8},{4,0},{8,16},{12,4},{16,24},{20,12},{24,28},{28,20},{1,9},{5... | collective-permute-start | bytes 344072 | tf_op jit(solution)/shard_map/ppermute | solution.py:32
  83.8 1.1 %shard_map.123.refs_8_ = s32[8,1024]{1,0:T(8,128)S(1)} custom-call(f32[6]{0:T(128)S(1)} %copy-done.11, s32[8,16,512]{2,1,0:T(8,128)S(1)} %copy-done.7, s32[8,128]{1,0:T(8,128)S(1)} %bitcast.30, bf16[512,1024]{1,0:T(8,128)(2,1)S(1)} %copy-done.2), custom_call_target="tpu_custom_call" | custom-call | flops 1000 | bytes 1000 | tf_op jit(solution)/shard_map/pallas_call | solution.py:512
  84.9 5.0 %shard_map.124 = (f32[384,512]{1,0:T(8,128)S(1)}, f32[8,256]{1,0:T(8,128)S(1)}) custom-call(s32[32]{0:T(128)S(1)} %get-tuple-element.115.bins_ref.refs_0_, f32[24,128]{1,0:T(8,128)S(1)} %get-tuple-element.95.own_ref.refs_1_, f32[24,640]{1,0:T(8,128)S(1)} %collective-permute-done.18.refs_4_.refs_2_.refs_9_, f32[1,24,128]{2,1,0:T(8,128)S(1)} %bitcast.35, ...), custom_call_target="tpu_custom_call" | custom-call | flops 1000 | bytes 1000 | tf_op jit(solution)/shard_map/pallas_call | solution.py:569
  90.0 2.7 %shard_map.125 = (f32[3,8,16,512]{3,2,1,0:T(8,128)}, f32[3,8,16,512]{3,2,1,0:T(8,128)}) custom-call(f32[6]{0:T(128)S(1)} %copy-done.11, f32[3,8,16,512]{3,2,1,0:T(8,128)S(1)} %get-tuple-element.93.disp_ref.refs_1_.refs_2_, f32[3,8,16,512]{3,2,1,0:T(8,128)S(1)} %get-tuple-element.94.refs_2_, f32[8,16,512]{2,1,0:T(8,128)S(1)} %copy-done.3, ...), custom_call_target="tpu_custom_call" | custom-call | flops 1000 | bytes 1000 | tf_op jit(solution)/shard_map/pallas_call | solution.py:585
  92.7 0.8 collective-permute-done.24
  93.6 0.7 collective-permute-start.25
  94.3 2.9 %collective-permute-done.25 = f32[256]{0:T(256)S(1)} collective-permute-done((f32[256]{0:T(256)S(1)}, f32[256]{0:T(256)S(1)}, u32[]{:S(2)}, u32[]{:S(2)}) %collective-permute-start.25) | collective-permute-done | bytes 1056 | tf_op jit(solution)/shard_map/ppermute | solution.py:32
  (64 shorter events, 5.0 us)
Async XLA Ops:
  0.6 8.7 %copy-start.1 = (f32[3,8,16,512]{3,2,1,0:T(8,128)S(1)}, f32[3,8,16,512]{3,2,1,0:T(8,128)}, u32[]{:S(2)}) copy-start(f32[3,8,16,512]{3,2,1,0:T(8,128)} %refs_1_.3) | copy-start | bytes 2359300
  1.4 8.0 %copy-start = (f32[2,8,16,512]{3,2,1,0:T(8,128)S(1)}, f32[2,8,16,512]{3,2,1,0:T(8,128)}, u32[]{:S(2)}) copy-start(f32[2,8,16,512]{3,2,1,0:T(8,128)} %moduli_ref.9) | copy-start | bytes 1572868
  4.6 7.5 %collective-permute-start = (f32[40,640]{1,0:T(8,128)}, f32[40,640]{1,0:T(8,128)S(1)}, u32[]{:S(2)}, u32[]{:S(2)}) collective-permute-start(f32[40,640]{1,0:T(8,128)} %get-tuple-element.59.refs_6_), channel_id=1, source_target_pairs={{0,1},{1,2},{2,3},{3,0},{4,5},{5,6},{6,7},{7,4},{8,9},{9,10},{10,1... | collective-permute-start | bytes 307208 | tf_op jit(solution)/shard_map/ppermute | solution.py:37
  5.1 7.1 %collective-permute-start.1 = (f32[32,640]{1,0:T(8,128)}, f32[32,640]{1,0:T(8,128)S(1)}, u32[]{:S(2)}, u32[]{:S(2)}) collective-permute-start(f32[32,640]{1,0:T(8,128)} %get-tuple-element.60.refs_7_), channel_id=1, source_target_pairs={{0,3},{1,0},{2,1},{3,2},{4,7},{5,4},{6,5},{7,6},{8,11},{9,8},{10,9... | collective-permute-start | bytes 245768 | tf_op jit(solution)/shard_map/ppermute | solution.py:37
  7.1 4.4 %copy-start.10 = (f32[32,128]{1,0:T(8,128)S(1)}, f32[32,128]{1,0:T(8,128)}, u32[]{:S(2)}) copy-start(f32[32,128]{1,0:T(8,128)} %get-tuple-element.58.own_ref.refs_1_) | copy-start | bytes 49156
  7.1 5.1 %collective-permute-start.2 = (f32[32,128]{1,0:T(8,128)}, f32[32,128]{1,0:T(8,128)S(1)}, u32[]{:S(2)}, u32[]{:S(2)}) collective-permute-start(f32[32,128]{1,0:T(8,128)} %get-tuple-element.58.own_ref.refs_1_), channel_id=1, source_target_pairs={{0,2},{1,3},{2,0},{3,1},{4,6},{5,7},{6,4},{7,5},{8,10},{9,11},{10,... | collective-permute-start | bytes 49160 | tf_op jit(solution)/shard_map/ppermute | solution.py:37
  12.1 0.6 copy-start.11
  13.3 6.2 %collective-permute-start.3 = (f32[88,512]{1,0:T(8,128)S(1)}, f32[88,512]{1,0:T(8,128)S(1)}, u32[]{:S(2)}, u32[]{:S(2)}) collective-permute-start(f32[88,512]{1,0:T(8,128)S(1)} %get-tuple-element.62._), channel_id=1, source_target_pairs={{0,4},{4,0},{8,12},{12,8},{16,20},{20,16},{24,28},{28,24},{1,5},{5... | collective-permute-start | bytes 540680 | tf_op jit(solution)/shard_map/ppermute | solution.py:25
  15.0 7.6 %copy-start.5 = (s32[1024]{0:T(1024)S(1)}, s32[1024]{0:T(1024)}, u32[]{:S(2)}) copy-start(s32[1024]{0:T(1024)} %param.12) | copy-start | bytes 12292
  19.5 9.1 %copy-start.2 = (bf16[512,1024]{1,0:T(8,128)(2,1)S(1)}, bf16[512,1024]{1,0:T(8,128)(2,1)}, u32[]{:S(2)}) copy-start(bf16[512,1024]{1,0:T(8,128)(2,1)} %get-tuple-element.67.refs_15_.hot_ref) | copy-start | bytes 3145732
  19.5 8.1 %collective-permute-start.4 = (f32[88,512]{1,0:T(8,128)S(1)}, f32[88,512]{1,0:T(8,128)S(1)}, u32[]{:S(2)}, u32[]{:S(2)}) collective-permute-start(f32[88,512]{1,0:T(8,128)S(1)} %get-tuple-element.65), channel_id=1, source_target_pairs={{0,4},{4,0},{8,12},{12,8},{16,20},{20,16},{24,28},{28,24},{1,5},{5... | collective-permute-start | bytes 540680 | tf_op jit(solution)/shard_map/ppermute | solution.py:25
  21.0 7.6 %collective-permute-start.5 = (f32[88,512]{1,0:T(8,128)S(1)}, f32[88,512]{1,0:T(8,128)S(1)}, u32[]{:S(2)}, u32[]{:S(2)}) collective-permute-start(f32[88,512]{1,0:T(8,128)S(1)} %collective-permute-done.3), channel_id=1, source_target_pairs={{0,8},{4,0},{8,16},{12,4},{16,24},{20,12},{24,28},{28,20},{1,9},{5... | collective-permute-start | bytes 540680 | tf_op jit(solution)/shard_map/ppermute | solution.py:32
  22.9 5.6 %copy-start.4 = (f32[3,8,16,512]{3,2,1,0:T(8,128)S(1)}, f32[3,8,16,512]{3,2,1,0:T(8,128)}, u32[]{:S(2)}) copy-start(f32[3,8,16,512]{3,2,1,0:T(8,128)} %refs_2_.3) | copy-start | bytes 2359300
  22.9 5.6 %copy-start.3 = (f32[8,16,512]{2,1,0:T(8,128)S(1)}, f32[8,16,512]{2,1,0:T(8,128)}, u32[]{:S(2)}) copy-start(f32[8,16,512]{2,1,0:T(8,128)} %refs_3_.7) | copy-start | bytes 786436
  22.9 5.6 %copy-start.6 = (f32[3,1024]{1,0:T(4,128)S(1)}, f32[3,1024]{1,0:T(4,128)}, u32[]{:S(2)}) copy-start(f32[3,1024]{1,0:T(4,128)} %refs_13_.5) | copy-start | bytes 36868
  22.9 5.6 %copy-start.8 = (f32[40,640]{1,0:T(8,128)S(1)}, f32[40,640]{1,0:T(8,128)}, u32[]{:S(2)}) copy-start(f32[40,640]{1,0:T(8,128)} %get-tuple-element.59.refs_6_) | copy-start | bytes 307204
  23.0 5.6 %copy-start.9 = (f32[32,640]{1,0:T(8,128)S(1)}, f32[32,640]{1,0:T(8,128)}, u32[]{:S(2)}) copy-start(f32[32,640]{1,0:T(8,128)} %get-tuple-element.60.refs_7_) | copy-start | bytes 245764
  31.1 4.3 %collective-permute-start.6 = (f32[24,640]{1,0:T(8,128)S(1)}, f32[24,640]{1,0:T(8,128)S(1)}, u32[]{:S(2)}, u32[]{:S(2)}) collective-permute-start(f32[24,640]{1,0:T(8,128)S(1)} %get-tuple-element.71.refs_7_), channel_id=1, source_target_pairs={{0,3},{1,0},{2,1},{3,2},{4,7},{5,4},{6,5},{7,6},{8,11},{9,8},{10,9... | collective-permute-start | bytes 184328 | tf_op jit(solution)/shard_map/ppermute | solution.py:37
  31.1 4.2 %collective-permute-start.8 = (f32[24,640]{1,0:T(8,128)S(1)}, f32[24,640]{1,0:T(8,128)S(1)}, u32[]{:S(2)}, u32[]{:S(2)}) collective-permute-start(f32[24,640]{1,0:T(8,128)S(1)} %get-tuple-element.72.refs_6_), channel_id=1, source_target_pairs={{0,1},{1,2},{2,3},{3,0},{4,5},{5,6},{6,7},{7,4},{8,9},{9,10},{10,1... | collective-permute-start | bytes 184328 | tf_op jit(solution)/shard_map/ppermute | solution.py:37
  31.6 3.7 %collective-permute-start.7 = (f32[24,128]{1,0:T(8,128)S(1)}, f32[24,128]{1,0:T(8,128)S(1)}, u32[]{:S(2)}, u32[]{:S(2)}) collective-permute-start(f32[24,128]{1,0:T(8,128)S(1)} %get-tuple-element.70.own_ref.refs_1_), channel_id=1, source_target_pairs={{0,2},{1,3},{2,0},{3,1},{4,6},{5,7},{6,4},{7,5},{8,10},{9,11},{10,... | collective-permute-start | bytes 36872 | tf_op jit(solution)/shard_map/ppermute | solution.py:37
  35.9 5.0 %collective-permute-start.9 = (f32[56,512]{1,0:T(8,128)S(1)}, f32[56,512]{1,0:T(8,128)S(1)}, u32[]{:S(2)}, u32[]{:S(2)}) collective-permute-start(f32[56,512]{1,0:T(8,128)S(1)} %get-tuple-element.74._), channel_id=1, source_target_pairs={{0,4},{4,0},{8,12},{12,8},{16,20},{20,16},{24,28},{28,24},{1,5},{5... | collective-permute-start | bytes 344072 | tf_op jit(solution)/shard_map/ppermute | solution.py:25
  41.0 7.0 %collective-permute-start.10 = (f32[56,512]{1,0:T(8,128)S(1)}, f32[56,512]{1,0:T(8,128)S(1)}, u32[]{:S(2)}, u32[]{:S(2)}) collective-permute-start(f32[56,512]{1,0:T(8,128)S(1)} %get-tuple-element.78), channel_id=1, source_target_pairs={{0,4},{4,0},{8,12},{12,8},{16,20},{20,16},{24,28},{28,24},{1,5},{5... | collective-permute-start | bytes 344072 | tf_op jit(solution)/shard_map/ppermute | solution.py:25
  42.0 6.0 %collective-permute-start.11 = (f32[56,512]{1,0:T(8,128)S(1)}, f32[56,512]{1,0:T(8,128)S(1)}, u32[]{:S(2)}, u32[]{:S(2)}) collective-permute-start(f32[56,512]{1,0:T(8,128)S(1)} %collective-permute-done.9), channel_id=1, source_target_pairs={{0,8},{4,0},{8,16},{12,4},{16,24},{20,12},{24,28},{28,20},{1,9},{5... | collective-permute-start | bytes 344072 | tf_op jit(solution)/shard_map/ppermute | solution.py:32
  50.5 4.3 %collective-permute-start.12 = (f32[24,640]{1,0:T(8,128)S(1)}, f32[24,640]{1,0:T(8,128)S(1)}, u32[]{:S(2)}, u32[]{:S(2)}) collective-permute-start(f32[24,640]{1,0:T(8,128)S(1)} %get-tuple-element.84.refs_7_), channel_id=1, source_target_pairs={{0,3},{1,0},{2,1},{3,2},{4,7},{5,4},{6,5},{7,6},{8,11},{9,8},{10,9... | collective-permute-start | bytes 184328 | tf_op jit(solution)/shard_map/ppermute | solution.py:37
  50.6 4.2 %collective-permute-start.14 = (f32[24,640]{1,0:T(8,128)S(1)}, f32[24,640]{1,0:T(8,128)S(1)}, u32[]{:S(2)}, u32[]{:S(2)}) collective-permute-start(f32[24,640]{1,0:T(8,128)S(1)} %get-tuple-element.85.refs_6_), channel_id=1, source_target_pairs={{0,1},{1,2},{2,3},{3,0},{4,5},{5,6},{6,7},{7,4},{8,9},{9,10},{10,1... | collective-permute-start | bytes 184328 | tf_op jit(solution)/shard_map/ppermute | solution.py:37
  51.1 3.7 %collective-permute-start.13 = (f32[24,128]{1,0:T(8,128)S(1)}, f32[24,128]{1,0:T(8,128)S(1)}, u32[]{:S(2)}, u32[]{:S(2)}) collective-permute-start(f32[24,128]{1,0:T(8,128)S(1)} %get-tuple-element.83.own_ref.refs_1_), channel_id=1, source_target_pairs={{0,2},{1,3},{2,0},{3,1},{4,6},{5,7},{6,4},{7,5},{8,10},{9,11},{10,... | collective-permute-start | bytes 36872 | tf_op jit(solution)/shard_map/ppermute | solution.py:37
  55.4 5.0 %collective-permute-start.15 = (f32[56,512]{1,0:T(8,128)S(1)}, f32[56,512]{1,0:T(8,128)S(1)}, u32[]{:S(2)}, u32[]{:S(2)}) collective-permute-start(f32[56,512]{1,0:T(8,128)S(1)} %get-tuple-element.87._), channel_id=1, source_target_pairs={{0,4},{4,0},{8,12},{12,8},{16,20},{20,16},{24,28},{28,24},{1,5},{5... | collective-permute-start | bytes 344072 | tf_op jit(solution)/shard_map/ppermute | solution.py:25
  60.4 6.8 %collective-permute-start.16 = (f32[56,512]{1,0:T(8,128)S(1)}, f32[56,512]{1,0:T(8,128)S(1)}, u32[]{:S(2)}, u32[]{:S(2)}) collective-permute-start(f32[56,512]{1,0:T(8,128)S(1)} %get-tuple-element.91), channel_id=1, source_target_pairs={{0,4},{4,0},{8,12},{12,8},{16,20},{20,16},{24,28},{28,24},{1,5},{5... | collective-permute-start | bytes 344072 | tf_op jit(solution)/shard_map/ppermute | solution.py:25
  61.1 6.1 %collective-permute-start.17 = (f32[56,512]{1,0:T(8,128)S(1)}, f32[56,512]{1,0:T(8,128)S(1)}, u32[]{:S(2)}, u32[]{:S(2)}) collective-permute-start(f32[56,512]{1,0:T(8,128)S(1)} %collective-permute-done.15), channel_id=1, source_target_pairs={{0,8},{4,0},{8,16},{12,4},{16,24},{20,12},{24,28},{28,20},{1,9},{5... | collective-permute-start | bytes 344072 | tf_op jit(solution)/shard_map/ppermute | solution.py:32
  69.7 4.3 %collective-permute-start.18 = (f32[24,640]{1,0:T(8,128)S(1)}, f32[24,640]{1,0:T(8,128)S(1)}, u32[]{:S(2)}, u32[]{:S(2)}) collective-permute-start(f32[24,640]{1,0:T(8,128)S(1)} %get-tuple-element.96.refs_7_), channel_id=1, source_target_pairs={{0,3},{1,0},{2,1},{3,2},{4,7},{5,4},{6,5},{7,6},{8,11},{9,8},{10,9... | collective-permute-start | bytes 184328 | tf_op jit(solution)/shard_map/ppermute | solution.py:37
  69.8 4.2 %collective-permute-start.20 = (f32[24,640]{1,0:T(8,128)S(1)}, f32[24,640]{1,0:T(8,128)S(1)}, u32[]{:S(2)}, u32[]{:S(2)}) collective-permute-start(f32[24,640]{1,0:T(8,128)S(1)} %get-tuple-element.97.refs_6_), channel_id=1, source_target_pairs={{0,1},{1,2},{2,3},{3,0},{4,5},{5,6},{6,7},{7,4},{8,9},{9,10},{10,1... | collective-permute-start | bytes 184328 | tf_op jit(solution)/shard_map/ppermute | solution.py:37
  70.3 3.7 %collective-permute-start.19 = (f32[24,128]{1,0:T(8,128)S(1)}, f32[24,128]{1,0:T(8,128)S(1)}, u32[]{:S(2)}, u32[]{:S(2)}) collective-permute-start(f32[24,128]{1,0:T(8,128)S(1)} %get-tuple-element.95.own_ref.refs_1_), channel_id=1, source_target_pairs={{0,2},{1,3},{2,0},{3,1},{4,6},{5,7},{6,4},{7,5},{8,10},{9,11},{10,... | collective-permute-start | bytes 36872 | tf_op jit(solution)/shard_map/ppermute | solution.py:37
  74.6 9.2 %copy-start.7 = (s32[8,16,512]{2,1,0:T(8,128)S(1)}, s32[8,16,512]{2,1,0:T(8,128)}, u32[]{:S(2)}) copy-start(s32[8,16,512]{2,1,0:T(8,128)} %tiles_ref.1) | copy-start | bytes 786436
  74.6 5.3 %collective-permute-start.21 = (f32[56,512]{1,0:T(8,128)S(1)}, f32[56,512]{1,0:T(8,128)S(1)}, u32[]{:S(2)}, u32[]{:S(2)}) collective-permute-start(f32[56,512]{1,0:T(8,128)S(1)} %get-tuple-element.99._), channel_id=1, source_target_pairs={{0,4},{4,0},{8,12},{12,8},{16,20},{20,16},{24,28},{28,24},{1,5},{5... | collective-permute-start | bytes 344072 | tf_op jit(solution)/shard_map/ppermute | solution.py:25
  79.8 10.1 %collective-permute-start.22 = (f32[56,512]{1,0:T(8,128)S(1)}, f32[56,512]{1,0:T(8,128)S(1)}, u32[]{:S(2)}, u32[]{:S(2)}) collective-permute-start(f32[56,512]{1,0:T(8,128)S(1)} %get-tuple-element.104), channel_id=1, source_target_pairs={{0,4},{4,0},{8,12},{12,8},{16,20},{20,16},{24,28},{28,24},{1,5},{5... | collective-permute-start | bytes 344072 | tf_op jit(solution)/shard_map/ppermute | solution.py:25
  80.9 9.0 %collective-permute-start.23 = (f32[56,512]{1,0:T(8,128)S(1)}, f32[56,512]{1,0:T(8,128)S(1)}, u32[]{:S(2)}, u32[]{:S(2)}) collective-permute-start(f32[56,512]{1,0:T(8,128)S(1)} %collective-permute-done.21), channel_id=1, source_target_pairs={{0,8},{4,0},{8,16},{12,4},{16,24},{20,12},{24,28},{28,20},{1,9},{5... | collective-permute-start | bytes 344072 | tf_op jit(solution)/shard_map/ppermute | solution.py:32
  89.9 3.7 %collective-permute-start.24 = (f32[2,256]{1,0:T(2,128)S(1)}, f32[2,256]{1,0:T(2,128)S(1)}, u32[]{:S(2)}, u32[]{:S(2)}) collective-permute-start(f32[2,256]{1,0:T(2,128)S(1)} %slice.48), channel_id=1, source_target_pairs={{0,4},{4,0},{8,12},{12,8},{16,20},{20,16},{24,28},{28,24},{1,5},{5... | collective-permute-start | bytes 6152 | tf_op jit(solution)/shard_map/ppermute | solution.py:25
  93.6 3.6 %collective-permute-start.25 = (f32[256]{0:T(256)S(1)}, f32[256]{0:T(256)S(1)}, u32[]{:S(2)}, u32[]{:S(2)}) collective-permute-start(f32[256]{0:T(256)S(1)} %bitcast.42), channel_id=1, source_target_pairs={{0,8},{4,0},{8,16},{12,4},{16,24},{20,12},{24,28},{28,20},{1,9},{5... | collective-permute-start | bytes 3080 | tf_op jit(solution)/shard_map/ppermute | solution.py:32
